TPU v7x, 32 devices: a whole 2x2x4 slice. The times are simulated.
32 devices in a mesh: aa: 8 (over z, x), ba: 4 (over y, core).
Axes of the slice: x: 2, y: 2, z: 4, core: 2. Of those that a mesh axis runs over, the one named last changes fastest.
Arguments:
- acts_a: bfloat16 [256, 28672], P('ba', 'aa'), may hold values from -13 to 13, as said below
- acts_b: bfloat16 [256, 28672], P('aa', 'ba'), may hold values from -13 to 13, as said below
Outputs:
- potential_a: float32 [28672], P('aa')
- potential_b: float32 [28672], P('ba')
Inputs may be any that keep to these rules, and one draw needn't show every extreme that they name: `acts_a`: activations of order one with unit scales that differ from unit to unit. `acts_b`: activations of order one with unit scales that differ from unit to unit.
All inputs are finite; a program needn't handle non-finite values.
Results may differ from a plain program's by a relative error of at most 0.0003.
Values may be sent and summed in bfloat16 or wider, within the bound.
No kernel may reach another device: no remote copies, remote signals or barrier semaphores. Data moves between devices by JAX's collectives and lax.ppermute only.
A program may use at most 128 MiB of HBM per device.

v0:
```python
import math

import jax
import jax.numpy as jnp
from jax import lax
from jax.sharding import PartitionSpec as P

NA = 28672
NB = 28672
ITERS = 2


epsilon = 0.01


def combine(first, second):
    upper = jnp.maximum(first[0], second[0])
    return (upper, first[1] * jnp.exp(first[0] - upper) + second[1] * jnp.exp(second[0] - upper))


def cost_rows(whole_a, whole_b, norm_a, norm_b, start, block, tokens):
    rows = lax.dynamic_slice_in_dim(whole_a, start, block, 1)
    cross = lax.dot_general(
        rows, whole_b, (((0,), (0,)), ((), ())), preferred_element_type=jnp.float32
    )
    norms = lax.dynamic_slice_in_dim(norm_a, start, block, 0)
    return (norms[:, None] + norm_b[None, :] - 2.0 * cross) / tokens


def per_device(acts_a, acts_b):
    whole_a = lax.all_gather(acts_a, "ba", axis=0, tiled=True)
    whole_b = lax.all_gather(acts_b, "aa", axis=0, tiled=True)
    tokens = whole_a.shape[0]
    rows_here = whole_a.shape[1]
    cols_here = whole_b.shape[1]
    block = min(896, rows_here)
    count = rows_here // block
    norm_a = jnp.sum(jnp.square(whole_a.astype(jnp.float32)), 0)
    norm_b = jnp.sum(jnp.square(whole_b.astype(jnp.float32)), 0)
    potential_b = jnp.zeros((cols_here,), jnp.float32)
    potential_a = jnp.zeros((rows_here,), jnp.float32)
    for step in range(ITERS):

        def row_part(index):
            cost = cost_rows(whole_a, whole_b, norm_a, norm_b, index * block, block, tokens)
            scores = (potential_b[None, :] - cost) / epsilon
            upper = jnp.max(scores, 1)
            return (upper, jnp.sum(jnp.exp(scores - upper[:, None]), 1))

        row_upper, row_sums = lax.map(row_part, jnp.arange(count, dtype=jnp.int32))
        row_upper = row_upper.reshape(rows_here)
        row_sums = row_sums.reshape(rows_here)
        top = lax.pmax(row_upper, "ba")
        total = lax.psum(row_sums * jnp.exp(row_upper - top), "ba")
        potential_a = -epsilon * math.log(NA) - epsilon * (top + jnp.log(total))

        def col_part(carry, index):
            cost = cost_rows(whole_a, whole_b, norm_a, norm_b, index * block, block, tokens)
            part_a = lax.dynamic_slice_in_dim(potential_a, index * block, block, 0)
            scores = (part_a[:, None] - cost) / epsilon
            upper = jnp.max(scores, 0)
            summed = jnp.sum(jnp.exp(scores - upper[None, :]), 0)
            return (combine(carry, (upper, summed)), None)

        start = (
            jnp.full((cols_here,), -jnp.inf, jnp.float32),
            jnp.zeros((cols_here,), jnp.float32),
        )
        (col_upper, col_sums), unused = lax.scan(
            col_part, start, jnp.arange(count, dtype=jnp.int32)
        )
        top_b = lax.pmax(col_upper, "aa")
        total_b = lax.psum(col_sums * jnp.exp(col_upper - top_b), "aa")
        potential_b = -epsilon * math.log(NB) - epsilon * (top_b + jnp.log(total_b))
    return (potential_a, potential_b)


def solution(mesh):
    in_specs = (P("ba", "aa"), P("aa", "ba"))
    out_specs = (P("aa"), P("ba"))
    return jax.shard_map(
        per_device, mesh=mesh, in_specs=in_specs, out_specs=out_specs, check_vma=False
    )
```

profile of v0, /device:TPU:0, one launch (start us, length us, event | category | flops | bytes accessed | tf_op | source)
XLA Modules:
  0.0 735.7 jit_solution(16227724581253749585)
XLA Ops:
  8.7 24.7 %all-gather.3.cloned.1.call-done = bf16[256,3584]{1,0:T(8,128)(2,1)} async-done(((bf16[64,3584]{1,0:T(8,128)(2,1)}), bf16[256,3584]{1,0:T(8,128)(2,1)}) %all-gather.3.cloned.1.call-update) | async-done | bytes 1835024 | tf_op jit(solution)/shard_map/all_gather | solution.py:31
  33.4 1.9 multiply_reduce_fusion.1
  35.3 67.1 %all-gather.5.cloned.1.call-done = bf16[256,7168]{1,0:T(8,128)(2,1)} async-done(((bf16[32,7168]{1,0:T(8,128)(2,1)}), bf16[256,7168]{1,0:T(8,128)(2,1)}) %all-gather.5.cloned.1.call-update) | async-done | bytes 3670032 | tf_op jit(solution)/shard_map/all_gather | solution.py:32
  102.4 2.8 multiply_reduce_fusion
  105.3 105.4 %while.50 = (s32[]{:T(128)}, f32[4,896]{1,0:T(4,128)S(1)}, f32[4,896]{1,0:T(4,128)S(1)}, s32[4]{0:T(128)S(1)}, f32[3584]{0:T(1024)S(1)}, /*index=5*/f32[7168]{0:...) while((s32[]{:T(128)}, f32[4,896]{1,0:T(4,128)S(1)}, ...), condition=%wide.region_5.6_spmd, body=%wide.region_2.5_spmd.sunk | while | flops 3384670208 | bytes 55620284 | solution.py:50
  106.7 13.3 %fusion.33 = (f32[896]{0:T(1024)S(1)}, f32[896,7168]{1,0:T(8,128)}) fusion(f32[7168]{0:T(1024)S(1)} %get-tuple-element.606, f32[896]{0:T(1024)S(1)} %dynamic_slice.83, bf16[256,7168]{1,0:T(8,128)(2,1)} %get-tuple-element.608, bf16[256,3584]{1,0:T(8,128)(2,1)} %get-tuple-element.607, s32[]{:T(128)S(6)} %select_n.24), kind=kOutput, calls=%fused_computation.2.clone.1 | convolution fusion | flops 3333291008 | bytes 29854724 | tf_op jit(solution)/shard_map/while/body/eval_jaxpr/dot_general | solution.py:23
  120.1 11.4 %exponential_reduce_fusion.8 = f32[896]{0:T(1024)S(1)} fusion(f32[896,7168]{1,0:T(8,128)} %get-tuple-element.539, f32[896]{0:T(1024)S(1)} %get-tuple-element.538, f32[7168]{0:T(1024)S(1)} %get-tuple-element.606, f32[896]{0:T(1024)S(1)} %dynamic_slice.83), kind=kLoop, calls=%fused_computation.clone.1 | loop fusion | flops 51379328 | bytes 25729536 | tf_op jit(solution)/shard_map/while/body/eval_jaxpr/reduce_sum | solution.py:48
  133.1 13.3 %fusion.33 = (f32[896]{0:T(1024)S(1)}, f32[896,7168]{1,0:T(8,128)}) fusion(f32[7168]{0:T(1024)S(1)} %get-tuple-element.606, f32[896]{0:T(1024)S(1)} %dynamic_slice.83, bf16[256,7168]{1,0:T(8,128)(2,1)} %get-tuple-element.608, bf16[256,3584]{1,0:T(8,128)(2,1)} %get-tuple-element.607, s32[]{:T(128)S(6)} %select_n.24), kind=kOutput, calls=%fused_computation.2.clone.1 | convolution fusion | flops 3333291008 | bytes 29854724 | tf_op jit(solution)/shard_map/while/body/eval_jaxpr/dot_general | solution.py:23
  146.4 11.4 %exponential_reduce_fusion.8 = f32[896]{0:T(1024)S(1)} fusion(f32[896,7168]{1,0:T(8,128)} %get-tuple-element.539, f32[896]{0:T(1024)S(1)} %get-tuple-element.538, f32[7168]{0:T(1024)S(1)} %get-tuple-element.606, f32[896]{0:T(1024)S(1)} %dynamic_slice.83), kind=kLoop, calls=%fused_computation.clone.1 | loop fusion | flops 51379328 | bytes 25729536 | tf_op jit(solution)/shard_map/while/body/eval_jaxpr/reduce_sum | solution.py:48
  159.4 13.3 %fusion.33 = (f32[896]{0:T(1024)S(1)}, f32[896,7168]{1,0:T(8,128)}) fusion(f32[7168]{0:T(1024)S(1)} %get-tuple-element.606, f32[896]{0:T(1024)S(1)} %dynamic_slice.83, bf16[256,7168]{1,0:T(8,128)(2,1)} %get-tuple-element.608, bf16[256,3584]{1,0:T(8,128)(2,1)} %get-tuple-element.607, s32[]{:T(128)S(6)} %select_n.24), kind=kOutput, calls=%fused_computation.2.clone.1 | convolution fusion | flops 3333291008 | bytes 29854724 | tf_op jit(solution)/shard_map/while/body/eval_jaxpr/dot_general | solution.py:23
  172.8 11.4 %exponential_reduce_fusion.8 = f32[896]{0:T(1024)S(1)} fusion(f32[896,7168]{1,0:T(8,128)} %get-tuple-element.539, f32[896]{0:T(1024)S(1)} %get-tuple-element.538, f32[7168]{0:T(1024)S(1)} %get-tuple-element.606, f32[896]{0:T(1024)S(1)} %dynamic_slice.83), kind=kLoop, calls=%fused_computation.clone.1 | loop fusion | flops 51379328 | bytes 25729536 | tf_op jit(solution)/shard_map/while/body/eval_jaxpr/reduce_sum | solution.py:48
  185.8 13.3 %fusion.33 = (f32[896]{0:T(1024)S(1)}, f32[896,7168]{1,0:T(8,128)}) fusion(f32[7168]{0:T(1024)S(1)} %get-tuple-element.606, f32[896]{0:T(1024)S(1)} %dynamic_slice.83, bf16[256,7168]{1,0:T(8,128)(2,1)} %get-tuple-element.608, bf16[256,3584]{1,0:T(8,128)(2,1)} %get-tuple-element.607, s32[]{:T(128)S(6)} %select_n.24), kind=kOutput, calls=%fused_computation.2.clone.1 | convolution fusion | flops 3333291008 | bytes 29854724 | tf_op jit(solution)/shard_map/while/body/eval_jaxpr/dot_general | solution.py:23
  199.1 11.4 %exponential_reduce_fusion.8 = f32[896]{0:T(1024)S(1)} fusion(f32[896,7168]{1,0:T(8,128)} %get-tuple-element.539, f32[896]{0:T(1024)S(1)} %get-tuple-element.538, f32[7168]{0:T(1024)S(1)} %get-tuple-element.606, f32[896]{0:T(1024)S(1)} %dynamic_slice.83), kind=kLoop, calls=%fused_computation.clone.1 | loop fusion | flops 51379328 | bytes 25729536 | tf_op jit(solution)/shard_map/while/body/eval_jaxpr/reduce_sum | solution.py:48
  210.7 10.1 %pmax.28 = f32[3584]{0:T(1024)S(1)} all-reduce(f32[3584]{0:T(1024)S(1)} %reshape.39), channel_id=1, replica_groups=mesh['aa'=8,'ba'=4] {'ba'}, use_global_device_ids=true, to_apply=%region_6.7 | all-reduce | flops 3584 | bytes 28672 | tf_op jit(solution)/shard_map/pmax | solution.py:53
  220.9 10.1 %psum.28 = f32[3584]{0:T(1024)S(1)} all-reduce(f32[3584]{0:T(1024)S(1)} %exponential_multiply_fusion.3), channel_id=1, replica_groups=mesh['aa'=8,'ba'=4] {'ba'}, use_global_device_ids=true, to_apply=%region_7.8 | all-reduce | flops 3584 | bytes 28672 | tf_op jit(solution)/shard_map/psum | solution.py:54
  231.0 113.6 %while.52 = (s32[]{:T(128)}, f32[7168]{0:T(1024)S(1)}, f32[7168]{0:T(1024)S(1)}, s32[4]{0:T(128)S(1)}, f32[3584]{0:T(1024)S(1)}, /*index=5*/f32[3584]{0:T(1024)S...) while((s32[]{:T(128)}, f32[7168]{0:T(1024)S(1)}, ...), condition=%wide.region_11.12_spmd.clone, body=%wide.region_8.11_spmd.clone.sunk | while | flops 3384715264 | bytes 55853256 | solution.py:69
  232.5 13.3 %fusion.37 = (f32[7168]{0:T(1024)S(1)}, f32[896,7168]{1,0:T(8,128)}) fusion(f32[7168]{0:T(1024)S(1)} %get-tuple-element.645, f32[896]{0:T(1024)S(1)} %dynamic_slice.89, f32[896]{0:T(1024)S(1)} %dynamic_slice.90, bf16[256,7168]{1,0:T(8,128)(2,1)} %get-tuple-element.647, bf16[256,3584]{1,0:T(8,128)(2,1)} %get-tuple-element.646, s32[]{:T(128)S(6)} %select_n.26), kind=kOutput, calls=%fused_computation.14.clone.1 | convolution fusion | flops 3333284864 | bytes 29883396 | tf_op jit(solution)/shard_map/while/body/eval_jaxpr/dot_general | solution.py:23
  245.9 13.5 %exponential_reduce_fusion.10 = f32[7168]{0:T(1024)S(1)} fusion(f32[896,7168]{1,0:T(8,128)} %get-tuple-element.560, f32[7168]{0:T(1024)S(1)} %get-tuple-element.561, f32[7168]{0:T(1024)S(1)} %get-tuple-element.645, f32[896]{0:T(1024)S(1)} %dynamic_slice.89, f32[896]{0:T(1024)S(1)} %dynamic_slice.90), kind=kLoop, calls=%fused_computation.12.clone.1 | loop fusion | flops 51373056 | bytes 25783296 | tf_op jit(solution)/shard_map/while/body/eval_jaxpr/reduce_sum | solution.py:62
  260.9 13.3 %fusion.37 = (f32[7168]{0:T(1024)S(1)}, f32[896,7168]{1,0:T(8,128)}) fusion(f32[7168]{0:T(1024)S(1)} %get-tuple-element.645, f32[896]{0:T(1024)S(1)} %dynamic_slice.89, f32[896]{0:T(1024)S(1)} %dynamic_slice.90, bf16[256,7168]{1,0:T(8,128)(2,1)} %get-tuple-element.647, bf16[256,3584]{1,0:T(8,128)(2,1)} %get-tuple-element.646, s32[]{:T(128)S(6)} %select_n.26), kind=kOutput, calls=%fused_computation.14.clone.1 | convolution fusion | flops 3333284864 | bytes 29883396 | tf_op jit(solution)/shard_map/while/body/eval_jaxpr/dot_general | solution.py:23
  274.3 13.5 %exponential_reduce_fusion.10 = f32[7168]{0:T(1024)S(1)} fusion(f32[896,7168]{1,0:T(8,128)} %get-tuple-element.560, f32[7168]{0:T(1024)S(1)} %get-tuple-element.561, f32[7168]{0:T(1024)S(1)} %get-tuple-element.645, f32[896]{0:T(1024)S(1)} %dynamic_slice.89, f32[896]{0:T(1024)S(1)} %dynamic_slice.90), kind=kLoop, calls=%fused_computation.12.clone.1 | loop fusion | flops 51373056 | bytes 25783296 | tf_op jit(solution)/shard_map/while/body/eval_jaxpr/reduce_sum | solution.py:62
  289.3 13.4 %fusion.37 = (f32[7168]{0:T(1024)S(1)}, f32[896,7168]{1,0:T(8,128)}) fusion(f32[7168]{0:T(1024)S(1)} %get-tuple-element.645, f32[896]{0:T(1024)S(1)} %dynamic_slice.89, f32[896]{0:T(1024)S(1)} %dynamic_slice.90, bf16[256,7168]{1,0:T(8,128)(2,1)} %get-tuple-element.647, bf16[256,3584]{1,0:T(8,128)(2,1)} %get-tuple-element.646, s32[]{:T(128)S(6)} %select_n.26), kind=kOutput, calls=%fused_computation.14.clone.1 | convolution fusion | flops 3333284864 | bytes 29883396 | tf_op jit(solution)/shard_map/while/body/eval_jaxpr/dot_general | solution.py:23
  302.7 13.5 %exponential_reduce_fusion.10 = f32[7168]{0:T(1024)S(1)} fusion(f32[896,7168]{1,0:T(8,128)} %get-tuple-element.560, f32[7168]{0:T(1024)S(1)} %get-tuple-element.561, f32[7168]{0:T(1024)S(1)} %get-tuple-element.645, f32[896]{0:T(1024)S(1)} %dynamic_slice.89, f32[896]{0:T(1024)S(1)} %dynamic_slice.90), kind=kLoop, calls=%fused_computation.12.clone.1 | loop fusion | flops 51373056 | bytes 25783296 | tf_op jit(solution)/shard_map/while/body/eval_jaxpr/reduce_sum | solution.py:62
  317.8 13.4 %fusion.37 = (f32[7168]{0:T(1024)S(1)}, f32[896,7168]{1,0:T(8,128)}) fusion(f32[7168]{0:T(1024)S(1)} %get-tuple-element.645, f32[896]{0:T(1024)S(1)} %dynamic_slice.89, f32[896]{0:T(1024)S(1)} %dynamic_slice.90, bf16[256,7168]{1,0:T(8,128)(2,1)} %get-tuple-element.647, bf16[256,3584]{1,0:T(8,128)(2,1)} %get-tuple-element.646, s32[]{:T(128)S(6)} %select_n.26), kind=kOutput, calls=%fused_computation.14.clone.1 | convolution fusion | flops 3333284864 | bytes 29883396 | tf_op jit(solution)/shard_map/while/body/eval_jaxpr/dot_general | solution.py:23
  331.1 13.5 %exponential_reduce_fusion.10 = f32[7168]{0:T(1024)S(1)} fusion(f32[896,7168]{1,0:T(8,128)} %get-tuple-element.560, f32[7168]{0:T(1024)S(1)} %get-tuple-element.561, f32[7168]{0:T(1024)S(1)} %get-tuple-element.645, f32[896]{0:T(1024)S(1)} %dynamic_slice.89, f32[896]{0:T(1024)S(1)} %dynamic_slice.90), kind=kLoop, calls=%fused_computation.12.clone.1 | loop fusion | flops 51373056 | bytes 25783296 | tf_op jit(solution)/shard_map/while/body/eval_jaxpr/reduce_sum | solution.py:62
  344.6 36.0 %pmax.29 = f32[7168]{0:T(1024)S(1)} all-reduce(f32[7168]{0:T(1024)S(1)} %get-tuple-element.191), channel_id=1, replica_groups=mesh['aa'=8,'ba'=4] {'aa'}, use_global_device_ids=true, to_apply=%region_12.13 | all-reduce | flops 7168 | bytes 57344 | tf_op jit(solution)/shard_map/pmax | solution.py:72
  380.6 33.1 %psum.29 = f32[7168]{0:T(1024)S(1)} all-reduce(f32[7168]{0:T(1024)S(1)} %exponential_multiply_fusion.1), channel_id=1, replica_groups=mesh['aa'=8,'ba'=4] {'aa'}, use_global_device_ids=true, to_apply=%region_13.14 | all-reduce | flops 7168 | bytes 57344 | tf_op jit(solution)/shard_map/psum | solution.py:73
  413.8 114.8 %while.51 = (s32[]{:T(128)}, f32[4,896]{1,0:T(4,128)S(1)}, f32[4,896]{1,0:T(4,128)S(1)}, f32[7168]{0:T(1024)S(1)}, s32[4]{0:T(128)S(1)}, /*index=5*/f32[3584]{0:...) while((s32[]{:T(128)}, f32[4,896]{1,0:T(4,128)S(1)}, ...), condition=%wide.region_17.18_spmd, body=%wide.region_14.17_spmd.sunk | while | flops 3384670208 | bytes 55677636 | solution.py:50
  415.3 13.4 %fusion.35 = (f32[896]{0:T(1024)S(1)}, f32[896,7168]{1,0:T(8,128)}) fusion(f32[7168]{0:T(1024)S(1)} %get-tuple-element.684, f32[896]{0:T(1024)S(1)} %dynamic_slice.86, f32[7168]{0:T(1024)S(1)} %get-tuple-element.681, bf16[256,7168]{1,0:T(8,128)(2,1)} %get-tuple-element.686, bf16[256,3584]{1,0:T(8,128)(2,1)} %get-tuple-element.685, s32[]{:T(128)S(6)} %select_n.25), kind=kOutput, calls=%fused_computation.8.clone.1 | convolution fusion | flops 3333291008 | bytes 29883396 | tf_op jit(solution)/shard_map/while/body/eval_jaxpr/dot_general | solution.py:23
  428.7 13.7 %exponential_reduce_fusion.9 = f32[896]{0:T(1024)S(1)} fusion(f32[896,7168]{1,0:T(8,128)} %get-tuple-element.550, f32[896]{0:T(1024)S(1)} %get-tuple-element.549, f32[7168]{0:T(1024)S(1)} %get-tuple-element.684, f32[896]{0:T(1024)S(1)} %dynamic_slice.86, f32[7168]{0:T(1024)S(1)} %get-tuple-element.681), kind=kLoop, calls=%fused_computation.6.clone.1 | loop fusion | flops 51379328 | bytes 25758208 | tf_op jit(solution)/shard_map/while/body/eval_jaxpr/reduce_sum | solution.py:48
  444.0 13.4 %fusion.35 = (f32[896]{0:T(1024)S(1)}, f32[896,7168]{1,0:T(8,128)}) fusion(f32[7168]{0:T(1024)S(1)} %get-tuple-element.684, f32[896]{0:T(1024)S(1)} %dynamic_slice.86, f32[7168]{0:T(1024)S(1)} %get-tuple-element.681, bf16[256,7168]{1,0:T(8,128)(2,1)} %get-tuple-element.686, bf16[256,3584]{1,0:T(8,128)(2,1)} %get-tuple-element.685, s32[]{:T(128)S(6)} %select_n.25), kind=kOutput, calls=%fused_computation.8.clone.1 | convolution fusion | flops 3333291008 | bytes 29883396 | tf_op jit(solution)/shard_map/while/body/eval_jaxpr/dot_general | solution.py:23
  457.4 13.7 %exponential_reduce_fusion.9 = f32[896]{0:T(1024)S(1)} fusion(f32[896,7168]{1,0:T(8,128)} %get-tuple-element.550, f32[896]{0:T(1024)S(1)} %get-tuple-element.549, f32[7168]{0:T(1024)S(1)} %get-tuple-element.684, f32[896]{0:T(1024)S(1)} %dynamic_slice.86, f32[7168]{0:T(1024)S(1)} %get-tuple-element.681), kind=kLoop, calls=%fused_computation.6.clone.1 | loop fusion | flops 51379328 | bytes 25758208 | tf_op jit(solution)/shard_map/while/body/eval_jaxpr/reduce_sum | solution.py:48
  472.7 13.4 %fusion.35 = (f32[896]{0:T(1024)S(1)}, f32[896,7168]{1,0:T(8,128)}) fusion(f32[7168]{0:T(1024)S(1)} %get-tuple-element.684, f32[896]{0:T(1024)S(1)} %dynamic_slice.86, f32[7168]{0:T(1024)S(1)} %get-tuple-element.681, bf16[256,7168]{1,0:T(8,128)(2,1)} %get-tuple-element.686, bf16[256,3584]{1,0:T(8,128)(2,1)} %get-tuple-element.685, s32[]{:T(128)S(6)} %select_n.25), kind=kOutput, calls=%fused_computation.8.clone.1 | convolution fusion | flops 3333291008 | bytes 29883396 | tf_op jit(solution)/shard_map/while/body/eval_jaxpr/dot_general | solution.py:23
  486.1 13.7 %exponential_reduce_fusion.9 = f32[896]{0:T(1024)S(1)} fusion(f32[896,7168]{1,0:T(8,128)} %get-tuple-element.550, f32[896]{0:T(1024)S(1)} %get-tuple-element.549, f32[7168]{0:T(1024)S(1)} %get-tuple-element.684, f32[896]{0:T(1024)S(1)} %dynamic_slice.86, f32[7168]{0:T(1024)S(1)} %get-tuple-element.681), kind=kLoop, calls=%fused_computation.6.clone.1 | loop fusion | flops 51379328 | bytes 25758208 | tf_op jit(solution)/shard_map/while/body/eval_jaxpr/reduce_sum | solution.py:48
  501.4 13.4 %fusion.35 = (f32[896]{0:T(1024)S(1)}, f32[896,7168]{1,0:T(8,128)}) fusion(f32[7168]{0:T(1024)S(1)} %get-tuple-element.684, f32[896]{0:T(1024)S(1)} %dynamic_slice.86, f32[7168]{0:T(1024)S(1)} %get-tuple-element.681, bf16[256,7168]{1,0:T(8,128)(2,1)} %get-tuple-element.686, bf16[256,3584]{1,0:T(8,128)(2,1)} %get-tuple-element.685, s32[]{:T(128)S(6)} %select_n.25), kind=kOutput, calls=%fused_computation.8.clone.1 | convolution fusion | flops 3333291008 | bytes 29883396 | tf_op jit(solution)/shard_map/while/body/eval_jaxpr/dot_general | solution.py:23
  514.8 13.7 %exponential_reduce_fusion.9 = f32[896]{0:T(1024)S(1)} fusion(f32[896,7168]{1,0:T(8,128)} %get-tuple-element.550, f32[896]{0:T(1024)S(1)} %get-tuple-element.549, f32[7168]{0:T(1024)S(1)} %get-tuple-element.684, f32[896]{0:T(1024)S(1)} %dynamic_slice.86, f32[7168]{0:T(1024)S(1)} %get-tuple-element.681), kind=kLoop, calls=%fused_computation.6.clone.1 | loop fusion | flops 51379328 | bytes 25758208 | tf_op jit(solution)/shard_map/while/body/eval_jaxpr/reduce_sum | solution.py:48
  528.6 10.1 %pmax.30 = f32[3584]{0:T(1024)S(1)} all-reduce(f32[3584]{0:T(1024)S(1)} %reshape.41), channel_id=1, replica_groups=mesh['aa'=8,'ba'=4] {'ba'}, use_global_device_ids=true, to_apply=%region_18.19 | all-reduce | flops 3584 | bytes 28672 | tf_op jit(solution)/shard_map/pmax | solution.py:53
  538.8 10.1 %psum.30 = f32[3584]{0:T(1024)S(1)} all-reduce(f32[3584]{0:T(1024)S(1)} %exponential_multiply_fusion.2), channel_id=1, replica_groups=mesh['aa'=8,'ba'=4] {'ba'}, use_global_device_ids=true, to_apply=%region_19.20 | all-reduce | flops 3584 | bytes 28672 | tf_op jit(solution)/shard_map/psum | solution.py:54
  548.9 113.1 %while.53 = (s32[]{:T(128)}, f32[7168]{0:T(1024)S(1)}, f32[7168]{0:T(1024)S(1)}, s32[4]{0:T(128)S(1)}, f32[3584]{0:T(1024)S(1)}, /*index=5*/f32[3584]{0:T(1024)S...) while((s32[]{:T(128)}, f32[7168]{0:T(1024)S(1)}, ...), condition=%wide.region_23.24_spmd.clone, body=%wide.region_20.23_spmd.clone.sunk | while | flops 3384715264 | bytes 55853256 | solution.py:69
  550.3 13.4 %fusion.40 = (f32[7168]{0:T(1024)S(1)}, f32[896,7168]{1,0:T(8,128)}) fusion(f32[7168]{0:T(1024)S(1)} %get-tuple-element.723, f32[896]{0:T(1024)S(1)} %dynamic_slice.93, f32[896]{0:T(1024)S(1)} %dynamic_slice.94, bf16[256,7168]{1,0:T(8,128)(2,1)} %get-tuple-element.725, bf16[256,3584]{1,0:T(8,128)(2,1)} %get-tuple-element.724, s32[]{:T(128)S(6)} %select_n.27), kind=kOutput, calls=%fused_computation.23.clone.1 | convolution fusion | flops 3333284864 | bytes 29883396 | tf_op jit(solution)/shard_map/while/body/eval_jaxpr/dot_general | solution.py:23
  563.7 13.5 %exponential_reduce_fusion.11 = f32[7168]{0:T(1024)S(1)} fusion(f32[896,7168]{1,0:T(8,128)} %get-tuple-element.573, f32[7168]{0:T(1024)S(1)} %get-tuple-element.574, f32[7168]{0:T(1024)S(1)} %get-tuple-element.723, f32[896]{0:T(1024)S(1)} %dynamic_slice.93, f32[896]{0:T(1024)S(1)} %dynamic_slice.94), kind=kLoop, calls=%fused_computation.21.clone.1 | loop fusion | flops 51373056 | bytes 25783296 | tf_op jit(solution)/shard_map/while/body/eval_jaxpr/reduce_sum | solution.py:62
  578.6 13.4 %fusion.40 = (f32[7168]{0:T(1024)S(1)}, f32[896,7168]{1,0:T(8,128)}) fusion(f32[7168]{0:T(1024)S(1)} %get-tuple-element.723, f32[896]{0:T(1024)S(1)} %dynamic_slice.93, f32[896]{0:T(1024)S(1)} %dynamic_slice.94, bf16[256,7168]{1,0:T(8,128)(2,1)} %get-tuple-element.725, bf16[256,3584]{1,0:T(8,128)(2,1)} %get-tuple-element.724, s32[]{:T(128)S(6)} %select_n.27), kind=kOutput, calls=%fused_computation.23.clone.1 | convolution fusion | flops 3333284864 | bytes 29883396 | tf_op jit(solution)/shard_map/while/body/eval_jaxpr/dot_general | solution.py:23
  592.0 13.5 %exponential_reduce_fusion.11 = f32[7168]{0:T(1024)S(1)} fusion(f32[896,7168]{1,0:T(8,128)} %get-tuple-element.573, f32[7168]{0:T(1024)S(1)} %get-tuple-element.574, f32[7168]{0:T(1024)S(1)} %get-tuple-element.723, f32[896]{0:T(1024)S(1)} %dynamic_slice.93, f32[896]{0:T(1024)S(1)} %dynamic_slice.94), kind=kLoop, calls=%fused_computation.21.clone.1 | loop fusion | flops 51373056 | bytes 25783296 | tf_op jit(solution)/shard_map/while/body/eval_jaxpr/reduce_sum | solution.py:62
  606.9 13.4 %fusion.40 = (f32[7168]{0:T(1024)S(1)}, f32[896,7168]{1,0:T(8,128)}) fusion(f32[7168]{0:T(1024)S(1)} %get-tuple-element.723, f32[896]{0:T(1024)S(1)} %dynamic_slice.93, f32[896]{0:T(1024)S(1)} %dynamic_slice.94, bf16[256,7168]{1,0:T(8,128)(2,1)} %get-tuple-element.725, bf16[256,3584]{1,0:T(8,128)(2,1)} %get-tuple-element.724, s32[]{:T(128)S(6)} %select_n.27), kind=kOutput, calls=%fused_computation.23.clone.1 | convolution fusion | flops 3333284864 | bytes 29883396 | tf_op jit(solution)/shard_map/while/body/eval_jaxpr/dot_general | solution.py:23
  620.3 13.5 %exponential_reduce_fusion.11 = f32[7168]{0:T(1024)S(1)} fusion(f32[896,7168]{1,0:T(8,128)} %get-tuple-element.573, f32[7168]{0:T(1024)S(1)} %get-tuple-element.574, f32[7168]{0:T(1024)S(1)} %get-tuple-element.723, f32[896]{0:T(1024)S(1)} %dynamic_slice.93, f32[896]{0:T(1024)S(1)} %dynamic_slice.94), kind=kLoop, calls=%fused_computation.21.clone.1 | loop fusion | flops 51373056 | bytes 25783296 | tf_op jit(solution)/shard_map/while/body/eval_jaxpr/reduce_sum | solution.py:62
  635.2 13.4 %fusion.40 = (f32[7168]{0:T(1024)S(1)}, f32[896,7168]{1,0:T(8,128)}) fusion(f32[7168]{0:T(1024)S(1)} %get-tuple-element.723, f32[896]{0:T(1024)S(1)} %dynamic_slice.93, f32[896]{0:T(1024)S(1)} %dynamic_slice.94, bf16[256,7168]{1,0:T(8,128)(2,1)} %get-tuple-element.725, bf16[256,3584]{1,0:T(8,128)(2,1)} %get-tuple-element.724, s32[]{:T(128)S(6)} %select_n.27), kind=kOutput, calls=%fused_computation.23.clone.1 | convolution fusion | flops 3333284864 | bytes 29883396 | tf_op jit(solution)/shard_map/while/body/eval_jaxpr/dot_general | solution.py:23
  648.6 13.5 %exponential_reduce_fusion.11 = f32[7168]{0:T(1024)S(1)} fusion(f32[896,7168]{1,0:T(8,128)} %get-tuple-element.573, f32[7168]{0:T(1024)S(1)} %get-tuple-element.574, f32[7168]{0:T(1024)S(1)} %get-tuple-element.723, f32[896]{0:T(1024)S(1)} %dynamic_slice.93, f32[896]{0:T(1024)S(1)} %dynamic_slice.94), kind=kLoop, calls=%fused_computation.21.clone.1 | loop fusion | flops 51373056 | bytes 25783296 | tf_op jit(solution)/shard_map/while/body/eval_jaxpr/reduce_sum | solution.py:62
  662.1 33.1 %pmax.31 = f32[7168]{0:T(1024)S(1)} all-reduce(f32[7168]{0:T(1024)S(1)} %get-tuple-element.195), channel_id=1, replica_groups=mesh['aa'=8,'ba'=4] {'aa'}, use_global_device_ids=true, to_apply=%region_24.25 | all-reduce | flops 7168 | bytes 57344 | tf_op jit(solution)/shard_map/pmax | solution.py:72
  695.2 33.1 %psum.31 = f32[7168]{0:T(1024)S(1)} all-reduce(f32[7168]{0:T(1024)S(1)} %exponential_multiply_fusion), channel_id=1, replica_groups=mesh['aa'=8,'ba'=4] {'aa'}, use_global_device_ids=true, to_apply=%region_25.26 | all-reduce | flops 7168 | bytes 57344 | tf_op jit(solution)/shard_map/psum | solution.py:73
  (114 shorter events, 15.8 us)
Async XLA Ops:
  7.2 26.3 %all-gather.3.cloned.1.call-start = ((), (), s32[]{:S(2)}) async-start(), calls=%async_computation | async-start | bytes 2293760 | tf_op jit(solution)/shard_map/all_gather | solution.py:31
  7.9 94.5 %all-gather.5.cloned.1.call-start = ((), (), s32[]{:S(2)}) async-start(), calls=%async_computation.1 | async-start | bytes 4128768 | tf_op jit(solution)/shard_map/all_gather | solution.py:32
  413.8 135.1 %copy-start = (f32[7168]{0:T(1024)S(1)}, f32[7168]{0:T(1024)}, u32[]{:S(2)}) copy-start(f32[7168]{0:T(1024)} %custom-call.2) | copy-start | bytes 86020
  413.8 135.1 %copy-start.1 = (f32[7168]{0:T(1024)S(1)}, f32[7168]{0:T(1024)}, u32[]{:S(2)}) copy-start(f32[7168]{0:T(1024)} %custom-call.3) | copy-start | bytes 86020
  662.1 66.8 %copy-start.2 = (f32[3584]{0:T(1024)}, f32[3584]{0:T(1024)S(1)}, u32[]{:S(2)}) copy-start(f32[3584]{0:T(1024)S(1)} %get-tuple-element.750) | copy-start | bytes 43012
Sparse Core Ops, SparseCore 0:
  9.6 23.8 all-gather.2
  35.6 66.8 all-gather.4
where the time goes:
time: 738 us; the launch traced here: 736 us
  other arithmetic  214 us (29%)
  matrix products  214 us (29%)
  blocking collectives  176 us (24%)
  waiting for transfers between devices  93.2 us (13%)
  between operations  14.2 us (2%)
  local copies, waits for them, and re-layouts  13.3 us (2%)
  loops' own time  11.7 us (2%)
    dot_general x16, matrix products, cost_rows(): lax.dot_general(rows, whole_b, (((0,), (0,)), ((), ())), preferred_elemen...  214 us
    reduce_sum x8, other arithmetic, col_part(): summed = jnp.sum(jnp.exp(scores - upper[None, :]), 0)  108 us
    reduce_sum x8, other arithmetic, row_part(): return (upper, jnp.sum(jnp.exp(scores - upper[:, None]), 1))  100 us
    pmax x2, blocking collectives, per_device(): top_b = lax.pmax(col_upper, 'aa')  69 us
    all_gather x1, waiting for transfers between devices, per_device(): whole_b = lax.all_gather(acts_b, 'aa', axis=0, tiled=True)  67.1 us
    psum x2, blocking collectives, per_device(): total_b = lax.psum(col_sums * jnp.exp(col_upper - top_b), 'aa')  66.2 us
    all_gather x1, waiting for transfers between devices, per_device(): whole_a = lax.all_gather(acts_a, 'ba', axis=0, tiled=True)  24.7 us
    pmax x2, blocking collectives, per_device(): top = lax.pmax(row_upper, 'ba')  20.2 us
  transfers between devices with their start and end apart: 2, of which 2 were waited for; matrix products, arithmetic and copies ran while one was open for 0% of the time, Pallas kernels for 0%

commit v1 on v0

v1 whole, which is shorter than its diff:
```python
import functools
import math

import jax
import jax.numpy as jnp
from jax import lax
from jax.experimental import pallas as pl
from jax.experimental.pallas import tpu as pltpu
from jax.sharding import PartitionSpec as P

NA = 28672
NB = 28672
TOKENS = 256
epsilon = 0.01

f32 = jnp.float32
bf16 = jnp.bfloat16
VMEM = pl.BlockSpec(memory_space=pltpu.VMEM)

KAPPA = math.log2(math.e) * 2.0 / (TOKENS * epsilon)
LN2 = math.log(2.0)
SMALLEST = 2.0**-60


def params(mib):
    return pltpu.CompilerParams(vmem_limit_bytes=mib << 20)


def largest_tile(size, *options):
    for tile in options:
        if size % tile == 0:
            return tile
    return size


def lse_kernel(tm, tn, keep, lhs_ref, rhs_ref, bias_ref, max_in, sum_in, max_ref, sum_ref, *rest):
    if keep:
        tile_max_ref, kept_ref, first_block, second_block = rest
    else:
        first_block, second_block = rest
    blocks = (first_block, second_block)
    row_tiles = lhs_ref.shape[0] // tm
    total = row_tiles * (rhs_ref.shape[1] // tn)
    sub = 64
    lanes = tn // 128

    def cols(n):
        return pl.ds(pl.multiple_of(n * tn, tn), tn)

    def product(n, t, block):
        rows = pl.ds(pl.multiple_of(t * tm, tm), tm)
        block[...] = jnp.dot(lhs_ref[rows, :], rhs_ref[:, cols(n)], preferred_element_type=f32)

    def reduce(n, t, block, upper, total_sum):
        new = upper
        for k in range(tm // sub):
            rows = pl.ds(pl.multiple_of(t * tm + k * sub, sub), sub)
            bias = jnp.concatenate([bias_ref[rows, :]] * lanes, 1)
            x = block[k * sub : (k + 1) * sub, :] + bias
            block[k * sub : (k + 1) * sub, :] = x
            new = jnp.maximum(new, x.reshape(sub // 8, 8, tn).max(0))
        row = new.max(0, keepdims=True)
        new = jnp.broadcast_to(row, (8, tn))
        total_sum = total_sum * jnp.exp2((upper - new) * KAPPA)
        for k in range(tm // sub):
            rows = pl.ds(pl.multiple_of(t * tm + k * sub, sub), sub)
            p = jnp.exp2((block[k * sub : (k + 1) * sub, :] - row) * KAPPA)
            total_sum = total_sum + p.reshape(sub // 8, 8, tn).sum(0)
            if keep:
                kept_ref[rows, cols(n)] = p.astype(bf16)
        if keep:
            tile_max_ref[pl.ds(t, 1), cols(n)] = row
        return new, total_sum

    product(0, 0, first_block)

    def pair(k, carry):
        upper, total_sum = carry
        for half in range(2):
            step = 2 * k + half
            n = step // row_tiles
            t = step - n * row_tiles
            after = jnp.minimum(step + 1, total - 1)
            n_after = after // row_tiles
            upper = jnp.where(t == 0, jnp.broadcast_to(max_in[:, cols(n)], (8, tn)), upper)
            total_sum = jnp.where(t == 0, sum_in[:, cols(n)], total_sum)
            product(n_after, after - n_after * row_tiles, blocks[1 - half])
            upper, total_sum = reduce(n, t, blocks[half], upper, total_sum)
            max_ref[:, cols(n)] = upper[:1]
            sum_ref[:, cols(n)] = total_sum
        return upper, total_sum

    zeros = jnp.zeros((8, tn), f32)
    lax.fori_loop(0, total // 2, pair, (zeros, zeros))


def lse_start(n):
    return (jnp.full((1, n), -1e30, f32), jnp.zeros((8, n), f32))


def lse_call(lhs, rhs, bias, state, keep):
    m, n = lhs.shape[0], rhs.shape[1]
    tm = largest_tile(m, 896)
    tn = largest_tile(n, 512, 256)
    outs = [jax.ShapeDtypeStruct((1, n), f32), jax.ShapeDtypeStruct((8, n), f32)]
    if keep:
        outs += [jax.ShapeDtypeStruct((m // tm, n), f32), pltpu.VMEM((m, n), bf16)]
    bias = jnp.broadcast_to(bias[:, None], (m, 128))
    return pl.pallas_call(
        functools.partial(lse_kernel, tm, tn, keep),
        out_shape=outs,
        in_specs=[VMEM] * 5,
        out_specs=[VMEM] * len(outs),
        scratch_shapes=[pltpu.VMEM((tm, tn), f32)] * 2,
        compiler_params=params(13 if keep else 20),
    )(lhs, rhs, bias, *state)


def row_sum_kernel(kept_ref, weight_ref, out_ref, wide, partial):
    rows_here, cols_here = kept_ref.shape
    tiles = weight_ref.shape[0]
    tm = rows_here // tiles
    lanes = cols_here // 128

    @pl.loop(0, tiles)
    def _(t):
        wide[...] = jnp.broadcast_to(weight_ref[pl.ds(t, 1), :], (16, cols_here)).astype(bf16)

        @pl.loop(0, tm // 32)
        def _(g):
            start = pl.multiple_of(t * tm + g * 32, 32)
            acc = [jnp.zeros((16, 128), f32)] * 2
            for c in range(0, lanes, 4):
                part = [None, None]
                for k in range(c, min(c + 4, lanes)):
                    w = wide[:, k * 128 : (k + 1) * 128]
                    for h in range(2):
                        term = kept_ref[pl.ds(start + h * 16, 16), k * 128 : (k + 1) * 128] * w
                        part[h] = term if part[h] is None else part[h] + term
                for h in range(2):
                    acc[h] = acc[h] + part[h].astype(f32)
            for h in range(2):
                partial[pl.ds(start + h * 16, 16), :] = acc[h]

    @pl.loop(0, rows_here // 128)
    def _(g):
        rows = pl.ds(pl.multiple_of(g * 128, 128), 128)
        out_ref[:, rows] = jnp.sum(partial[rows, :].T, axis=0, keepdims=True)


def row_sum_call(kept, weight):
    return pl.pallas_call(
        row_sum_kernel,
        out_shape=jax.ShapeDtypeStruct((1, kept.shape[0]), f32),
        in_specs=[VMEM] * 2,
        out_specs=VMEM,
        scratch_shapes=[pltpu.VMEM((16, kept.shape[1]), bf16), pltpu.VMEM((kept.shape[0], 128), f32)],
        compiler_params=params(10),
    )(kept, weight)


def col_sum_kernel(kept_ref, weight_ref, scale_ref, out_ref):
    rows_here, cols_here = kept_ref.shape
    tiles = weight_ref.shape[0]
    tm = rows_here // tiles
    width = 512 if cols_here % 512 == 0 else 256

    @pl.loop(0, cols_here // width)
    def _(n):
        start = pl.multiple_of(n * width, width)

        def tile(t, total):
            def group(g, acc):
                acc = list(acc)
                first = pl.multiple_of(t * tm + g * 64, 64)
                scale = [scale_ref[pl.ds(first + h * 16, 16), :] for h in range(4)]
                for k in range(width // 128):
                    part = None
                    for h in range(4):
                        cols = pl.ds(pl.multiple_of(start + k * 128, 128), 128)
                        term = kept_ref[pl.ds(first + h * 16, 16), cols] * scale[h]
                        part = term if part is None else part + term
                    acc[k] = acc[k] + part.astype(f32)
                return tuple(acc)

            acc = lax.fori_loop(0, tm // 64, group, (jnp.zeros((16, 128), f32),) * (width // 128), unroll=2)
            acc = jnp.concatenate(acc, 1)
            return total + jnp.sum(acc, 0, keepdims=True) * weight_ref[pl.ds(t, 1), pl.ds(start, width)]

        out_ref[:, pl.ds(start, width)] = lax.fori_loop(0, tiles, tile, jnp.zeros((1, width), f32))


def col_sum_call(kept, weight, scale):
    wide = jnp.broadcast_to(scale.astype(bf16)[:, None], (scale.shape[0], 128))
    return pl.pallas_call(
        col_sum_kernel,
        out_shape=jax.ShapeDtypeStruct((1, kept.shape[1]), f32),
        in_specs=[VMEM] * 3,
        out_specs=VMEM,
        compiler_params=params(10),
    )(kept, weight, wide)


def group_steps(axis, size):
    step = 1
    while step < size:
        yield lambda x, s=step: lax.ppermute(x, axis, [(i, i ^ s) for i in range(size)])
        step *= 2


def group_lse(upper, total, exchange_steps):
    pair = jnp.stack([upper, total])
    for exchange in exchange_steps:
        other = exchange(pair)
        top = jnp.maximum(pair[0], other[0])
        total = pair[1] * jnp.exp2((pair[0] - top) * KAPPA) + other[1] * jnp.exp2((other[0] - top) * KAPPA)
        pair = jnp.stack([top, total])
    return KAPPA * pair[0] + jnp.log2(pair[1])


def group_sum(x, exchange_steps):
    for exchange in exchange_steps:
        x = x + exchange(x)
    return x


def per_device(aa_size, ba_size, acts_a, acts_b):
    def over_a():
        return group_steps("aa", aa_size)

    def over_b():
        return group_steps("ba", ba_size)

    whole_a = lax.all_gather(acts_a, "ba", axis=0, tiled=True)
    whole_b = lax.all_gather(acts_b, "aa", axis=0, tiled=True)
    turned_a = whole_a.T
    turned_b = whole_b.T
    norm_a = jnp.sum(jnp.square(whole_a.astype(f32)), 0)
    norm_b = jnp.sum(jnp.square(whole_b.astype(f32)), 0)
    rows_here, cols_here = norm_a.shape[0], norm_b.shape[0]
    log_n = math.log(NA)

    def row_pass(bias):
        upper, total = lse_call(turned_b, whole_a, bias, lse_start(rows_here), False)
        return group_lse(upper[0], total.sum(0), over_b())

    def potential_a_of(row_lse):
        return -epsilon * (log_n + LN2 * (row_lse - (0.5 * KAPPA) * norm_a))

    def potential_b_of(col_lse):
        return -epsilon * LN2 * (col_lse - (0.5 * KAPPA) * norm_b)

    row_lse = row_pass(-0.5 * norm_b)
    upper, total, tile_max, kept = lse_call(
        turned_a, whole_b, row_lse * (-1.0 / KAPPA), lse_start(cols_here), True
    )
    col_lse = group_lse(upper[0], total.sum(0), over_a())
    weight = jnp.exp2(KAPPA * tile_max - col_lse[None, :])
    kept = pltpu.with_memory_space_constraint(kept, pltpu.VMEM)
    row_sums = group_sum(row_sum_call(kept, weight)[0], over_b())
    low = jnp.min(row_sums) < SMALLEST
    safe = jnp.maximum(row_sums, SMALLEST)
    col_sums = col_sum_call(kept, weight, 1.0 / safe)[0]
    flagged = jnp.concatenate([col_sums, jnp.where(low, jnp.ones((128,), f32), 0.0)])
    flagged = group_sum(flagged, over_a())
    col_sums = flagged[:cols_here]

    def quick(_):
        return (
            potential_a_of(row_lse) - epsilon * jnp.log(safe),
            potential_b_of(col_lse) - epsilon * jnp.log(col_sums),
        )

    def exact(_):
        again = row_pass(col_lse * (-1.0 / KAPPA))
        upper, total = lse_call(
            turned_a, whole_b, again * (-1.0 / KAPPA), lse_start(cols_here), False
        )
        return potential_a_of(again), potential_b_of(group_lse(upper[0], total.sum(0), over_a()))

    return lax.cond(flagged[cols_here] > 0.0, exact, quick, 0)


def solution(mesh):
    in_specs = (P("ba", "aa"), P("aa", "ba"))
    out_specs = (P("aa"), P("ba"))
    return jax.shard_map(
        functools.partial(per_device, mesh.shape["aa"], mesh.shape["ba"]),
        mesh=mesh, in_specs=in_specs, out_specs=out_specs, check_vma=False,
    )
```

time: 738 us -> 329 us (0.45)
  matrix products: 214 us -> 0 us
  other arithmetic: 214 us -> 11.9 us
  blocking collectives: 176 us -> 0 us
  Pallas kernels: 0 us -> 117 us
  local copies, waits for them, and re-layouts: 13.3 us -> 65.2 us
  starting transfers between devices: 0.08 us -> 13 us
  waiting for transfers between devices: 93.2 us -> 106 us
  loops' own time: 11.7 us -> 0.03 us
    dot_general x16 -> x0, matrix products: 214 us -> none  [cost_rows(): lax.dot_general(rows, whole_b, (((0,), (0,)), ((), ())), preferred_elemen...]
    reduce_sum x18 -> x4, other arithmetic: 213 us -> 4.4 us  [the longest x1 2.98 us: per_device(): norm_b = jnp.sum(jnp.square(whole_b.astype(f32)), 0)]
    pallas_call x0 -> x4, Pallas kernels: none -> 117 us  [the longest x2 75.5 us: lse_call(): pl.pallas_call(functools.partial(lse_kernel, tm, tn, keep), out_shape=out...]
    pmax x4 -> x0, blocking collectives: 89.3 us -> none  [the longest x2 69 us: per_device(): top_b = lax.pmax(col_upper, 'aa')]
    psum x4 -> x0, blocking collectives: 86.4 us -> none  [the longest x2 66.2 us: per_device(): total_b = lax.psum(col_sums * jnp.exp(col_upper - top_b), 'aa')]
    unnamed x6 -> x14, local copies, waits for them, and re-layouts: 0.02 us -> 49.5 us
    ppermute x0 -> x10, waiting for transfers between devices: none -> 20.8 us  [group_steps(): lax.ppermute(x, axis, [(i, i ^ s) for i in range(size)])]
    ppermute x0 -> x10, starting transfers between devices: none -> 12.9 us  [group_steps(): lax.ppermute(x, axis, [(i, i ^ s) for i in range(size)])]
  transfers between devices with their start and end apart: 2 -> 12, of which waited for: 2 -> 12; matrix products, arithmetic and copies ran while one was open for 0% -> 4% of each run, Pallas kernels for 0% -> 0%
where the time goes in v1:
time: 329 us; the launch traced here: 328 us
  Pallas kernels  117 us (36%)
  waiting for transfers between devices  106 us (32%)
  local copies, waits for them, and re-layouts  65.2 us (20%)
  between operations  15.5 us (5%)
  starting transfers between devices  13 us (4%)
  other arithmetic  11.9 us (4%)
    pallas_call x2, Pallas kernels, lse_call(): pl.pallas_call(functools.partial(lse_kernel, tm, tn, keep), out_shape=out...  75.5 us
    all_gather x1, waiting for transfers between devices, per_device(): whole_b = lax.all_gather(acts_b, 'aa', axis=0, tiled=True)  71.1 us
    unnamed x14, local copies, waits for them, and re-layouts  49.5 us
    pallas_call x1, Pallas kernels, col_sum_call(): pl.pallas_call(col_sum_kernel, out_shape=jax.ShapeDtypeStruct((1, kept.sh...  24.2 us
    ppermute x10, waiting for transfers between devices, group_steps(): lax.ppermute(x, axis, [(i, i ^ s) for i in range(size)])  20.8 us
    pallas_call x1, Pallas kernels, row_sum_call(): pl.pallas_call(row_sum_kernel, out_shape=jax.ShapeDtypeStruct((1, kept.sh...  17.5 us
    ppermute x10, starting transfers between devices, group_steps(): lax.ppermute(x, axis, [(i, i ^ s) for i in range(size)])  12.9 us
    all_gather x1, waiting for transfers between devices, per_device(): whole_a = lax.all_gather(acts_a, 'ba', axis=0, tiled=True)  12.3 us
  transfers between devices with their start and end apart: 12, of which 12 were waited for; matrix products, arithmetic and copies ran while one was open for 4% of the time, Pallas kernels for 0%

profile of v1, /device:TPU:0, one launch (start us, length us, event | category | flops | bytes accessed | tf_op | source)
XLA Modules:
  0.0 328.3 jit_solution(7803260085161434463)
XLA Ops:
  7.2 0.7 all-gather.5.cloned.1.call-update
  7.9 0.7 all-gather.3.cloned.1.call-update
  8.6 71.1 %all-gather.5.cloned.1.call-done.rhs_ref = bf16[256,7168]{1,0:T(8,128)(2,1)} async-done(((bf16[32,7168]{1,0:T(8,128)(2,1)}), bf16[256,7168]{1,0:T(8,128)(2,1)}) %all-gather.5.cloned.1.call-update) | async-done | bytes 3670032 | tf_op jit(solution)/shard_map/all_gather | solution.py:235
  79.7 5.9 %copy.14.lhs_ref = bf16[7168,256]{1,0:T(8,128)(2,1)} copy(bf16[7168,256]{0,1:T(8,128)(2,1)} %bitcast.22) | data formatting | bytes 7340032 | tf_op jit(solution)/shard_map/transpose | solution.py:237
  85.6 3.0 multiply_reduce_fusion
  88.6 12.3 %all-gather.3.cloned.1.call-done.rhs_ref = bf16[256,3584]{1,0:T(8,128)(2,1)} async-done(((bf16[64,3584]{1,0:T(8,128)(2,1)}), bf16[256,3584]{1,0:T(8,128)(2,1)}) %all-gather.3.cloned.1.call-update) | async-done | bytes 1835024 | tf_op jit(solution)/shard_map/all_gather | solution.py:234
  100.9 1.0 broadcast_in_dim.11.bias_ref
  101.9 1.0 copy-done.3
  102.9 35.7 %shard_map.45 = (f32[1,3584]{1,0:T(1,128)S(1)}, f32[8,3584]{1,0:T(8,128)S(1)}) custom-call(bf16[7168,256]{1,0:T(8,128)(2,1)S(1)} %copy-done.3, bf16[256,3584]{1,0:T(8,128)(2,1)} %all-gather.3.cloned.1.call-done.rhs_ref, f32[7168,128]{1,0:T(8,128)S(1)} %broadcast_in_dim.11.bias_ref, f32[1,3584]{1,0:T(1,128)S(1)} %broadcast_71_max_in.2.max_in, ...), custom_call_target="tpu_custom_call" | custom-call | tf_op jit(solution)/shard_map/pallas_call | solution.py:109
  139.1 1.0 collective-permute-done.5
  140.6 2.3 copy.13
  142.9 1.3 collective-permute-done.6
  144.2 0.6 slice_reduce_fusion.4
  144.8 1.8 broadcast_in_dim.12.bias_ref
  146.6 0.7 broadcast_64_sum_in.2.sum_in
  147.3 0.6 broadcast_65_max_in.2.max_in
  148.0 39.8 %shard_map.46 = (f32[1,7168]{1,0:T(1,128)}, f32[8,7168]{1,0:T(8,128)}, f32[4,7168]{1,0:T(4,128)}, bf16[3584,7168]{1,0:T(8,128)(2,1)S(1)}) custom-call(bf16[3584,256]{1,0:T(8,128)(2,1)} %bitcast.25, bf16[256,7168]{1,0:T(8,128)(2,1)} %all-gather.5.cloned.1.call-done.rhs_ref, f32[3584,128]{1,0:T(8,128)} %broadcast_in_dim.12.bias_ref, ...), custom_call_target="tpu_custom_call" | custom-call | tf_op jit(solution)/shard_map/pallas_call | solution.py:109
  187.8 16.9 %copy-done = bf16[3584,7168]{1,0:T(8,128)(2,1)} copy-done((bf16[3584,7168]{1,0:T(8,128)(2,1)}, bf16[3584,7168]{1,0:T(8,128)(2,1)S(1)}, u32[]{:S(2)}) %copy-start) | copy-done | bytes 51380248
  204.7 1.0 reduce_sum.56
  205.7 0.8 pad_maximum_fusion.5
  206.5 1.5 collective-permute-start.7
  208.0 2.7 collective-permute-done.7
  210.7 0.9 multiply_add_fusion.7
  211.7 1.6 collective-permute-start.8
  213.2 2.7 collective-permute-done.8
  216.1 2.8 collective-permute-start.9
  219.0 2.3 collective-permute-done.9
  221.4 1.6 multiply_exponential_fusion.weight_ref
  223.0 15.8 %copy-done.1 = bf16[3584,7168]{1,0:T(8,128)(2,1)S(1)} copy-done((bf16[3584,7168]{1,0:T(8,128)(2,1)S(1)}, bf16[3584,7168]{1,0:T(8,128)(2,1)}, u32[]{:S(2)}) %copy-start.1) | copy-done | bytes 51380248
  238.8 17.5 %shard_map.47 = f32[1,3584]{1,0:T(1,128)} custom-call(bf16[3584,7168]{1,0:T(8,128)(2,1)S(1)} %copy-done.1, f32[4,7168]{1,0:T(4,128)} %multiply_exponential_fusion.weight_ref), custom_call_target="tpu_custom_call" | custom-call | tf_op jit(solution)/shard_map/pallas_call | solution.py:152
  256.3 0.8 reduce.12
  257.1 1.2 collective-permute-done.10
  258.7 3.3 %collective-permute-done.11 = f32[3584]{0:T(1024)S(1)} collective-permute-done((f32[3584]{0:T(1024)S(1)}, f32[3584]{0:T(1024)S(1)}, u32[]{:S(2)}, u32[]{:S(2)}) %collective-permute-start.11) | collective-permute-done | bytes 14368 | tf_op jit(solution)/shard_map/ppermute | solution.py:207
  262.0 0.7 divide_convert_fusion
  262.7 1.5 broadcast_in_dim.13.scale_ref
  264.1 15.8 %copy-done.2 = bf16[3584,7168]{1,0:T(8,128)(2,1)S(1)} copy-done((bf16[3584,7168]{1,0:T(8,128)(2,1)S(1)}, bf16[3584,7168]{1,0:T(8,128)(2,1)}, u32[]{:S(2)}) %copy-start.2) | copy-done | bytes 51380248
  279.9 24.2 %shard_map.48 = f32[1,7168]{1,0:T(1,128)} custom-call(bf16[3584,7168]{1,0:T(8,128)(2,1)S(1)} %copy-done.2, f32[4,7168]{1,0:T(4,128)} %multiply_exponential_fusion.weight_ref, bf16[3584,128]{1,0:T(8,128)(2,1)} %broadcast_in_dim.13.scale_ref), custom_call_target="tpu_custom_call" | custom-call | tf_op jit(solution)/shard_map/pallas_call | solution.py:195
  304.7 0.8 concatenate.3
  305.5 1.5 collective-permute-start.12
  306.9 2.5 collective-permute-done.12
  309.4 0.8 pad_add_fusion
  310.1 1.5 collective-permute-start.13
  312.0 2.0 collective-permute-done.13
  314.1 2.9 collective-permute-start.14
  317.0 1.9 collective-permute-done.14
  320.1 1.4 conditional.1
  320.2 0.6 multiply_subtract_fusion.1
  320.8 0.6 multiply_subtract_fusion
  (38 shorter events, 3.0 us)
Async XLA Ops:
  7.2 72.6 %all-gather.5.cloned.1.call-start = ((), (), s32[]{:S(2)}) async-start(), calls=%async_computation.1 | async-start | bytes 4128768 | tf_op jit(solution)/shard_map/all_gather | solution.py:235
  7.9 93.0 %all-gather.3.cloned.1.call-start = ((), (), s32[]{:S(2)}) async-start(), calls=%async_computation | async-start | bytes 2293760 | tf_op jit(solution)/shard_map/all_gather | solution.py:234
  100.9 2.0 copy-start.3
  102.9 37.7 %copy-start.5 = (bf16[256,3584]{1,0:T(8,128)(2,1)S(1)}, bf16[256,3584]{1,0:T(8,128)(2,1)}, u32[]{:S(2)}) copy-start(bf16[256,3584]{1,0:T(8,128)(2,1)} %all-gather.3.cloned.1.call-done.rhs_ref) | copy-start | bytes 5505028
  138.8 1.3 collective-permute-start.5
  140.2 3.9 %collective-permute-start.6 = (f32[2,3584]{1,0:T(2,128)S(1)}, f32[2,3584]{1,0:T(2,128)S(1)}, u32[]{:S(2)}, u32[]{:S(2)}) collective-permute-start(f32[2,3584]{1,0:T(2,128)S(1)} %pad_maximum_fusion.9), channel_id=1, source_target_pairs={{0,2},{1,3},{2,0},{3,1},{4,6},{5,7},{6,4},{7,5},{8,10},{9,11},{10,... | collective-permute-start | bytes 86024 | tf_op jit(solution)/shard_map/ppermute | solution.py:207
  187.8 16.9 %copy-start = (bf16[3584,7168]{1,0:T(8,128)(2,1)}, bf16[3584,7168]{1,0:T(8,128)(2,1)S(1)}, u32[]{:S(2)}) copy-start(bf16[3584,7168]{1,0:T(8,128)(2,1)S(1)} %get-tuple-element.113.kept_ref) | copy-start | bytes 154140672
  206.5 4.2 %collective-permute-start.7 = (f32[2,7168]{1,0:T(2,128)S(1)}, f32[2,7168]{1,0:T(2,128)S(1)}, u32[]{:S(2)}, u32[]{:S(2)}) collective-permute-start(f32[2,7168]{1,0:T(2,128)S(1)} %pad_maximum_fusion.5), channel_id=1, source_target_pairs={{0,4},{4,0},{8,12},{12,8},{16,20},{20,16},{24,28},{28,24},{1,5},{5... | collective-permute-start | bytes 172040 | tf_op jit(solution)/shard_map/ppermute | solution.py:207
  211.7 4.2 %collective-permute-start.8 = (f32[2,7168]{1,0:T(2,128)S(1)}, f32[2,7168]{1,0:T(2,128)S(1)}, u32[]{:S(2)}, u32[]{:S(2)}) collective-permute-start(f32[2,7168]{1,0:T(2,128)S(1)} %pad_maximum_fusion.6), channel_id=1, source_target_pairs={{0,8},{4,12},{8,0},{12,4},{16,24},{20,28},{24,16},{28,20},{1,9},{5... | collective-permute-start | bytes 172040 | tf_op jit(solution)/shard_map/ppermute | solution.py:207
  216.1 5.1 %collective-permute-start.9 = (f32[2,7168]{1,0:T(2,128)S(1)}, f32[2,7168]{1,0:T(2,128)S(1)}, u32[]{:S(2)}, u32[]{:S(2)}) collective-permute-start(f32[2,7168]{1,0:T(2,128)S(1)} %pad_maximum_fusion.7), channel_id=1, source_target_pairs={{0,16},{4,20},{8,24},{12,28},{16,0},{20,4},{24,8},{28,12},{1,17},{... | collective-permute-start | bytes 172040 | tf_op jit(solution)/shard_map/ppermute | solution.py:207
  223.0 15.8 %copy-start.1 = (bf16[3584,7168]{1,0:T(8,128)(2,1)S(1)}, bf16[3584,7168]{1,0:T(8,128)(2,1)}, u32[]{:S(2)}) copy-start(bf16[3584,7168]{1,0:T(8,128)(2,1)} %copy-done) | copy-start | bytes 154140672
  257.0 1.2 collective-permute-start.10
  258.3 3.7 %collective-permute-start.11 = (f32[3584]{0:T(1024)S(1)}, f32[3584]{0:T(1024)S(1)}, u32[]{:S(2)}, u32[]{:S(2)}) collective-permute-start(f32[3584]{0:T(1024)S(1)} %add.134), channel_id=1, source_target_pairs={{0,2},{1,3},{2,0},{3,1},{4,6},{5,7},{6,4},{7,5},{8,10},{9,11},{10,... | collective-permute-start | bytes 43016 | tf_op jit(solution)/shard_map/ppermute | solution.py:207
  264.1 15.8 %copy-start.2 = (bf16[3584,7168]{1,0:T(8,128)(2,1)S(1)}, bf16[3584,7168]{1,0:T(8,128)(2,1)}, u32[]{:S(2)}) copy-start(bf16[3584,7168]{1,0:T(8,128)(2,1)} %copy-done) | copy-start | bytes 154140672
  279.9 37.0 %copy-start.6 = (f32[1,7168]{1,0:T(1,128)S(1)}, f32[1,7168]{1,0:T(1,128)}, u32[]{:S(2)}) copy-start(f32[1,7168]{1,0:T(1,128)} %get-tuple-element.115) | copy-start | bytes 86020
  279.9 40.2 %copy-start.7 = (f32[1,3584]{1,0:T(1,128)S(1)}, f32[1,3584]{1,0:T(1,128)}, u32[]{:S(2)}) copy-start(f32[1,3584]{1,0:T(1,128)} %get-tuple-element.177) | copy-start | bytes 43012
  305.5 3.9 %collective-permute-start.12 = (f32[7296]{0:T(1024)S(1)}, f32[7296]{0:T(1024)S(1)}, u32[]{:S(2)}, u32[]{:S(2)}) collective-permute-start(f32[7296]{0:T(1024)S(1)} %concatenate.3), channel_id=1, source_target_pairs={{0,4},{4,0},{8,12},{12,8},{16,20},{20,16},{24,28},{28,24},{1,5},{5... | collective-permute-start | bytes 87560 | tf_op jit(solution)/shard_map/ppermute | solution.py:207
  310.1 3.9 %collective-permute-start.13 = (f32[7296]{0:T(1024)S(1)}, f32[7296]{0:T(1024)S(1)}, u32[]{:S(2)}, u32[]{:S(2)}) collective-permute-start(f32[7296]{0:T(1024)S(1)} %pad_add_fusion), channel_id=1, source_target_pairs={{0,8},{4,12},{8,0},{12,4},{16,24},{20,28},{24,16},{28,20},{1,9},{5... | collective-permute-start | bytes 87560 | tf_op jit(solution)/shard_map/ppermute | solution.py:207
  314.1 4.8 %collective-permute-start.14 = (f32[7296]{0:T(1024)S(1)}, f32[7296]{0:T(1024)S(1)}, u32[]{:S(2)}, u32[]{:S(2)}) collective-permute-start(f32[7296]{0:T(1024)S(1)} %add.137), channel_id=1, source_target_pairs={{0,16},{4,20},{8,24},{12,28},{16,0},{20,4},{24,8},{28,12},{1,17},{... | collective-permute-start | bytes 87560 | tf_op jit(solution)/shard_map/ppermute | solution.py:207
Sparse Core Ops, SparseCore 0:
  10.2 69.4 all-gather.4
  81.3 19.5 all-gather.2

commit v2 on v1

v2 whole, which is shorter than its diff:
```python
import functools
import math

import jax
import jax.numpy as jnp
from jax import lax
from jax.experimental import pallas as pl
from jax.experimental.pallas import tpu as pltpu
from jax.sharding import PartitionSpec as P

NA = 28672
NB = 28672
TOKENS = 256
epsilon = 0.01

f32 = jnp.float32
bf16 = jnp.bfloat16
VMEM = pl.BlockSpec(memory_space=pltpu.VMEM)

KAPPA = math.log2(math.e) * 2.0 / (TOKENS * epsilon)
LN2 = math.log(2.0)
SMALLEST = 2.0**-60


def params(mib):
    return pltpu.CompilerParams(vmem_limit_bytes=mib << 20)


def lse_kernel(tm, tn, biased, chained, keep, lhs_ref, rhs_ref, *rest):
    rest = list(rest)
    bias_ref = rest.pop(0) if biased else None
    state_in = rest.pop(0) if chained else None
    state_ref = rest.pop(0)
    norm_ref = None if biased else rest.pop(0)
    if keep:
        tile_max_ref, kept_ref = rest.pop(0), rest.pop(0)
    turned, wide, *blocks = rest
    row_tiles = lhs_ref.shape[1] // tm
    total = row_tiles * (rhs_ref.shape[1] // tn)
    sub = 64
    lanes = tn // 128

    @pl.loop(0, lhs_ref.shape[1] // 128)
    def _(g):
        rows = pl.ds(pl.multiple_of(g * 128, 128), 128)
        turned[rows, :] = lhs_ref[:, rows].T
        if biased:
            bias = bias_ref[:, rows]
        else:
            norm = jnp.sum(jnp.square(lhs_ref[:, rows].astype(f32)), 0, keepdims=True)
            norm_ref[:, rows] = norm
            bias = -0.5 * norm
        wide[rows, :] = jnp.broadcast_to(bias, (128, 128)).T

    def cols(n):
        return pl.ds(pl.multiple_of(n * tn, tn), tn)

    def product(n, t, block):
        rows = pl.ds(pl.multiple_of(t * tm, tm), tm)
        block[...] = jnp.dot(turned[rows, :], rhs_ref[:, cols(n)], preferred_element_type=f32)

    def reduce(n, t, block, upper, total_sum):
        new = upper
        for k in range(tm // sub):
            rows = pl.ds(pl.multiple_of(t * tm + k * sub, sub), sub)
            bias = jnp.concatenate([wide[rows, :]] * lanes, 1)
            x = block[k * sub : (k + 1) * sub, :] + bias
            block[k * sub : (k + 1) * sub, :] = x
            new = jnp.maximum(new, x.reshape(sub // 8, 8, tn).max(0))
        row = new.max(0, keepdims=True)
        new = jnp.broadcast_to(row, (8, tn))
        total_sum = total_sum * jnp.exp2((upper - new) * KAPPA)
        for k in range(tm // sub):
            rows = pl.ds(pl.multiple_of(t * tm + k * sub, sub), sub)
            p = jnp.exp2((block[k * sub : (k + 1) * sub, :] - row) * KAPPA)
            total_sum = total_sum + p.reshape(sub // 8, 8, tn).sum(0)
            if keep:
                kept_ref[rows, cols(n)] = p.astype(bf16)
        if keep:
            tile_max_ref[pl.ds(t, 1), cols(n)] = row
        return new, total_sum

    product(0, 0, blocks[0])
    first_sublane = lax.broadcasted_iota(jnp.int32, (8, tn), 0) == 0

    def pair(k, carry):
        upper, total_sum = carry
        for half in range(2):
            step = 2 * k + half
            n = step // row_tiles
            t = step - n * row_tiles
            after = jnp.minimum(step + 1, total - 1)
            n_after = after // row_tiles
            if chained:
                start = state_in[:, cols(n)]
                start_max = jnp.broadcast_to(start[:1], (8, tn))
                start_sum = jnp.where(first_sublane, jnp.broadcast_to(start[1:], (8, tn)), 0.0)
            else:
                start_max, start_sum = jnp.full((8, tn), -1e30, f32), jnp.zeros((8, tn), f32)
            upper = jnp.where(t == 0, start_max, upper)
            total_sum = jnp.where(t == 0, start_sum, total_sum)
            product(n_after, after - n_after * row_tiles, blocks[1 - half])
            upper, total_sum = reduce(n, t, blocks[half], upper, total_sum)
            state_ref[0:1, cols(n)] = upper[:1]
            state_ref[1:2, cols(n)] = jnp.sum(total_sum, 0, keepdims=True)
        return upper, total_sum

    zeros = jnp.zeros((8, tn), f32)
    lax.fori_loop(0, total // 2, pair, (zeros, zeros))


def lse_call(lhs, rhs, bias=None, state=None, keep=False):
    depth, m = lhs.shape
    n = rhs.shape[1]
    tm, tn = (896, 512) if n % 512 == 0 else (448, 896)
    outs = [jax.ShapeDtypeStruct((2, n), f32)]
    operands = [lhs, rhs]
    if bias is None:
        outs += [jax.ShapeDtypeStruct((1, m), f32)]
    else:
        operands += [bias]
    if state is not None:
        operands += [state]
    if keep:
        outs += [jax.ShapeDtypeStruct((m // tm, n), f32), pltpu.VMEM((m, n), bf16)]
    return pl.pallas_call(
        functools.partial(lse_kernel, tm, tn, bias is not None, state is not None, keep),
        out_shape=outs,
        in_specs=[VMEM] * len(operands),
        out_specs=[VMEM] * len(outs),
        scratch_shapes=[pltpu.VMEM((m, depth), bf16), pltpu.VMEM((m, 128), f32)]
        + [pltpu.VMEM((tm, tn), f32)] * 2,
        compiler_params=params(12),
        cost_estimate=pl.CostEstimate(flops=512 * m * n, bytes_accessed=512 * (m + n), transcendentals=m * n),
    )(*operands)


def reorder_kernel(tokens, table_ref, arrived_ref, out_ref, norm_ref):
    for p in range(table_ref.shape[0]):
        start = pl.multiple_of(table_ref[p] * tokens, tokens)
        out_ref[p * tokens : (p + 1) * tokens, :] = arrived_ref[pl.ds(start, tokens), :]

    @pl.loop(0, arrived_ref.shape[1] // 128)
    def _(g):
        cols = pl.ds(pl.multiple_of(g * 128, 128), 128)
        norm_ref[:, cols] = jnp.sum(jnp.square(arrived_ref[:, cols].astype(f32)), 0, keepdims=True)


def reorder_call(arrived, table, tokens):
    return pl.pallas_call(
        functools.partial(reorder_kernel, tokens),
        out_shape=[
            jax.ShapeDtypeStruct(arrived.shape, bf16),
            jax.ShapeDtypeStruct((1, arrived.shape[1]), f32),
        ],
        in_specs=[pl.BlockSpec(memory_space=pltpu.SMEM), VMEM],
        out_specs=[VMEM] * 2,
        compiler_params=params(8),
    )(table, arrived)


def weights(tile_max_ref, lse_ref, t):
    return jnp.exp2(KAPPA * tile_max_ref[pl.ds(t, 1), :] - lse_ref[...])


def row_sum_kernel(chained, kept_ref, tile_max_ref, lse_ref, *rest):
    rest = list(rest)
    first = rest.pop(0) if chained else None
    out_ref, wide, partial = rest
    rows_here, cols_here = kept_ref.shape
    tiles = tile_max_ref.shape[0]
    tm = rows_here // tiles
    span, lane_block, height = 1024, 256, 64

    @pl.loop(0, tiles)
    def _(t):
        wide[...] = jnp.broadcast_to(weights(tile_max_ref, lse_ref, t), (16, cols_here)).astype(bf16)

        @pl.loop(0, tm // height)
        def _(g):
            rows = pl.ds(pl.multiple_of(t * tm + g * height, height), height)
            acc = jnp.zeros((height, 128), f32)
            for c in range(0, cols_here, span):
                part = None
                for k in range(c, min(c + span, cols_here), lane_block):
                    w = jnp.concatenate([wide[:, k : k + lane_block]] * (height // 16), 0)
                    term = kept_ref[rows, k : k + lane_block] * w
                    part = term if part is None else part + term
                part = part.astype(f32)
                for k in range(0, lane_block, 128):
                    acc = acc + part[:, k : k + 128]
            partial[rows, :] = acc

    @pl.loop(0, rows_here // 128)
    def _(g):
        rows = pl.ds(pl.multiple_of(g * 128, 128), 128)
        total = jnp.sum(partial[rows, :].T, axis=0, keepdims=True)
        out_ref[:, rows] = first[:, rows] + total if chained else total


def row_sum_call(kept, tile_max, lse, first=None):
    operands = (kept, tile_max, lse) if first is None else (kept, tile_max, lse, first)
    m, n = kept.shape
    return pl.pallas_call(
        functools.partial(row_sum_kernel, first is not None),
        out_shape=jax.ShapeDtypeStruct((1, m), f32),
        in_specs=[VMEM] * len(operands),
        out_specs=VMEM,
        scratch_shapes=[pltpu.VMEM((16, n), bf16), pltpu.VMEM((m, 128), f32)],
        compiler_params=params(6),
        cost_estimate=pl.CostEstimate(flops=2 * m * n, bytes_accessed=2 * m * n, transcendentals=0),
    )(*operands)


def col_sum_kernel(kept_ref, tile_max_ref, lse_ref, row_sum_ref, out_ref, wide):
    rows_here, cols_here = kept_ref.shape
    tiles = tile_max_ref.shape[0]
    tm = rows_here // tiles
    width = 896

    @pl.loop(0, rows_here // 128)
    def _(g):
        rows = pl.ds(pl.multiple_of(g * 128, 128), 128)
        scale = 1.0 / jnp.maximum(row_sum_ref[:, rows], SMALLEST)
        wide[rows, :] = jnp.broadcast_to(scale, (128, 128)).T.astype(bf16)

    least = jnp.min(row_sum_ref[...], axis=1, keepdims=True)
    out_ref[:, cols_here:] = jnp.broadcast_to(jnp.where(least < SMALLEST, 1.0, 0.0), (1, 128))

    @pl.loop(0, cols_here // width)
    def _(n):
        start = pl.multiple_of(n * width, 128)

        def tile(t, total):
            acc = jnp.zeros((16, width), f32)
            for g in range(tm // 64):
                part = None
                for h in range(4):
                    rows = pl.ds(pl.multiple_of(t * tm + g * 64 + h * 16, 16), 16)
                    scale = jnp.concatenate([wide[rows, :]] * (width // 128), 1)
                    term = kept_ref[rows, pl.ds(start, width)] * scale
                    part = term if part is None else part + term
                acc = acc + part.astype(f32)
            acc = jnp.sum(acc, 0, keepdims=True)
            cols = pl.ds(start, width)
            return total + acc * jnp.exp2(KAPPA * tile_max_ref[pl.ds(t, 1), cols] - lse_ref[:, cols])

        out_ref[:, pl.ds(start, width)] = lax.fori_loop(0, tiles, tile, jnp.zeros((1, width), f32))


def col_sum_call(kept, tile_max, lse, row_sums):
    m, n = kept.shape
    return pl.pallas_call(
        col_sum_kernel,
        out_shape=jax.ShapeDtypeStruct((1, n + 128), f32),
        in_specs=[VMEM] * 4,
        out_specs=VMEM,
        scratch_shapes=[pltpu.VMEM((m, 128), bf16)],
        compiler_params=params(6),
        cost_estimate=pl.CostEstimate(flops=2 * m * n, bytes_accessed=2 * m * n, transcendentals=0),
    )(kept, tile_max, lse, row_sums)


def group_steps(axis, size):
    step = 1
    while step < size:
        yield lambda x, s=step: lax.ppermute(x, axis, [(i, i ^ s) for i in range(size)])
        step *= 2


def group_lse(pair, exchange_steps):
    for exchange in exchange_steps:
        other = exchange(pair)
        top = jnp.maximum(pair[:1], other[:1])
        total = pair[1:] * jnp.exp2((pair[:1] - top) * KAPPA) + other[1:] * jnp.exp2((other[:1] - top) * KAPPA)
        pair = jnp.concatenate([top, total], 0)
    return KAPPA * pair[:1] + jnp.log2(pair[1:])


def group_sum(x, exchange_steps):
    for exchange in exchange_steps:
        x = x + exchange(x)
    return x


def swap(x, axis, size, mask):
    return lax.ppermute(x, axis, [(i, i ^ mask) for i in range(size)])


def gather_order(size, near):
    far = size // near
    return [f * near + k for k in range(near) for f in range(far)]


def gather_near(x, axis, size, near):
    mine = jnp.concatenate([x] + [swap(x, axis, size, f * near) for f in range(1, size // near)], 0)
    return jnp.concatenate([mine] + [swap(mine, axis, size, k) for k in range(1, near)], 0)


CHUNKS = 4
HALVES = 2


def per_device(aa_size, ba_size, acts_a, acts_b):
    def over_a():
        return group_steps("aa", aa_size)

    def over_b():
        return group_steps("ba", ba_size)

    cols_here = acts_b.shape[1]
    width = cols_here // CHUNKS
    half = cols_here // HALVES
    near = aa_size // 4
    far_masks = [f * near for f in range(1, 4)]

    tokens = acts_b.shape[0]
    per_block = aa_size // ba_size
    arrival = gather_order(ba_size, 2)
    place = jnp.array([arrival.index(v) for v in range(ba_size)], jnp.int32)
    token_block = lax.axis_index("aa") ^ jnp.array(gather_order(aa_size, near), jnp.int32)
    table = place[(token_block // per_block) ^ lax.axis_index("ba")] * per_block + token_block % per_block
    whole_a, norm_a = reorder_call(gather_near(acts_a, "ba", ba_size, 2), table, tokens)

    chunks, norms_b = [], []
    state = None
    states = []
    for c in range(CHUNKS):
        own = acts_b[:, c * width : (c + 1) * width]
        group = [own] + [swap(own, "aa", aa_size, mask) for mask in far_masks]
        if c >= 2:
            group, states[c - 2] = lax.optimization_barrier((group, states[c - 2]))
        mine = jnp.concatenate(group, 0)
        chunk = jnp.concatenate([mine] + [swap(mine, "aa", aa_size, k) for k in range(1, near)], 0)
        state, norm = lse_call(chunk, whole_a, None, states[c - 1] if c else None)
        states.append(state)
        chunks.append(chunk)
        norms_b.append(norm)
    row_lse = group_lse(states[-1], over_b())
    per_half = CHUNKS // HALVES
    norms_b = [jnp.concatenate(norms_b[h * per_half : (h + 1) * per_half], 1) for h in range(HALVES)]
    halves = [jnp.concatenate(chunks[h * per_half : (h + 1) * per_half], 1) for h in range(HALVES)]
    log_n = math.log(NA)

    def potential_a_of(row_lse):
        return -epsilon * (log_n + LN2 * (row_lse - (0.5 * KAPPA) * norm_a))

    def potential_b_of(col_lse, norm_b):
        return -epsilon * LN2 * (col_lse - (0.5 * KAPPA) * norm_b)

    col_lse, tile_max, kept = [], [], []
    for part in halves:
        state, top, p = lse_call(whole_a, part, row_lse * (-1.0 / KAPPA), keep=True)
        col_lse.append(group_lse(state, over_a()))
        tile_max.append(top)
        kept.append(pltpu.with_memory_space_constraint(p, pltpu.VMEM))
    row_sums = None
    for h in range(HALVES):
        row_sums = row_sum_call(kept[h], tile_max[h], col_lse[h], row_sums)
    row_sums = group_sum(row_sums, over_b())
    col_sums = []
    for h in range(HALVES):
        sums = col_sum_call(kept[h], tile_max[h], col_lse[h], row_sums)
        col_sums.append(group_sum(sums, over_a()))

    def quick(_):
        second_a = potential_a_of(row_lse) - epsilon * jnp.log(row_sums)
        second_b = [
            potential_b_of(col_lse[h], norms_b[h]) - epsilon * jnp.log(col_sums[h][:, :half])
            for h in range(HALVES)
        ]
        return second_a, jnp.concatenate(second_b, 1)

    def exact(_):
        state = None
        for part, lse in zip(halves, col_lse):
            (state,) = lse_call(part, whole_a, lse * (-1.0 / KAPPA), state)
        again = group_lse(state, over_b())
        second_b = []
        for part, norm_b in zip(halves, norms_b):
            (state,) = lse_call(whole_a, part, again * (-1.0 / KAPPA))
            second_b.append(potential_b_of(group_lse(state, over_a()), norm_b))
        return potential_a_of(again), jnp.concatenate(second_b, 1)

    second_a, second_b = lax.cond(col_sums[0][0, half] > 0.0, exact, quick, 0)
    return second_a.reshape(-1), second_b.reshape(-1)


def solution(mesh):
    in_specs = (P("ba", "aa"), P("aa", "ba"))
    out_specs = (P("aa"), P("ba"))
    return jax.shard_map(
        functools.partial(per_device, mesh.shape["aa"], mesh.shape["ba"]),
        mesh=mesh, in_specs=in_specs, out_specs=out_specs, check_vma=False,
    )
```

time: 329 us -> 240 us (0.73)
  waiting for transfers between devices: 106 us -> 51.4 us
  local copies, waits for them, and re-layouts: 65.2 us -> 28.4 us
  starting transfers between devices: 13 us -> 41.3 us
  between operations: 15.5 us -> 1.8 us
  other arithmetic: 11.9 us -> 5.5 us
  Pallas kernels: 117 us -> 111 us
    all_gather x2 -> x0, waiting for transfers between devices: 83.3 us -> none  [the longest x1 71.1 us: per_device(): whole_b = lax.all_gather(acts_b, 'aa', axis=0, tiled=True)]
    ppermute x0 -> x18, waiting for transfers between devices: none -> 33.1 us  [swap(): return lax.ppermute(x, axis, [(i, i ^ mask) for i in range(size)])]
    ppermute x0 -> x18, starting transfers between devices: none -> 27.4 us  [swap(): return lax.ppermute(x, axis, [(i, i ^ mask) for i in range(size)])]
    unnamed x14 -> x34, local copies, waits for them, and re-layouts: 49.5 us -> 25.3 us
    pallas_call x4 -> x11, Pallas kernels: 117 us -> 111 us  [the longest x6 84.5 us: lse_call(): pl.pallas_call(functools.partial(lse_kernel, tm, tn, bias is not None, st...]
    transpose x1 -> x0, local copies, waits for them, and re-layouts: 5.9 us -> none  [per_device(): turned_b = whole_b.T]
    reduce_sum x4 -> x0, other arithmetic: 4.4 us -> none  [the longest x1 2.98 us: per_device(): norm_b = jnp.sum(jnp.square(whole_b.astype(f32)), 0)]
    broadcast_in_dim x3 -> x0, local copies, waits for them, and re-layouts: 4.27 us -> none  [the longest x2 2.79 us: lse_call(): bias = jnp.broadcast_to(bias[:, None], (m, 128))]
  transfers between devices with their start and end apart: 12 -> 34, of which waited for: 12 -> 20; matrix products, arithmetic and copies ran while one was open for 4% -> 2% of each run, Pallas kernels for 0% -> 26%
where the time goes in v2:
time: 240 us; the launch traced here: 239 us
  Pallas kernels  111 us (46%)
  waiting for transfers between devices  51.4 us (21%)
  starting transfers between devices  41.3 us (17%)
  local copies, waits for them, and re-layouts  28.4 us (12%)
  other arithmetic  5.5 us (2%)
    pallas_call x6, Pallas kernels, lse_call(): pl.pallas_call(functools.partial(lse_kernel, tm, tn, bias is not None, st...  84.5 us
    ppermute x18, waiting for transfers between devices, swap(): return lax.ppermute(x, axis, [(i, i ^ mask) for i in range(size)])  33.1 us
    ppermute x18, starting transfers between devices, swap(): return lax.ppermute(x, axis, [(i, i ^ mask) for i in range(size)])  27.4 us
    unnamed x34, local copies, waits for them, and re-layouts  25.3 us
    ppermute x16, waiting for transfers between devices, group_steps(): lax.ppermute(x, axis, [(i, i ^ s) for i in range(size)])  18.3 us
    ppermute x16, starting transfers between devices, group_steps(): lax.ppermute(x, axis, [(i, i ^ s) for i in range(size)])  13.9 us
    pallas_call x2, Pallas kernels, row_sum_call(): pl.pallas_call(functools.partial(row_sum_kernel, first is not None), out_...  12.3 us
    pallas_call x2, Pallas kernels, col_sum_call(): pl.pallas_call(col_sum_kernel, out_shape=jax.ShapeDtypeStruct((1, n + 128...  12.2 us
  transfers between devices with their start and end apart: 34, of which 20 were waited for; matrix products, arithmetic and copies ran while one was open for 2% of the time, Pallas kernels for 26%

profile of v2, /device:TPU:0, one launch (start us, length us, event | category | flops | bytes accessed | tf_op | source)
XLA Modules:
  0.0 239.3 jit_solution(17709541448355311584)
XLA Ops:
  1.8 5.1 %collective-permute-start.24 = (bf16[32,1792]{1,0:T(8,128)(2,1)S(1)}, bf16[32,1792]{1,0:T(8,128)(2,1)S(1)}, u32[]{:S(2)}, u32[]{:S(2)}) collective-permute-start(bf16[32,1792]{1,0:T(8,128)(2,1)S(1)} %get-tuple-element.90), channel_id=1, source_target_pairs={{0,24},{4,28},{8,16},{12,20},{16,8},{20,12},{24,0},{28,4},{1,25},{... | collective-permute-start | bytes 344072 | tf_op jit(solution)/shard_map/ppermute | solution.py:287
  6.9 1.9 collective-permute-start.12
  9.9 1.5 collective-permute-start.10
  12.0 1.3 gather_fusion
  14.0 2.0 collective-permute-done.12
  15.9 3.8 %collective-permute-start.16 = (bf16[32,1792]{1,0:T(8,128)(2,1)S(1)}, bf16[32,1792]{1,0:T(8,128)(2,1)S(1)}, u32[]{:S(2)}, u32[]{:S(2)}) collective-permute-start(bf16[32,1792]{1,0:T(8,128)(2,1)S(1)} %get-tuple-element.140), channel_id=1, source_target_pairs={{0,24},{4,28},{8,16},{12,20},{16,8},{20,12},{24,0},{28,4},{1,25},{... | collective-permute-start | bytes 344072 | tf_op jit(solution)/shard_map/ppermute | solution.py:287
  19.7 9.8 %collective-permute-done.11 = bf16[32,1792]{1,0:T(8,128)(2,1)S(1)} collective-permute-done((bf16[32,1792]{1,0:T(8,128)(2,1)S(1)}, bf16[32,1792]{1,0:T(8,128)(2,1)S(1)}, u32[]{:S(2)}, u32[]{:S(2)}) %collective-permute-start.11) | collective-permute-done | bytes 114720 | tf_op jit(solution)/shard_map/ppermute | solution.py:287
  29.5 3.2 %collective-permute-start.14 = (bf16[32,1792]{1,0:T(8,128)(2,1)S(1)}, bf16[32,1792]{1,0:T(8,128)(2,1)S(1)}, u32[]{:S(2)}, u32[]{:S(2)}) collective-permute-start(bf16[32,1792]{1,0:T(8,128)(2,1)S(1)} %get-tuple-element.140), channel_id=1, source_target_pairs={{0,8},{4,12},{8,0},{12,4},{16,24},{20,28},{24,16},{28,20},{1,9},{5... | collective-permute-start | bytes 344072 | tf_op jit(solution)/shard_map/ppermute | solution.py:287
  32.8 1.6 collective-permute-start.8
  34.4 2.8 %collective-permute-done.15 = bf16[32,1792]{1,0:T(8,128)(2,1)S(1)} collective-permute-done((bf16[32,1792]{1,0:T(8,128)(2,1)S(1)}, bf16[32,1792]{1,0:T(8,128)(2,1)S(1)}, u32[]{:S(2)}, u32[]{:S(2)}) %collective-permute-start.15) | collective-permute-done | bytes 114720 | tf_op jit(solution)/shard_map/ppermute | solution.py:287
  37.2 1.5 collective-permute-start.13
  39.4 3.5 %collective-permute-done.8 = bf16[64,3584]{1,0:T(8,128)(2,1)S(1)} collective-permute-done((bf16[64,3584]{1,0:T(8,128)(2,1)S(1)}, bf16[64,3584]{1,0:T(8,128)(2,1)S(1)}, u32[]{:S(2)}, u32[]{:S(2)}) %collective-permute-start.8) | collective-permute-done | bytes 458784 | tf_op jit(solution)/shard_map/ppermute | solution.py:287
  43.1 7.6 %collective-permute-done.13 = bf16[128,1792]{1,0:T(8,128)(2,1)S(1)} collective-permute-done((bf16[128,1792]{1,0:T(8,128)(2,1)S(1)}, bf16[128,1792]{1,0:T(8,128)(2,1)S(1)}, u32[]{:S(2)}, u32[]{:S(2)}) %collective-permute-start.13) | collective-permute-done | bytes 458784 | tf_op jit(solution)/shard_map/ppermute | solution.py:287
  51.1 7.4 %collective-permute-done.17 = bf16[128,1792]{1,0:T(8,128)(2,1)S(1)} collective-permute-done((bf16[128,1792]{1,0:T(8,128)(2,1)S(1)}, bf16[128,1792]{1,0:T(8,128)(2,1)S(1)}, u32[]{:S(2)}, u32[]{:S(2)}) %collective-permute-start.17) | collective-permute-done | bytes 458784 | tf_op jit(solution)/shard_map/ppermute | solution.py:287
  58.6 1.5 collective-permute-start.20
  60.3 1.8 shard_map.63
  62.1 10.4 %shard_map.64 = (f32[2,3584]{1,0:T(2,128)S(1)}, f32[1,1792]{1,0:T(1,128)S(1)}) custom-call(bf16[256,1792]{1,0:T(8,128)(2,1)S(1)} %constant_dynamic-update-slice_fusion.lhs_ref, bf16[256,3584]{1,0:T(8,128)(2,1)S(1)} %get-tuple-element.83.rhs_ref.lhs_ref), custom_call_target="tpu_custom_call" | custom-call | flops 3288334336 | bytes 2752512 | tf_op jit(solution)/shard_map/pallas_call | solution.py:126
  72.5 3.0 %collective-permute-start.18 = (bf16[32,1792]{1,0:T(8,128)(2,1)S(1)}, bf16[32,1792]{1,0:T(8,128)(2,1)S(1)}, u32[]{:S(2)}, u32[]{:S(2)}) collective-permute-start(bf16[32,1792]{1,0:T(8,128)(2,1)S(1)} %get-tuple-element.86), channel_id=1, source_target_pairs={{0,8},{4,12},{8,0},{12,4},{16,24},{20,28},{24,16},{28,20},{1,9},{5... | collective-permute-start | bytes 344072 | tf_op jit(solution)/shard_map/ppermute | solution.py:287
  75.5 1.6 collective-permute-start.25
  77.1 10.4 %shard_map.65 = (f32[2,3584]{1,0:T(2,128)S(1)}, f32[1,1792]{1,0:T(1,128)S(1)}) custom-call(bf16[256,1792]{1,0:T(8,128)(2,1)S(1)} %constant_dynamic-update-slice_fusion.5.lhs_ref, bf16[256,3584]{1,0:T(8,128)(2,1)S(1)} %get-tuple-element.83.rhs_ref.lhs_ref, f32[2,3584]{1,0:T(2,128)S(1)} %get-tuple-element.84.rest_0_), custom_call_target="tpu_custom_call" | custom-call | flops 3288334336 | bytes 2752512 | tf_op jit(solution)/shard_map/pallas_call | solution.py:126
  88.4 10.4 %shard_map.66 = (f32[2,3584]{1,0:T(2,128)S(1)}, f32[1,1792]{1,0:T(1,128)S(1)}) custom-call(bf16[256,1792]{1,0:T(8,128)(2,1)S(1)} %constant_dynamic-update-slice_fusion.15.lhs_ref, bf16[256,3584]{1,0:T(8,128)(2,1)S(1)} %get-tuple-element.83.rhs_ref.lhs_ref, f32[2,3584]{1,0:T(2,128)S(1)} %get-tuple-element.85.rest_0_), custom_call_target="tpu_custom_call" | custom-call | flops 3288334336 | bytes 2752512 | tf_op jit(solution)/shard_map/pallas_call | solution.py:126
  98.9 10.4 %shard_map.67 = (f32[2,3584]{1,0:T(2,128)S(1)}, f32[1,1792]{1,0:T(1,128)S(1)}) custom-call(bf16[256,1792]{1,0:T(8,128)(2,1)S(1)} %constant_dynamic-update-slice_fusion.10.lhs_ref, bf16[256,3584]{1,0:T(8,128)(2,1)S(1)} %get-tuple-element.83.rhs_ref.lhs_ref, f32[2,3584]{1,0:T(2,128)S(1)} %get-tuple-element.94.rest_0_), custom_call_target="tpu_custom_call" | custom-call | flops 3288334336 | bytes 2752512 | tf_op jit(solution)/shard_map/pallas_call | solution.py:126
  110.7 1.6 collective-permute-start.27
  112.3 1.4 pad_maximum_fusion.9.rhs_ref
  114.7 20.4 %shard_map.68 = (f32[2,3584]{1,0:T(2,128)S(1)}, f32[4,3584]{1,0:T(4,128)S(1)}, bf16[3584,3584]{1,0:T(8,128)(2,1)S(1)}) custom-call(bf16[256,3584]{1,0:T(8,128)(2,1)S(1)} %get-tuple-element.83.rhs_ref.lhs_ref, bf16[256,3584]{1,0:T(8,128)(2,1)S(1)} %pad_maximum_fusion.8.rhs_ref, f32[1,3584]{1,0:T(1,128)S(1)} %get-tuple-element.129.rest_0_), custom_call_target="tpu_custom_call" | custom-call | flops 6576668672 | bytes 3670016 | tf_op jit(solution)/shard_map/pallas_call | solution.py:126
  135.1 1.5 collective-permute-start.28
  136.7 22.4 %shard_map.69 = (f32[2,3584]{1,0:T(2,128)S(1)}, f32[4,3584]{1,0:T(4,128)S(1)}, bf16[3584,3584]{1,0:T(8,128)(2,1)S(1)}) custom-call(bf16[256,3584]{1,0:T(8,128)(2,1)} %copy-done.7, bf16[256,3584]{1,0:T(8,128)(2,1)} %pad_maximum_fusion.9.rhs_ref, f32[1,3584]{1,0:T(1,128)S(1)} %get-tuple-element.129.rest_0_), custom_call_target="tpu_custom_call" | custom-call | flops 6576668672 | bytes 3670016 | tf_op jit(solution)/shard_map/pallas_call | solution.py:126
  159.1 8.5 %copy-done = bf16[3584,3584]{1,0:T(8,128)(2,1)} copy-done((bf16[3584,3584]{1,0:T(8,128)(2,1)}, bf16[3584,3584]{1,0:T(8,128)(2,1)S(1)}, u32[]{:S(2)}) %copy-start) | copy-done | bytes 25690136
  168.4 3.1 %collective-permute-done.31 = f32[2,3584]{1,0:T(2,128)S(1)} collective-permute-done((f32[2,3584]{1,0:T(2,128)S(1)}, f32[2,3584]{1,0:T(2,128)S(1)}, u32[]{:S(2)}, u32[]{:S(2)}) %collective-permute-start.31) | collective-permute-done | bytes 28704 | tf_op jit(solution)/shard_map/ppermute | solution.py:267
  172.5 1.3 collective-permute-start.30
  173.8 1.7 collective-permute-done.32
  175.7 1.7 collective-permute-done.30
  177.5 6.2 %shard_map.70.rest_0_ = f32[1,3584]{1,0:T(1,128)S(1)} custom-call(bf16[3584,3584]{1,0:T(8,128)(2,1)S(1)} %get-tuple-element.96.kept_ref, f32[4,3584]{1,0:T(4,128)S(1)} %get-tuple-element.97.tile_max_ref, f32[1,3584]{1,0:T(1,128)S(1)} %multiply_add_fusion.2.lse_ref), custom_call_target="tpu_custom_call" | custom-call | flops 25690112 | bytes 25690112 | tf_op jit(solution)/shard_map/pallas_call | solution.py:204
  183.8 8.3 %copy-done.1 = bf16[3584,3584]{1,0:T(8,128)(2,1)S(1)} copy-done((bf16[3584,3584]{1,0:T(8,128)(2,1)S(1)}, bf16[3584,3584]{1,0:T(8,128)(2,1)}, u32[]{:S(2)}) %copy-start.1) | copy-done | bytes 25690136
  192.1 6.2 %shard_map.71 = f32[1,3584]{1,0:T(1,128)S(1)} custom-call(bf16[3584,3584]{1,0:T(8,128)(2,1)S(1)} %copy-done.1, f32[4,3584]{1,0:T(4,128)S(1)} %get-tuple-element.100.tile_max_ref, f32[1,3584]{1,0:T(1,128)S(1)} %multiply_add_fusion.1.lse_ref, f32[1,3584]{1,0:T(1,128)S(1)} %shard_map.70.rest_0_), custom_call_target="tpu_custom_call" | custom-call | flops 25690112 | bytes 25690112 | tf_op jit(solution)/shard_map/pallas_call | solution.py:204
  199.5 1.6 collective-permute-start.35
  201.1 2.2 collective-permute-done.35
  203.3 8.3 %copy-done.2 = bf16[3584,3584]{1,0:T(8,128)(2,1)S(1)} copy-done((bf16[3584,3584]{1,0:T(8,128)(2,1)S(1)}, bf16[3584,3584]{1,0:T(8,128)(2,1)}, u32[]{:S(2)}) %copy-start.2) | copy-done | bytes 25690136
  211.6 6.2 %shard_map.73 = f32[1,3712]{1,0:T(1,128)S(1)} custom-call(bf16[3584,3584]{1,0:T(8,128)(2,1)S(1)} %copy-done.2, f32[4,3584]{1,0:T(4,128)S(1)} %get-tuple-element.100.tile_max_ref, f32[1,3584]{1,0:T(1,128)S(1)} %multiply_add_fusion.1.lse_ref, f32[1,3584]{1,0:T(1,128)S(1)} %add.125.row_sum_ref), custom_call_target="tpu_custom_call" | custom-call | flops 25690112 | bytes 25690112 | tf_op jit(solution)/shard_map/pallas_call | solution.py:253
  217.8 6.0 %shard_map.72 = f32[1,3712]{1,0:T(1,128)S(1)} custom-call(bf16[3584,3584]{1,0:T(8,128)(2,1)S(1)} %get-tuple-element.96.kept_ref, f32[4,3584]{1,0:T(4,128)S(1)} %get-tuple-element.97.tile_max_ref, f32[1,3584]{1,0:T(1,128)S(1)} %multiply_add_fusion.2.lse_ref, f32[1,3584]{1,0:T(1,128)S(1)} %add.125.row_sum_ref), custom_call_target="tpu_custom_call" | custom-call | flops 25690112 | bytes 25690112 | tf_op jit(solution)/shard_map/pallas_call | solution.py:253
  223.9 1.6 collective-permute-start.36
  226.0 1.7 collective-permute-done.36
  227.7 1.3 collective-permute-start.37
  229.8 1.6 collective-permute-done.37
  231.5 1.3 collective-permute-start.38
  233.0 1.6 collective-permute-start.41
  234.6 1.6 collective-permute-done.38
  237.9 1.4 conditional.1
  (109 shorter events, 15.8 us)
Async XLA Ops:
  0.6 32.2 %copy-start.3 = (bf16[64,3584]{1,0:T(8,128)(2,1)S(1)}, bf16[64,3584]{1,0:T(8,128)(2,1)}, u32[]{:S(2)}) copy-start(bf16[64,3584]{1,0:T(8,128)(2,1)} %param.6) | copy-start | bytes 1376260
  1.8 70.7 %collective-permute-start.24 = (bf16[32,1792]{1,0:T(8,128)(2,1)S(1)}, bf16[32,1792]{1,0:T(8,128)(2,1)S(1)}, u32[]{:S(2)}, u32[]{:S(2)}) collective-permute-start(bf16[32,1792]{1,0:T(8,128)(2,1)S(1)} %get-tuple-element.90), channel_id=1, source_target_pairs={{0,24},{4,28},{8,16},{12,20},{16,8},{20,12},{24,0},{28,4},{1,25},{... | collective-permute-start | bytes 344072 | tf_op jit(solution)/shard_map/ppermute | solution.py:287
  6.9 68.6 %collective-permute-start.23 = (bf16[32,1792]{1,0:T(8,128)(2,1)S(1)}, bf16[32,1792]{1,0:T(8,128)(2,1)S(1)}, u32[]{:S(2)}, u32[]{:S(2)}) collective-permute-start(bf16[32,1792]{1,0:T(8,128)(2,1)S(1)} %get-tuple-element.90), channel_id=1, source_target_pairs={{0,16},{4,20},{8,24},{12,28},{16,0},{20,4},{24,8},{28,12},{1,17},{... | collective-permute-start | bytes 344072 | tf_op jit(solution)/shard_map/ppermute | solution.py:287
  6.9 9.0 %collective-permute-start.12 = (bf16[32,1792]{1,0:T(8,128)(2,1)S(1)}, bf16[32,1792]{1,0:T(8,128)(2,1)S(1)}, u32[]{:S(2)}, u32[]{:S(2)}) collective-permute-start(bf16[32,1792]{1,0:T(8,128)(2,1)S(1)} %get-tuple-element.141), channel_id=1, source_target_pairs={{0,24},{4,28},{8,16},{12,20},{16,8},{20,12},{24,0},{28,4},{1,25},{... | collective-permute-start | bytes 344072 | tf_op jit(solution)/shard_map/ppermute | solution.py:287
  8.8 20.7 %collective-permute-start.11 = (bf16[32,1792]{1,0:T(8,128)(2,1)S(1)}, bf16[32,1792]{1,0:T(8,128)(2,1)S(1)}, u32[]{:S(2)}, u32[]{:S(2)}) collective-permute-start(bf16[32,1792]{1,0:T(8,128)(2,1)S(1)} %get-tuple-element.141), channel_id=1, source_target_pairs={{0,16},{4,20},{8,24},{12,28},{16,0},{20,4},{24,8},{28,12},{1,17},{... | collective-permute-start | bytes 344072 | tf_op jit(solution)/shard_map/ppermute | solution.py:287
  9.9 19.7 %collective-permute-start.10 = (bf16[32,1792]{1,0:T(8,128)(2,1)S(1)}, bf16[32,1792]{1,0:T(8,128)(2,1)S(1)}, u32[]{:S(2)}, u32[]{:S(2)}) collective-permute-start(bf16[32,1792]{1,0:T(8,128)(2,1)S(1)} %get-tuple-element.141), channel_id=1, source_target_pairs={{0,8},{4,12},{8,0},{12,4},{16,24},{20,28},{24,16},{28,20},{1,9},{5... | collective-permute-start | bytes 344072 | tf_op jit(solution)/shard_map/ppermute | solution.py:287
  15.9 16.9 %collective-permute-start.16 = (bf16[32,1792]{1,0:T(8,128)(2,1)S(1)}, bf16[32,1792]{1,0:T(8,128)(2,1)S(1)}, u32[]{:S(2)}, u32[]{:S(2)}) collective-permute-start(bf16[32,1792]{1,0:T(8,128)(2,1)S(1)} %get-tuple-element.140), channel_id=1, source_target_pairs={{0,24},{4,28},{8,16},{12,20},{16,8},{20,12},{24,0},{28,4},{1,25},{... | collective-permute-start | bytes 344072 | tf_op jit(solution)/shard_map/ppermute | solution.py:287
  29.5 7.7 %collective-permute-start.15 = (bf16[32,1792]{1,0:T(8,128)(2,1)S(1)}, bf16[32,1792]{1,0:T(8,128)(2,1)S(1)}, u32[]{:S(2)}, u32[]{:S(2)}) collective-permute-start(bf16[32,1792]{1,0:T(8,128)(2,1)S(1)} %get-tuple-element.140), channel_id=1, source_target_pairs={{0,16},{4,20},{8,24},{12,28},{16,0},{20,4},{24,8},{28,12},{1,17},{... | collective-permute-start | bytes 344072 | tf_op jit(solution)/shard_map/ppermute | solution.py:287
  29.5 9.2 %collective-permute-start.14 = (bf16[32,1792]{1,0:T(8,128)(2,1)S(1)}, bf16[32,1792]{1,0:T(8,128)(2,1)S(1)}, u32[]{:S(2)}, u32[]{:S(2)}) collective-permute-start(bf16[32,1792]{1,0:T(8,128)(2,1)S(1)} %get-tuple-element.140), channel_id=1, source_target_pairs={{0,8},{4,12},{8,0},{12,4},{16,24},{20,28},{24,16},{28,20},{1,9},{5... | collective-permute-start | bytes 344072 | tf_op jit(solution)/shard_map/ppermute | solution.py:287
  32.8 10.1 %collective-permute-start.8 = (bf16[64,3584]{1,0:T(8,128)(2,1)S(1)}, bf16[64,3584]{1,0:T(8,128)(2,1)S(1)}, u32[]{:S(2)}, u32[]{:S(2)}) collective-permute-start(bf16[64,3584]{1,0:T(8,128)(2,1)S(1)} %copy-done.3), channel_id=1, source_target_pairs={{0,2},{1,3},{2,0},{3,1},{4,6},{5,7},{6,4},{7,5},{8,10},{9,11},{10,... | collective-permute-start | bytes 1376264 | tf_op jit(solution)/shard_map/ppermute | solution.py:287
  37.2 13.5 %collective-permute-start.13 = (bf16[128,1792]{1,0:T(8,128)(2,1)S(1)}, bf16[128,1792]{1,0:T(8,128)(2,1)S(1)}, u32[]{:S(2)}, u32[]{:S(2)}) collective-permute-start(bf16[128,1792]{1,0:T(8,128)(2,1)S(1)} %pad_maximum_fusion.11), channel_id=1, source_target_pairs={{0,4},{4,0},{8,12},{12,8},{16,20},{20,16},{24,28},{28,24},{1,5},{5... | collective-permute-start | bytes 1376264 | tf_op jit(solution)/shard_map/ppermute | solution.py:287
  38.7 19.8 %collective-permute-start.17 = (bf16[128,1792]{1,0:T(8,128)(2,1)S(1)}, bf16[128,1792]{1,0:T(8,128)(2,1)S(1)}, u32[]{:S(2)}, u32[]{:S(2)}) collective-permute-start(bf16[128,1792]{1,0:T(8,128)(2,1)S(1)} %pad_maximum_fusion.12), channel_id=1, source_target_pairs={{0,4},{4,0},{8,12},{12,8},{16,20},{20,16},{24,28},{28,24},{1,5},{5... | collective-permute-start | bytes 1376264 | tf_op jit(solution)/shard_map/ppermute | solution.py:287
  42.9 17.1 %collective-permute-start.9 = (bf16[128,3584]{1,0:T(8,128)(2,1)S(1)}, bf16[128,3584]{1,0:T(8,128)(2,1)S(1)}, u32[]{:S(2)}, u32[]{:S(2)}) collective-permute-start(bf16[128,3584]{1,0:T(8,128)(2,1)S(1)} %pad_maximum_fusion.10), channel_id=1, source_target_pairs={{0,1},{1,0},{2,3},{3,2},{4,5},{5,4},{6,7},{7,6},{8,9},{9,8},{10,11... | collective-permute-start | bytes 2752520 | tf_op jit(solution)/shard_map/ppermute | solution.py:287
  50.7 24.8 %collective-permute-start.22 = (bf16[32,1792]{1,0:T(8,128)(2,1)S(1)}, bf16[32,1792]{1,0:T(8,128)(2,1)S(1)}, u32[]{:S(2)}, u32[]{:S(2)}) collective-permute-start(bf16[32,1792]{1,0:T(8,128)(2,1)S(1)} %get-tuple-element.90), channel_id=1, source_target_pairs={{0,8},{4,12},{8,0},{12,4},{16,24},{20,28},{24,16},{28,20},{1,9},{5... | collective-permute-start | bytes 344072 | tf_op jit(solution)/shard_map/ppermute | solution.py:287
  58.6 29.0 %collective-permute-start.20 = (bf16[32,1792]{1,0:T(8,128)(2,1)S(1)}, bf16[32,1792]{1,0:T(8,128)(2,1)S(1)}, u32[]{:S(2)}, u32[]{:S(2)}) collective-permute-start(bf16[32,1792]{1,0:T(8,128)(2,1)S(1)} %get-tuple-element.86), channel_id=1, source_target_pairs={{0,24},{4,28},{8,16},{12,20},{16,8},{20,12},{24,0},{28,4},{1,25},{... | collective-permute-start | bytes 344072 | tf_op jit(solution)/shard_map/ppermute | solution.py:287
  60.1 27.5 %collective-permute-start.19 = (bf16[32,1792]{1,0:T(8,128)(2,1)S(1)}, bf16[32,1792]{1,0:T(8,128)(2,1)S(1)}, u32[]{:S(2)}, u32[]{:S(2)}) collective-permute-start(bf16[32,1792]{1,0:T(8,128)(2,1)S(1)} %get-tuple-element.86), channel_id=1, source_target_pairs={{0,16},{4,20},{8,24},{12,28},{16,0},{20,4},{24,8},{28,12},{1,17},{... | collective-permute-start | bytes 344072 | tf_op jit(solution)/shard_map/ppermute | solution.py:287
  62.1 52.6 %copy-start.7 = (bf16[256,3584]{1,0:T(8,128)(2,1)}, bf16[256,3584]{1,0:T(8,128)(2,1)S(1)}, u32[]{:S(2)}) copy-start(bf16[256,3584]{1,0:T(8,128)(2,1)S(1)} %get-tuple-element.83.rhs_ref.lhs_ref) | copy-start | bytes 5505028
  72.5 15.1 %collective-permute-start.18 = (bf16[32,1792]{1,0:T(8,128)(2,1)S(1)}, bf16[32,1792]{1,0:T(8,128)(2,1)S(1)}, u32[]{:S(2)}, u32[]{:S(2)}) collective-permute-start(bf16[32,1792]{1,0:T(8,128)(2,1)S(1)} %get-tuple-element.86), channel_id=1, source_target_pairs={{0,8},{4,12},{8,0},{12,4},{16,24},{20,28},{24,16},{28,20},{1,9},{5... | collective-permute-start | bytes 344072 | tf_op jit(solution)/shard_map/ppermute | solution.py:287
  75.5 12.8 %collective-permute-start.25 = (bf16[128,1792]{1,0:T(8,128)(2,1)S(1)}, bf16[128,1792]{1,0:T(8,128)(2,1)S(1)}, u32[]{:S(2)}, u32[]{:S(2)}) collective-permute-start(bf16[128,1792]{1,0:T(8,128)(2,1)S(1)} %pad_maximum_fusion.14), channel_id=1, source_target_pairs={{0,4},{4,0},{8,12},{12,8},{16,20},{20,16},{24,28},{28,24},{1,5},{5... | collective-permute-start | bytes 1376264 | tf_op jit(solution)/shard_map/ppermute | solution.py:287
  87.6 11.2 %collective-permute-start.21 = (bf16[128,1792]{1,0:T(8,128)(2,1)S(1)}, bf16[128,1792]{1,0:T(8,128)(2,1)S(1)}, u32[]{:S(2)}, u32[]{:S(2)}) collective-permute-start(bf16[128,1792]{1,0:T(8,128)(2,1)S(1)} %pad_maximum_fusion.13), channel_id=1, source_target_pairs={{0,4},{4,0},{8,12},{12,8},{16,20},{20,16},{24,28},{28,24},{1,5},{5... | collective-permute-start | bytes 1376264 | tf_op jit(solution)/shard_map/ppermute | solution.py:287
  109.3 1.3 collective-permute-start.26
  109.5 5.2 %copy-start.4 = (bf16[256,3584]{1,0:T(8,128)(2,1)}, bf16[256,3584]{1,0:T(8,128)(2,1)S(1)}, u32[]{:S(2)}) copy-start(bf16[256,3584]{1,0:T(8,128)(2,1)S(1)} %pad_maximum_fusion.8.rhs_ref) | copy-start | bytes 5505028
  110.7 3.9 %collective-permute-start.27 = (f32[2,3584]{1,0:T(2,128)S(1)}, f32[2,3584]{1,0:T(2,128)S(1)}, u32[]{:S(2)}, u32[]{:S(2)}) collective-permute-start(f32[2,3584]{1,0:T(2,128)S(1)} %pad_maximum_fusion.15), channel_id=1, source_target_pairs={{0,2},{1,3},{2,0},{3,1},{4,6},{5,7},{6,4},{7,5},{8,10},{9,11},{10,... | collective-permute-start | bytes 86024 | tf_op jit(solution)/shard_map/ppermute | solution.py:267
  135.1 33.0 %collective-permute-start.28 = (f32[2,3584]{1,0:T(2,128)S(1)}, f32[2,3584]{1,0:T(2,128)S(1)}, u32[]{:S(2)}, u32[]{:S(2)}) collective-permute-start(f32[2,3584]{1,0:T(2,128)S(1)} %get-tuple-element.98), channel_id=1, source_target_pairs={{0,4},{4,0},{8,12},{12,8},{16,20},{20,16},{24,28},{28,24},{1,5},{5... | collective-permute-start | bytes 86024 | tf_op jit(solution)/shard_map/ppermute | solution.py:267
  159.1 8.5 %copy-start = (bf16[3584,3584]{1,0:T(8,128)(2,1)}, bf16[3584,3584]{1,0:T(8,128)(2,1)S(1)}, u32[]{:S(2)}) copy-start(bf16[3584,3584]{1,0:T(8,128)(2,1)S(1)} %get-tuple-element.99.kept_ref) | copy-start | bytes 77070336
  167.6 3.9 %collective-permute-start.31 = (f32[2,3584]{1,0:T(2,128)S(1)}, f32[2,3584]{1,0:T(2,128)S(1)}, u32[]{:S(2)}, u32[]{:S(2)}) collective-permute-start(f32[2,3584]{1,0:T(2,128)S(1)} %get-tuple-element.101), channel_id=1, source_target_pairs={{0,4},{4,0},{8,12},{12,8},{16,20},{20,16},{24,28},{28,24},{1,5},{5... | collective-permute-start | bytes 86024 | tf_op jit(solution)/shard_map/ppermute | solution.py:267
  168.3 4.2 %collective-permute-start.29 = (f32[2,3584]{1,0:T(2,128)S(1)}, f32[2,3584]{1,0:T(2,128)S(1)}, u32[]{:S(2)}, u32[]{:S(2)}) collective-permute-start(f32[2,3584]{1,0:T(2,128)S(1)} %pad_maximum_fusion.16), channel_id=1, source_target_pairs={{0,8},{4,12},{8,0},{12,4},{16,24},{20,28},{24,16},{28,20},{1,9},{5... | collective-permute-start | bytes 86024 | tf_op jit(solution)/shard_map/ppermute | solution.py:267
  171.6 3.9 %collective-permute-start.32 = (f32[2,3584]{1,0:T(2,128)S(1)}, f32[2,3584]{1,0:T(2,128)S(1)}, u32[]{:S(2)}, u32[]{:S(2)}) collective-permute-start(f32[2,3584]{1,0:T(2,128)S(1)} %pad_maximum_fusion.18), channel_id=1, source_target_pairs={{0,8},{4,12},{8,0},{12,4},{16,24},{20,28},{24,16},{28,20},{1,9},{5... | collective-permute-start | bytes 86024 | tf_op jit(solution)/shard_map/ppermute | solution.py:267
  172.5 4.8 %collective-permute-start.30 = (f32[2,3584]{1,0:T(2,128)S(1)}, f32[2,3584]{1,0:T(2,128)S(1)}, u32[]{:S(2)}, u32[]{:S(2)}) collective-permute-start(f32[2,3584]{1,0:T(2,128)S(1)} %pad_maximum_fusion.17), channel_id=1, source_target_pairs={{0,16},{4,20},{8,24},{12,28},{16,0},{20,4},{24,8},{28,12},{1,17},{... | collective-permute-start | bytes 86024 | tf_op jit(solution)/shard_map/ppermute | solution.py:267
  175.6 8.0 %collective-permute-start.33 = (f32[2,3584]{1,0:T(2,128)S(1)}, f32[2,3584]{1,0:T(2,128)S(1)}, u32[]{:S(2)}, u32[]{:S(2)}) collective-permute-start(f32[2,3584]{1,0:T(2,128)S(1)} %pad_maximum_fusion.19), channel_id=1, source_target_pairs={{0,16},{4,20},{8,24},{12,28},{16,0},{20,4},{24,8},{28,12},{1,17},{... | collective-permute-start | bytes 86024 | tf_op jit(solution)/shard_map/ppermute | solution.py:267
  183.8 8.3 %copy-start.1 = (bf16[3584,3584]{1,0:T(8,128)(2,1)S(1)}, bf16[3584,3584]{1,0:T(8,128)(2,1)}, u32[]{:S(2)}) copy-start(bf16[3584,3584]{1,0:T(8,128)(2,1)} %copy-done) | copy-start | bytes 77070336
  198.2 1.2 collective-permute-start.34
  199.5 3.8 %collective-permute-start.35 = (f32[1,3584]{1,0:T(1,128)S(1)}, f32[1,3584]{1,0:T(1,128)S(1)}, u32[]{:S(2)}, u32[]{:S(2)}) collective-permute-start(f32[1,3584]{1,0:T(1,128)S(1)} %add.124), channel_id=1, source_target_pairs={{0,2},{1,3},{2,0},{3,1},{4,6},{5,7},{6,4},{7,5},{8,10},{9,11},{10,... | collective-permute-start | bytes 43016 | tf_op jit(solution)/shard_map/ppermute | solution.py:267
  203.3 8.3 %copy-start.2 = (bf16[3584,3584]{1,0:T(8,128)(2,1)S(1)}, bf16[3584,3584]{1,0:T(8,128)(2,1)}, u32[]{:S(2)}) copy-start(bf16[3584,3584]{1,0:T(8,128)(2,1)} %copy-done) | copy-start | bytes 77070336
  217.8 20.1 %copy-start.5 = (bf16[256,3584]{1,0:T(8,128)(2,1)S(1)}, bf16[256,3584]{1,0:T(8,128)(2,1)}, u32[]{:S(2)}) copy-start(bf16[256,3584]{1,0:T(8,128)(2,1)} %copy-done.4) | copy-start | bytes 5505028
  217.8 20.0 %copy-start.6 = (bf16[256,3584]{1,0:T(8,128)(2,1)S(1)}, bf16[256,3584]{1,0:T(8,128)(2,1)}, u32[]{:S(2)}) copy-start(bf16[256,3584]{1,0:T(8,128)(2,1)} %pad_maximum_fusion.9.rhs_ref) | copy-start | bytes 5505028
  217.8 20.0 %copy-start.8 = (bf16[256,3584]{1,0:T(8,128)(2,1)S(1)}, bf16[256,3584]{1,0:T(8,128)(2,1)}, u32[]{:S(2)}) copy-start(bf16[256,3584]{1,0:T(8,128)(2,1)} %copy-done.7) | copy-start | bytes 5505028
  223.9 3.8 %collective-permute-start.36 = (f32[1,3712]{1,0:T(1,128)S(1)}, f32[1,3712]{1,0:T(1,128)S(1)}, u32[]{:S(2)}, u32[]{:S(2)}) collective-permute-start(f32[1,3712]{1,0:T(1,128)S(1)} %shard_map.72), channel_id=1, source_target_pairs={{0,4},{4,0},{8,12},{12,8},{16,20},{20,16},{24,28},{28,24},{1,5},{5... | collective-permute-start | bytes 44552 | tf_op jit(solution)/shard_map/ppermute | solution.py:267
  225.4 3.7 %collective-permute-start.39 = (f32[1,3712]{1,0:T(1,128)S(1)}, f32[1,3712]{1,0:T(1,128)S(1)}, u32[]{:S(2)}, u32[]{:S(2)}) collective-permute-start(f32[1,3712]{1,0:T(1,128)S(1)} %shard_map.73), channel_id=1, source_target_pairs={{0,4},{4,0},{8,12},{12,8},{16,20},{20,16},{24,28},{28,24},{1,5},{5... | collective-permute-start | bytes 44552 | tf_op jit(solution)/shard_map/ppermute | solution.py:267
  227.7 3.8 %collective-permute-start.37 = (f32[1,3712]{1,0:T(1,128)S(1)}, f32[1,3712]{1,0:T(1,128)S(1)}, u32[]{:S(2)}, u32[]{:S(2)}) collective-permute-start(f32[1,3712]{1,0:T(1,128)S(1)} %add.126), channel_id=1, source_target_pairs={{0,8},{4,12},{8,0},{12,4},{16,24},{20,28},{24,16},{28,20},{1,9},{5... | collective-permute-start | bytes 44552 | tf_op jit(solution)/shard_map/ppermute | solution.py:267
  229.2 3.8 %collective-permute-start.40 = (f32[1,3712]{1,0:T(1,128)S(1)}, f32[1,3712]{1,0:T(1,128)S(1)}, u32[]{:S(2)}, u32[]{:S(2)}) collective-permute-start(f32[1,3712]{1,0:T(1,128)S(1)} %add.129), channel_id=1, source_target_pairs={{0,8},{4,12},{8,0},{12,4},{16,24},{20,28},{24,16},{28,20},{1,9},{5... | collective-permute-start | bytes 44552 | tf_op jit(solution)/shard_map/ppermute | solution.py:267
  231.5 4.7 %collective-permute-start.38 = (f32[1,3712]{1,0:T(1,128)S(1)}, f32[1,3712]{1,0:T(1,128)S(1)}, u32[]{:S(2)}, u32[]{:S(2)}) collective-permute-start(f32[1,3712]{1,0:T(1,128)S(1)} %add.127), channel_id=1, source_target_pairs={{0,16},{4,20},{8,24},{12,28},{16,0},{20,4},{24,8},{28,12},{1,17},{... | collective-permute-start | bytes 44552 | tf_op jit(solution)/shard_map/ppermute | solution.py:267
  233.0 4.8 %collective-permute-start.41 = (f32[1,3712]{1,0:T(1,128)S(1)}, f32[1,3712]{1,0:T(1,128)S(1)}, u32[]{:S(2)}, u32[]{:S(2)}) collective-permute-start(f32[1,3712]{1,0:T(1,128)S(1)} %add.130), channel_id=1, source_target_pairs={{0,16},{4,20},{8,24},{12,28},{16,0},{20,4},{24,8},{28,12},{1,17},{... | collective-permute-start | bytes 44552 | tf_op jit(solution)/shard_map/ppermute | solution.py:267

commit v3 on v2

--- a/solution.py
+++ b/solution.py
@@ -130,7 +130,7 @@
         out_specs=[VMEM] * len(outs),
         scratch_shapes=[pltpu.VMEM((m, depth), bf16), pltpu.VMEM((m, 128), f32)]
         + [pltpu.VMEM((tm, tn), f32)] * 2,
-        compiler_params=params(12),
+        compiler_params=params(9 if keep else 12),
         cost_estimate=pl.CostEstimate(flops=512 * m * n, bytes_accessed=512 * (m + n), transcendentals=m * n),
     )(*operands)
 
@@ -207,7 +207,7 @@
         in_specs=[VMEM] * len(operands),
         out_specs=VMEM,
         scratch_shapes=[pltpu.VMEM((16, n), bf16), pltpu.VMEM((m, 128), f32)],
-        compiler_params=params(6),
+        compiler_params=params(3),
         cost_estimate=pl.CostEstimate(flops=2 * m * n, bytes_accessed=2 * m * n, transcendentals=0),
     )(*operands)
 
@@ -256,7 +256,7 @@
         in_specs=[VMEM] * 4,
         out_specs=VMEM,
         scratch_shapes=[pltpu.VMEM((m, 128), bf16)],
-        compiler_params=params(6),
+        compiler_params=params(3),
         cost_estimate=pl.CostEstimate(flops=2 * m * n, bytes_accessed=2 * m * n, transcendentals=0),
     )(kept, tile_max, lse, row_sums)
 
@@ -268,18 +268,43 @@
         step *= 2
 
 
+def merge_kernel(last, mine_ref, other_ref, out_ref):
+    mine, other = mine_ref[...], other_ref[...]
+    top = jnp.maximum(mine[:1], other[:1])
+    total = mine[1:] * jnp.exp2((mine[:1] - top) * KAPPA) + other[1:] * jnp.exp2((other[:1] - top) * KAPPA)
+    if last:
+        out_ref[...] = KAPPA * top + jnp.log2(total)
+    else:
+        out_ref[0:1, :] = top
+        out_ref[1:2, :] = total
+
+
+def add_kernel(mine_ref, other_ref, out_ref):
+    out_ref[...] = mine_ref[...] + other_ref[...]
+
+
+def small_call(kernel, shape, *operands):
+    return pl.pallas_call(
+        kernel,
+        out_shape=jax.ShapeDtypeStruct(shape, f32),
+        in_specs=[VMEM] * len(operands),
+        out_specs=VMEM,
+        compiler_params=params(1),
+    )(*operands)
+
+
 def group_lse(pair, exchange_steps):
-    for exchange in exchange_steps:
-        other = exchange(pair)
-        top = jnp.maximum(pair[:1], other[:1])
-        total = pair[1:] * jnp.exp2((pair[:1] - top) * KAPPA) + other[1:] * jnp.exp2((other[:1] - top) * KAPPA)
-        pair = jnp.concatenate([top, total], 0)
-    return KAPPA * pair[:1] + jnp.log2(pair[1:])
+    exchange_steps = list(exchange_steps)
+    for k, exchange in enumerate(exchange_steps):
+        last = k + 1 == len(exchange_steps)
+        shape = (1 if last else 2, pair.shape[1])
+        pair = small_call(functools.partial(merge_kernel, last), shape, pair, exchange(pair))
+    return pair
 
 
 def group_sum(x, exchange_steps):
     for exchange in exchange_steps:
-        x = x + exchange(x)
+        x = small_call(add_kernel, x.shape, x, exchange(x))
     return x
 
 
@@ -292,9 +317,8 @@
     return [f * near + k for k in range(near) for f in range(far)]
 
 
-def gather_near(x, axis, size, near):
-    mine = jnp.concatenate([x] + [swap(x, axis, size, f * near) for f in range(1, size // near)], 0)
-    return jnp.concatenate([mine] + [swap(mine, axis, size, k) for k in range(1, near)], 0)
+def after(x, other):
+    return lax.optimization_barrier((x, other))[0]
 
 
 CHUNKS = 4
@@ -320,25 +344,37 @@
     place = jnp.array([arrival.index(v) for v in range(ba_size)], jnp.int32)
     token_block = lax.axis_index("aa") ^ jnp.array(gather_order(aa_size, near), jnp.int32)
     table = place[(token_block // per_block) ^ lax.axis_index("ba")] * per_block + token_block % per_block
-    whole_a, norm_a = reorder_call(gather_near(acts_a, "ba", ba_size, 2), table, tokens)
-
-    chunks, norms_b = [], []
-    state = None
-    states = []
+    group = [acts_a] + [swap(acts_a, "ba", ba_size, mask) for mask in range(2, ba_size, 2)]
+    far_a = jnp.concatenate(group, 0)
+    arrived_a = jnp.concatenate([far_a, swap(far_a, "ba", ba_size, 1)], 0)
+    whole_a, norm_a = reorder_call(arrived_a, table, tokens)
+
+    chunks, norms_b, states, sides = [], [], [], []
+
+    def start_chunk(c):
+        own = acts_b[:, c * width : (c + 1) * width]
+        if c:
+            own = after(own, sides[c - 1] if c >= 2 else far_a)
+        group = [own] + [swap(own, "aa", aa_size, mask) for mask in far_masks]
+        group[-1] = after(group[-1], states[c - 2] if c >= 2 else far_a)
+        mine = jnp.concatenate(group, 0)
+        sides.append(mine)
+        return [mine] + [swap(mine, "aa", aa_size, k) for k in range(1, near)]
+
+    coming = start_chunk(0)
     for c in range(CHUNKS):
-        own = acts_b[:, c * width : (c + 1) * width]
-        group = [own] + [swap(own, "aa", aa_size, mask) for mask in far_masks]
-        if c >= 2:
-            group, states[c - 2] = lax.optimization_barrier((group, states[c - 2]))
-        mine = jnp.concatenate(group, 0)
-        chunk = jnp.concatenate([mine] + [swap(mine, "aa", aa_size, k) for k in range(1, near)], 0)
+        group = coming
+        group[-1] = after(group[-1], states[c - 1] if c else whole_a)
+        chunk = jnp.concatenate(group, 0)
+        chunks.append(chunk)
+        if c + 1 < CHUNKS:
+            coming = start_chunk(c + 1)
+            chunk = after(chunk, sides[c + 1])
         state, norm = lse_call(chunk, whole_a, None, states[c - 1] if c else None)
         states.append(state)
-        chunks.append(chunk)
         norms_b.append(norm)
     row_lse = group_lse(states[-1], over_b())
     per_half = CHUNKS // HALVES
-    norms_b = [jnp.concatenate(norms_b[h * per_half : (h + 1) * per_half], 1) for h in range(HALVES)]
     halves = [jnp.concatenate(chunks[h * per_half : (h + 1) * per_half], 1) for h in range(HALVES)]
     log_n = math.log(NA)
 
@@ -348,9 +384,10 @@
     def potential_b_of(col_lse, norm_b):
         return -epsilon * LN2 * (col_lse - (0.5 * KAPPA) * norm_b)
 
+    row_bias, halves = lax.optimization_barrier((row_lse * (-1.0 / KAPPA), halves))
     col_lse, tile_max, kept = [], [], []
     for part in halves:
-        state, top, p = lse_call(whole_a, part, row_lse * (-1.0 / KAPPA), keep=True)
+        state, top, p = lse_call(whole_a, part, row_bias, keep=True)
         col_lse.append(group_lse(state, over_a()))
         tile_max.append(top)
         kept.append(pltpu.with_memory_space_constraint(p, pltpu.VMEM))
@@ -363,10 +400,13 @@
         sums = col_sum_call(kept[h], tile_max[h], col_lse[h], row_sums)
         col_sums.append(group_sum(sums, over_a()))
 
+    def half_norms(h):
+        return jnp.concatenate(norms_b[h * per_half : (h + 1) * per_half], 1)
+
     def quick(_):
         second_a = potential_a_of(row_lse) - epsilon * jnp.log(row_sums)
         second_b = [
-            potential_b_of(col_lse[h], norms_b[h]) - epsilon * jnp.log(col_sums[h][:, :half])
+            potential_b_of(col_lse[h], half_norms(h)) - epsilon * jnp.log(col_sums[h][:, :half])
             for h in range(HALVES)
         ]
         return second_a, jnp.concatenate(second_b, 1)
@@ -377,12 +417,12 @@
             (state,) = lse_call(part, whole_a, lse * (-1.0 / KAPPA), state)
         again = group_lse(state, over_b())
         second_b = []
-        for part, norm_b in zip(halves, norms_b):
+        for h, part in enumerate(halves):
             (state,) = lse_call(whole_a, part, again * (-1.0 / KAPPA))
-            second_b.append(potential_b_of(group_lse(state, over_a()), norm_b))
+            second_b.append(potential_b_of(group_lse(state, over_a()), half_norms(h)))
         return potential_a_of(again), jnp.concatenate(second_b, 1)
 
-    second_a, second_b = lax.cond(col_sums[0][0, half] > 0.0, exact, quick, 0)
+    second_a, second_b = lax.cond(col_sums[-1][0, half] > 0.0, exact, quick, 0)
     return second_a.reshape(-1), second_b.reshape(-1)
 
 

time: 240 us -> 211 us (0.88)
  local copies, waits for them, and re-layouts: 28.4 us -> 14.3 us
  waiting for transfers between devices: 51.4 us -> 40.5 us
  other arithmetic: 5.5 us -> 1.86 us
    unnamed x34 -> x29, local copies, waits for them, and re-layouts: 25.3 us -> 11.9 us
    ppermute x18, waiting for transfers between devices: 33.1 us -> 22.2 us  [swap(): return lax.ppermute(x, axis, [(i, i ^ mask) for i in range(size)])]
  transfers between devices with their start and end apart: 34 -> 34, of which waited for: 20 -> 21; matrix products, arithmetic and copies ran while one was open for 2% -> 1% of each run, Pallas kernels for 26% -> 32%
where the time goes in v3:
time: 211 us; the launch traced here: 210 us
  Pallas kernels  111 us (53%)
  starting transfers between devices  41.1 us (19%)
  waiting for transfers between devices  40.5 us (19%)
  local copies, waits for them, and re-layouts  14.3 us (7%)
    pallas_call x6, Pallas kernels, lse_call(): pl.pallas_call(functools.partial(lse_kernel, tm, tn, bias is not None, st...  84 us
    ppermute x18, starting transfers between devices, swap(): return lax.ppermute(x, axis, [(i, i ^ mask) for i in range(size)])  26 us
    ppermute x18, waiting for transfers between devices, swap(): return lax.ppermute(x, axis, [(i, i ^ mask) for i in range(size)])  22.2 us
    ppermute x16, waiting for transfers between devices, group_steps(): lax.ppermute(x, axis, [(i, i ^ s) for i in range(size)])  18.4 us
    ppermute x16, starting transfers between devices, group_steps(): lax.ppermute(x, axis, [(i, i ^ s) for i in range(size)])  15.1 us
    pallas_call x2, Pallas kernels, row_sum_call(): pl.pallas_call(functools.partial(row_sum_kernel, first is not None), out_...  12.3 us
    pallas_call x2, Pallas kernels, col_sum_call(): pl.pallas_call(col_sum_kernel, out_shape=jax.ShapeDtypeStruct((1, n + 128...  12.3 us
    unnamed x29, local copies, waits for them, and re-layouts  11.9 us
  transfers between devices with their start and end apart: 34, of which 21 were waited for; matrix products, arithmetic and copies ran while one was open for 1% of the time, Pallas kernels for 32%

profile of v3, /device:TPU:0, one launch (start us, length us, event | category | flops | bytes accessed | tf_op | source)
XLA Modules:
  0.0 210.3 jit_solution(9934695368825655784)
XLA Ops:
  0.7 1.1 fusion.7
  1.8 5.1 %collective-permute-start.18 = (bf16[32,1792]{1,0:T(8,128)(2,1)S(1)}, bf16[32,1792]{1,0:T(8,128)(2,1)S(1)}, u32[]{:S(2)}, u32[]{:S(2)}) collective-permute-start(bf16[32,1792]{1,0:T(8,128)(2,1)S(1)} %get-tuple-element.141), channel_id=1, source_target_pairs={{0,24},{4,28},{8,16},{12,20},{16,8},{20,12},{24,0},{28,4},{1,25},{... | collective-permute-start | bytes 344072 | tf_op jit(solution)/shard_map/ppermute | solution.py:312
  7.5 1.7 collective-permute-start.8
  9.2 1.1 constant_dynamic-update-slice_fusion.1
  11.0 3.3 %collective-permute-done.16 = bf16[32,1792]{1,0:T(8,128)(2,1)S(1)} collective-permute-done((bf16[32,1792]{1,0:T(8,128)(2,1)S(1)}, bf16[32,1792]{1,0:T(8,128)(2,1)S(1)}, u32[]{:S(2)}, u32[]{:S(2)}) %collective-permute-start.16) | collective-permute-done | bytes 114720 | tf_op jit(solution)/shard_map/ppermute | solution.py:312
  14.3 2.3 %collective-permute-done.17 = bf16[32,1792]{1,0:T(8,128)(2,1)S(1)} collective-permute-done((bf16[32,1792]{1,0:T(8,128)(2,1)S(1)}, bf16[32,1792]{1,0:T(8,128)(2,1)S(1)}, u32[]{:S(2)}, u32[]{:S(2)}) %collective-permute-start.17) | collective-permute-done | bytes 114720 | tf_op jit(solution)/shard_map/ppermute | solution.py:312
  16.6 2.9 %collective-permute-done.8 = bf16[64,3584]{1,0:T(8,128)(2,1)S(1)} collective-permute-done((bf16[64,3584]{1,0:T(8,128)(2,1)}, bf16[64,3584]{1,0:T(8,128)(2,1)S(1)}, u32[]{:S(2)}, u32[]{:S(2)}) %collective-permute-start.8) | collective-permute-done | bytes 458784 | tf_op jit(solution)/shard_map/ppermute | solution.py:312
  19.6 3.5 %collective-permute-start.12 = (bf16[32,1792]{1,0:T(8,128)(2,1)S(1)}, bf16[32,1792]{1,0:T(8,128)(2,1)S(1)}, u32[]{:S(2)}, u32[]{:S(2)}) collective-permute-start(bf16[32,1792]{1,0:T(8,128)(2,1)S(1)} %get-tuple-element.101), channel_id=1, source_target_pairs={{0,24},{4,28},{8,16},{12,20},{16,8},{20,12},{24,0},{28,4},{1,25},{... | collective-permute-start | bytes 344072 | tf_op jit(solution)/shard_map/ppermute | solution.py:312
  24.1 1.6 collective-permute-start.19
  25.7 5.5 %collective-permute-done.10 = bf16[32,1792]{1,0:T(8,128)(2,1)S(1)} collective-permute-done((bf16[32,1792]{1,0:T(8,128)(2,1)S(1)}, bf16[32,1792]{1,0:T(8,128)(2,1)S(1)}, u32[]{:S(2)}, u32[]{:S(2)}) %collective-permute-start.10) | collective-permute-done | bytes 114720 | tf_op jit(solution)/shard_map/ppermute | solution.py:312
  31.1 2.2 %collective-permute-done.11 = bf16[32,1792]{1,0:T(8,128)(2,1)S(1)} collective-permute-done((bf16[32,1792]{1,0:T(8,128)(2,1)S(1)}, bf16[32,1792]{1,0:T(8,128)(2,1)S(1)}, u32[]{:S(2)}, u32[]{:S(2)}) %collective-permute-start.11) | collective-permute-done | bytes 114720 | tf_op jit(solution)/shard_map/ppermute | solution.py:312
  33.4 2.5 %collective-permute-start.15 = (bf16[32,1792]{1,0:T(8,128)(2,1)S(1)}, bf16[32,1792]{1,0:T(8,128)(2,1)S(1)}, u32[]{:S(2)}, u32[]{:S(2)}) collective-permute-start(bf16[32,1792]{1,0:T(8,128)(2,1)S(1)} %get-tuple-element.103), channel_id=1, source_target_pairs={{0,24},{4,28},{8,16},{12,20},{16,8},{20,12},{24,0},{28,4},{1,25},{... | collective-permute-start | bytes 344072 | tf_op jit(solution)/shard_map/ppermute | solution.py:312
  35.8 2.0 collective-permute-start.13
  37.8 5.2 %collective-permute-done.13 = bf16[32,1792]{1,0:T(8,128)(2,1)S(1)} collective-permute-done((bf16[32,1792]{1,0:T(8,128)(2,1)S(1)}, bf16[32,1792]{1,0:T(8,128)(2,1)S(1)}, u32[]{:S(2)}, u32[]{:S(2)}) %collective-permute-start.13) | collective-permute-done | bytes 114720 | tf_op jit(solution)/shard_map/ppermute | solution.py:312
  43.0 1.5 collective-permute-start.23
  45.5 1.8 shard_map.63
  47.4 10.4 %shard_map.64 = (f32[2,3584]{1,0:T(2,128)S(1)}, f32[1,1792]{1,0:T(1,128)S(1)}) custom-call(bf16[256,1792]{1,0:T(8,128)(2,1)S(1)} %constant_dynamic-update-slice_fusion.6.lhs_ref, bf16[256,3584]{1,0:T(8,128)(2,1)S(1)} %get-tuple-element.100.rhs_ref.lhs_ref), custom_call_target="tpu_custom_call" | custom-call | flops 3288334336 | bytes 2752512 | tf_op jit(solution)/shard_map/pallas_call | solution.py:126
  57.8 2.3 %collective-permute-start.22 = (bf16[32,1792]{1,0:T(8,128)(2,1)S(1)}, bf16[32,1792]{1,0:T(8,128)(2,1)S(1)}, u32[]{:S(2)}, u32[]{:S(2)}) collective-permute-start(bf16[32,1792]{1,0:T(8,128)(2,1)S(1)} %get-tuple-element.109), channel_id=1, source_target_pairs={{0,24},{4,28},{8,16},{12,20},{16,8},{20,12},{24,0},{28,4},{1,25},{... | collective-permute-start | bytes 344072 | tf_op jit(solution)/shard_map/ppermute | solution.py:312
  61.0 1.2 collective-permute-start.20
  62.3 1.5 collective-permute-start.25
  63.8 10.4 %shard_map.65 = (f32[2,3584]{1,0:T(2,128)S(1)}, f32[1,1792]{1,0:T(1,128)S(1)}) custom-call(bf16[256,1792]{1,0:T(8,128)(2,1)S(1)} %constant_dynamic-update-slice_fusion.15.lhs_ref, bf16[256,3584]{1,0:T(8,128)(2,1)S(1)} %get-tuple-element.100.rhs_ref.lhs_ref, f32[2,3584]{1,0:T(2,128)S(1)} %get-tuple-element.107.rest_0_), custom_call_target="tpu_custom_call" | custom-call | flops 3288334336 | bytes 2752512 | tf_op jit(solution)/shard_map/pallas_call | solution.py:126
  75.0 10.4 %shard_map.66 = (f32[2,3584]{1,0:T(2,128)S(1)}, f32[1,1792]{1,0:T(1,128)S(1)}) custom-call(bf16[256,1792]{1,0:T(8,128)(2,1)S(1)} %constant_dynamic-update-slice_fusion.24.lhs_ref, bf16[256,3584]{1,0:T(8,128)(2,1)S(1)} %get-tuple-element.100.rhs_ref.lhs_ref, f32[2,3584]{1,0:T(2,128)S(1)} %get-tuple-element.112.rest_0_), custom_call_target="tpu_custom_call" | custom-call | flops 3288334336 | bytes 2752512 | tf_op jit(solution)/shard_map/pallas_call | solution.py:126
  85.6 10.4 %shard_map.67 = (f32[2,3584]{1,0:T(2,128)S(1)}, f32[1,1792]{1,0:T(1,128)S(1)}) custom-call(bf16[256,1792]{1,0:T(8,128)(2,1)S(1)} %constant_dynamic-update-slice_fusion.29.lhs_ref, bf16[256,3584]{1,0:T(8,128)(2,1)S(1)} %get-tuple-element.100.rhs_ref.lhs_ref, f32[2,3584]{1,0:T(2,128)S(1)} %get-tuple-element.116.rest_0_), custom_call_target="tpu_custom_call" | custom-call | flops 3288334336 | bytes 2752512 | tf_op jit(solution)/shard_map/pallas_call | solution.py:126
  97.3 1.6 collective-permute-start.27
  99.0 2.2 %collective-permute-done.27.other_ref = f32[2,3584]{1,0:T(2,128)S(1)} collective-permute-done((f32[2,3584]{1,0:T(2,128)S(1)}, f32[2,3584]{1,0:T(2,128)S(1)}, u32[]{:S(2)}, u32[]{:S(2)}) %collective-permute-start.27) | collective-permute-done | bytes 28704 | tf_op jit(solution)/shard_map/ppermute | solution.py:267
  101.3 20.4 %shard_map.74 = (f32[2,3584]{1,0:T(2,128)S(1)}, f32[4,3584]{1,0:T(4,128)S(1)}, bf16[3584,3584]{1,0:T(8,128)(2,1)S(1)}) custom-call(bf16[256,3584]{1,0:T(8,128)(2,1)S(1)} %get-tuple-element.100.rhs_ref.lhs_ref, bf16[256,3584]{1,0:T(8,128)(2,1)S(1)} %pad_maximum_fusion.3.rhs_ref, f32[1,3584]{1,0:T(1,128)S(1)} %broadcast_multiply_fusion.3.rest_0_), custom_call_target="tpu_custom_call" | custom-call | flops 6576668672 | bytes 3670016 | tf_op jit(solution)/shard_map/pallas_call | solution.py:126
  121.7 1.5 collective-permute-start.31
  123.2 22.0 %shard_map.70 = (f32[2,3584]{1,0:T(2,128)S(1)}, f32[4,3584]{1,0:T(4,128)S(1)}, bf16[3584,3584]{1,0:T(8,128)(2,1)S(1)}) custom-call(bf16[256,3584]{1,0:T(8,128)(2,1)} %copy-done.5, bf16[256,3584]{1,0:T(8,128)(2,1)S(1)} %pad_maximum_fusion.4.rhs_ref, f32[1,3584]{1,0:T(1,128)S(1)} %broadcast_multiply_fusion.3.rest_0_), custom_call_target="tpu_custom_call" | custom-call | flops 6576668672 | bytes 3670016 | tf_op jit(solution)/shard_map/pallas_call | solution.py:126
  145.2 8.5 %copy-done = bf16[3584,3584]{1,0:T(8,128)(2,1)} copy-done((bf16[3584,3584]{1,0:T(8,128)(2,1)}, bf16[3584,3584]{1,0:T(8,128)(2,1)S(1)}, u32[]{:S(2)}) %copy-start) | copy-done | bytes 25690136
  155.1 2.5 %collective-permute-done.28.other_ref = f32[2,3584]{1,0:T(2,128)S(1)} collective-permute-done((f32[2,3584]{1,0:T(2,128)S(1)}, f32[2,3584]{1,0:T(2,128)S(1)}, u32[]{:S(2)}, u32[]{:S(2)}) %collective-permute-start.28) | collective-permute-done | bytes 28704 | tf_op jit(solution)/shard_map/ppermute | solution.py:267
  158.4 1.7 collective-permute-start.33
  160.2 1.3 collective-permute-done.29.other_ref
  162.2 1.1 collective-permute-done.33.other_ref
  163.3 6.2 %shard_map.78.rest_0_ = f32[1,3584]{1,0:T(1,128)S(1)} custom-call(bf16[3584,3584]{1,0:T(8,128)(2,1)S(1)} %get-tuple-element.125.kept_ref, f32[4,3584]{1,0:T(4,128)S(1)} %get-tuple-element.126.tile_max_ref, f32[1,3584]{1,0:T(1,128)S(1)} %shard_map.77.lse_ref), custom_call_target="tpu_custom_call" | custom-call | flops 25690112 | bytes 25690112 | tf_op jit(solution)/shard_map/pallas_call | solution.py:204
  169.6 2.1 copy-done.1
  171.6 6.2 %shard_map.79.mine_ref = f32[1,3584]{1,0:T(1,128)S(1)} custom-call(bf16[3584,3584]{1,0:T(8,128)(2,1)S(1)} %copy-done.1, f32[4,3584]{1,0:T(4,128)S(1)} %get-tuple-element.122.tile_max_ref, f32[1,3584]{1,0:T(1,128)S(1)} %shard_map.73.lse_ref, f32[1,3584]{1,0:T(1,128)S(1)} %shard_map.78.rest_0_), custom_call_target="tpu_custom_call" | custom-call | flops 25690112 | bytes 25690112 | tf_op jit(solution)/shard_map/pallas_call | solution.py:204
  177.9 1.2 collective-permute-done.34.other_ref
  179.1 1.5 collective-permute-start.35
  180.6 2.2 %collective-permute-done.35.other_ref = f32[1,3584]{1,0:T(1,128)S(1)} collective-permute-done((f32[1,3584]{1,0:T(1,128)S(1)}, f32[1,3584]{1,0:T(1,128)S(1)}, u32[]{:S(2)}, u32[]{:S(2)}) %collective-permute-start.35) | collective-permute-done | bytes 14368 | tf_op jit(solution)/shard_map/ppermute | solution.py:267
  182.8 6.1 %shard_map.82.mine_ref = f32[1,3712]{1,0:T(1,128)S(1)} custom-call(bf16[3584,3584]{1,0:T(8,128)(2,1)S(1)} %copy-done.1, f32[4,3584]{1,0:T(4,128)S(1)} %get-tuple-element.122.tile_max_ref, f32[1,3584]{1,0:T(1,128)S(1)} %shard_map.73.lse_ref, f32[1,3584]{1,0:T(1,128)S(1)} %shard_map.81.row_sum_ref), custom_call_target="tpu_custom_call" | custom-call | flops 25690112 | bytes 25690112 | tf_op jit(solution)/shard_map/pallas_call | solution.py:253
  188.9 1.6 collective-permute-start.36
  190.5 6.2 %shard_map.86.mine_ref = f32[1,3712]{1,0:T(1,128)S(1)} custom-call(bf16[3584,3584]{1,0:T(8,128)(2,1)S(1)} %get-tuple-element.125.kept_ref, f32[4,3584]{1,0:T(4,128)S(1)} %get-tuple-element.126.tile_max_ref, f32[1,3584]{1,0:T(1,128)S(1)} %shard_map.77.lse_ref, f32[1,3584]{1,0:T(1,128)S(1)} %shard_map.81.row_sum_ref), custom_call_target="tpu_custom_call" | custom-call | flops 25690112 | bytes 25690112 | tf_op jit(solution)/shard_map/pallas_call | solution.py:253
  197.2 1.3 collective-permute-start.37
  198.5 1.9 collective-permute-done.39.other_ref
  201.0 1.7 collective-permute-start.38
  202.7 1.5 collective-permute-done.40.other_ref
  206.8 2.0 collective-permute-done.41.other_ref
  208.8 1.4 conditional.1
  (97 shorter events, 14.4 us)
Async XLA Ops:
  0.6 9.7 %copy-start.4 = (s32[8]{0:T(128)S(1)}, s32[8]{0:T(128)}, u32[]{:S(2)}) copy-start(s32[8]{0:T(128)} %constant.73.clone) | copy-start | bytes 100
  0.6 9.7 %copy-start.2 = (s32[4]{0:T(128)S(1)}, s32[4]{0:T(128)}, u32[]{:S(2)}) copy-start(s32[4]{0:T(128)} %constant.72.clone) | copy-start | bytes 52
  1.8 22.3 %collective-permute-start.18 = (bf16[32,1792]{1,0:T(8,128)(2,1)S(1)}, bf16[32,1792]{1,0:T(8,128)(2,1)S(1)}, u32[]{:S(2)}, u32[]{:S(2)}) collective-permute-start(bf16[32,1792]{1,0:T(8,128)(2,1)S(1)} %get-tuple-element.141), channel_id=1, source_target_pairs={{0,24},{4,28},{8,16},{12,20},{16,8},{20,12},{24,0},{28,4},{1,25},{... | collective-permute-start | bytes 344072 | tf_op jit(solution)/shard_map/ppermute | solution.py:312
  6.9 9.7 %collective-permute-start.17 = (bf16[32,1792]{1,0:T(8,128)(2,1)S(1)}, bf16[32,1792]{1,0:T(8,128)(2,1)S(1)}, u32[]{:S(2)}, u32[]{:S(2)}) collective-permute-start(bf16[32,1792]{1,0:T(8,128)(2,1)S(1)} %get-tuple-element.141), channel_id=1, source_target_pairs={{0,16},{4,20},{8,24},{12,28},{16,0},{20,4},{24,8},{28,12},{1,17},{... | collective-permute-start | bytes 344072 | tf_op jit(solution)/shard_map/ppermute | solution.py:312
  6.9 7.4 %collective-permute-start.16 = (bf16[32,1792]{1,0:T(8,128)(2,1)S(1)}, bf16[32,1792]{1,0:T(8,128)(2,1)S(1)}, u32[]{:S(2)}, u32[]{:S(2)}) collective-permute-start(bf16[32,1792]{1,0:T(8,128)(2,1)S(1)} %get-tuple-element.141), channel_id=1, source_target_pairs={{0,8},{4,12},{8,0},{12,4},{16,24},{20,28},{24,16},{28,20},{1,9},{5... | collective-permute-start | bytes 344072 | tf_op jit(solution)/shard_map/ppermute | solution.py:312
  7.5 11.9 %collective-permute-start.8 = (bf16[64,3584]{1,0:T(8,128)(2,1)}, bf16[64,3584]{1,0:T(8,128)(2,1)S(1)}, u32[]{:S(2)}, u32[]{:S(2)}) collective-permute-start(bf16[64,3584]{1,0:T(8,128)(2,1)} %param.6), channel_id=1, source_target_pairs={{0,2},{1,3},{2,0},{3,1},{4,6},{5,7},{6,4},{7,5},{8,10},{9,11},{10,... | collective-permute-start | bytes 1376264 | tf_op jit(solution)/shard_map/ppermute | solution.py:312
  19.5 25.9 %copy-start.3 = (bf16[64,3584]{1,0:T(8,128)(2,1)S(1)}, bf16[64,3584]{1,0:T(8,128)(2,1)}, u32[]{:S(2)}) copy-start(bf16[64,3584]{1,0:T(8,128)(2,1)} %param.6) | copy-start | bytes 1376260
  19.5 25.9 %collective-permute-start.9 = (bf16[128,3584]{1,0:T(8,128)(2,1)S(1)}, bf16[128,3584]{1,0:T(8,128)(2,1)S(1)}, u32[]{:S(2)}, u32[]{:S(2)}) collective-permute-start(bf16[128,3584]{1,0:T(8,128)(2,1)S(1)} %constant_dynamic-update-slice_fusion), channel_id=1, source_target_pairs={{0,1},{1,0},{2,3},{3,2},{4,5},{5,4},{6,7},{7,6},{8,9},{9,8},{10,11... | collective-permute-start | bytes 2752520 | tf_op jit(solution)/shard_map/ppermute | solution.py:312
  19.6 11.6 %collective-permute-start.12 = (bf16[32,1792]{1,0:T(8,128)(2,1)S(1)}, bf16[32,1792]{1,0:T(8,128)(2,1)S(1)}, u32[]{:S(2)}, u32[]{:S(2)}) collective-permute-start(bf16[32,1792]{1,0:T(8,128)(2,1)S(1)} %get-tuple-element.101), channel_id=1, source_target_pairs={{0,24},{4,28},{8,16},{12,20},{16,8},{20,12},{24,0},{28,4},{1,25},{... | collective-permute-start | bytes 344072 | tf_op jit(solution)/shard_map/ppermute | solution.py:312
  23.1 10.2 %collective-permute-start.11 = (bf16[32,1792]{1,0:T(8,128)(2,1)S(1)}, bf16[32,1792]{1,0:T(8,128)(2,1)S(1)}, u32[]{:S(2)}, u32[]{:S(2)}) collective-permute-start(bf16[32,1792]{1,0:T(8,128)(2,1)S(1)} %get-tuple-element.101), channel_id=1, source_target_pairs={{0,16},{4,20},{8,24},{12,28},{16,0},{20,4},{24,8},{28,12},{1,17},{... | collective-permute-start | bytes 344072 | tf_op jit(solution)/shard_map/ppermute | solution.py:312
  23.1 8.0 %collective-permute-start.10 = (bf16[32,1792]{1,0:T(8,128)(2,1)S(1)}, bf16[32,1792]{1,0:T(8,128)(2,1)S(1)}, u32[]{:S(2)}, u32[]{:S(2)}) collective-permute-start(bf16[32,1792]{1,0:T(8,128)(2,1)S(1)} %get-tuple-element.101), channel_id=1, source_target_pairs={{0,8},{4,12},{8,0},{12,4},{16,24},{20,28},{24,16},{28,20},{1,9},{5... | collective-permute-start | bytes 344072 | tf_op jit(solution)/shard_map/ppermute | solution.py:312
  24.1 23.3 %collective-permute-start.19 = (bf16[128,1792]{1,0:T(8,128)(2,1)S(1)}, bf16[128,1792]{1,0:T(8,128)(2,1)S(1)}, u32[]{:S(2)}, u32[]{:S(2)}) collective-permute-start(bf16[128,1792]{1,0:T(8,128)(2,1)S(1)} %pad_maximum_fusion.5), channel_id=1, source_target_pairs={{0,4},{4,0},{8,12},{12,8},{16,20},{20,16},{24,28},{28,24},{1,5},{5... | collective-permute-start | bytes 1376264 | tf_op jit(solution)/shard_map/ppermute | solution.py:312
  33.4 24.4 %collective-permute-start.15 = (bf16[32,1792]{1,0:T(8,128)(2,1)S(1)}, bf16[32,1792]{1,0:T(8,128)(2,1)S(1)}, u32[]{:S(2)}, u32[]{:S(2)}) collective-permute-start(bf16[32,1792]{1,0:T(8,128)(2,1)S(1)} %get-tuple-element.103), channel_id=1, source_target_pairs={{0,24},{4,28},{8,16},{12,20},{16,8},{20,12},{24,0},{28,4},{1,25},{... | collective-permute-start | bytes 344072 | tf_op jit(solution)/shard_map/ppermute | solution.py:312
  35.8 9.5 %collective-permute-start.14 = (bf16[32,1792]{1,0:T(8,128)(2,1)S(1)}, bf16[32,1792]{1,0:T(8,128)(2,1)S(1)}, u32[]{:S(2)}, u32[]{:S(2)}) collective-permute-start(bf16[32,1792]{1,0:T(8,128)(2,1)S(1)} %get-tuple-element.103), channel_id=1, source_target_pairs={{0,16},{4,20},{8,24},{12,28},{16,0},{20,4},{24,8},{28,12},{1,17},{... | collective-permute-start | bytes 344072 | tf_op jit(solution)/shard_map/ppermute | solution.py:312
  35.8 7.2 %collective-permute-start.13 = (bf16[32,1792]{1,0:T(8,128)(2,1)S(1)}, bf16[32,1792]{1,0:T(8,128)(2,1)S(1)}, u32[]{:S(2)}, u32[]{:S(2)}) collective-permute-start(bf16[32,1792]{1,0:T(8,128)(2,1)S(1)} %get-tuple-element.103), channel_id=1, source_target_pairs={{0,8},{4,12},{8,0},{12,4},{16,24},{20,28},{24,16},{28,20},{1,9},{5... | collective-permute-start | bytes 344072 | tf_op jit(solution)/shard_map/ppermute | solution.py:312
  43.0 20.8 %collective-permute-start.23 = (bf16[128,1792]{1,0:T(8,128)(2,1)S(1)}, bf16[128,1792]{1,0:T(8,128)(2,1)S(1)}, u32[]{:S(2)}, u32[]{:S(2)}) collective-permute-start(bf16[128,1792]{1,0:T(8,128)(2,1)S(1)} %get-tuple-element.163), channel_id=1, source_target_pairs={{0,4},{4,0},{8,12},{12,8},{16,20},{20,16},{24,28},{28,24},{1,5},{5... | collective-permute-start | bytes 1376264 | tf_op jit(solution)/shard_map/ppermute | solution.py:312
  47.4 53.9 %copy-start.5 = (bf16[256,3584]{1,0:T(8,128)(2,1)}, bf16[256,3584]{1,0:T(8,128)(2,1)S(1)}, u32[]{:S(2)}) copy-start(bf16[256,3584]{1,0:T(8,128)(2,1)S(1)} %get-tuple-element.100.rhs_ref.lhs_ref) | copy-start | bytes 5505028
  57.8 16.5 %collective-permute-start.22 = (bf16[32,1792]{1,0:T(8,128)(2,1)S(1)}, bf16[32,1792]{1,0:T(8,128)(2,1)S(1)}, u32[]{:S(2)}, u32[]{:S(2)}) collective-permute-start(bf16[32,1792]{1,0:T(8,128)(2,1)S(1)} %get-tuple-element.109), channel_id=1, source_target_pairs={{0,24},{4,28},{8,16},{12,20},{16,8},{20,12},{24,0},{28,4},{1,25},{... | collective-permute-start | bytes 344072 | tf_op jit(solution)/shard_map/ppermute | solution.py:312
  60.2 14.2 %collective-permute-start.21 = (bf16[32,1792]{1,0:T(8,128)(2,1)S(1)}, bf16[32,1792]{1,0:T(8,128)(2,1)S(1)}, u32[]{:S(2)}, u32[]{:S(2)}) collective-permute-start(bf16[32,1792]{1,0:T(8,128)(2,1)S(1)} %get-tuple-element.109), channel_id=1, source_target_pairs={{0,16},{4,20},{8,24},{12,28},{16,0},{20,4},{24,8},{28,12},{1,17},{... | collective-permute-start | bytes 344072 | tf_op jit(solution)/shard_map/ppermute | solution.py:312
  61.0 13.2 %collective-permute-start.20 = (bf16[32,1792]{1,0:T(8,128)(2,1)S(1)}, bf16[32,1792]{1,0:T(8,128)(2,1)S(1)}, u32[]{:S(2)}, u32[]{:S(2)}) collective-permute-start(bf16[32,1792]{1,0:T(8,128)(2,1)S(1)} %get-tuple-element.109), channel_id=1, source_target_pairs={{0,8},{4,12},{8,0},{12,4},{16,24},{20,28},{24,16},{28,20},{1,9},{5... | collective-permute-start | bytes 344072 | tf_op jit(solution)/shard_map/ppermute | solution.py:312
  62.3 12.7 %collective-permute-start.25 = (bf16[128,1792]{1,0:T(8,128)(2,1)S(1)}, bf16[128,1792]{1,0:T(8,128)(2,1)S(1)}, u32[]{:S(2)}, u32[]{:S(2)}) collective-permute-start(bf16[128,1792]{1,0:T(8,128)(2,1)S(1)} %get-tuple-element.147), channel_id=1, source_target_pairs={{0,4},{4,0},{8,12},{12,8},{16,20},{20,16},{24,28},{28,24},{1,5},{5... | collective-permute-start | bytes 1376264 | tf_op jit(solution)/shard_map/ppermute | solution.py:312
  74.4 11.2 %collective-permute-start.24 = (bf16[128,1792]{1,0:T(8,128)(2,1)S(1)}, bf16[128,1792]{1,0:T(8,128)(2,1)S(1)}, u32[]{:S(2)}, u32[]{:S(2)}) collective-permute-start(bf16[128,1792]{1,0:T(8,128)(2,1)S(1)} %get-tuple-element.154), channel_id=1, source_target_pairs={{0,4},{4,0},{8,12},{12,8},{16,20},{20,16},{24,28},{28,24},{1,5},{5... | collective-permute-start | bytes 1376264 | tf_op jit(solution)/shard_map/ppermute | solution.py:312
  96.0 1.3 collective-permute-start.26
  97.3 3.9 %collective-permute-start.27 = (f32[2,3584]{1,0:T(2,128)S(1)}, f32[2,3584]{1,0:T(2,128)S(1)}, u32[]{:S(2)}, u32[]{:S(2)}) collective-permute-start(f32[2,3584]{1,0:T(2,128)S(1)} %shard_map.68.mine_ref), channel_id=1, source_target_pairs={{0,2},{1,3},{2,0},{3,1},{4,6},{5,7},{6,4},{7,5},{8,10},{9,11},{10,... | collective-permute-start | bytes 86024 | tf_op jit(solution)/shard_map/ppermute | solution.py:267
  121.7 32.6 %collective-permute-start.31 = (f32[2,3584]{1,0:T(2,128)S(1)}, f32[2,3584]{1,0:T(2,128)S(1)}, u32[]{:S(2)}, u32[]{:S(2)}) collective-permute-start(f32[2,3584]{1,0:T(2,128)S(1)} %get-tuple-element.127.mine_ref), channel_id=1, source_target_pairs={{0,4},{4,0},{8,12},{12,8},{16,20},{20,16},{24,28},{28,24},{1,5},{5... | collective-permute-start | bytes 86024 | tf_op jit(solution)/shard_map/ppermute | solution.py:267
  145.1 8.5 %copy-start = (bf16[3584,3584]{1,0:T(8,128)(2,1)}, bf16[3584,3584]{1,0:T(8,128)(2,1)S(1)}, u32[]{:S(2)}) copy-start(bf16[3584,3584]{1,0:T(8,128)(2,1)S(1)} %get-tuple-element.121.kept_ref) | copy-start | bytes 77070336
  153.6 3.9 %collective-permute-start.28 = (f32[2,3584]{1,0:T(2,128)S(1)}, f32[2,3584]{1,0:T(2,128)S(1)}, u32[]{:S(2)}, u32[]{:S(2)}) collective-permute-start(f32[2,3584]{1,0:T(2,128)S(1)} %get-tuple-element.123.mine_ref), channel_id=1, source_target_pairs={{0,4},{4,0},{8,12},{12,8},{16,20},{20,16},{24,28},{28,24},{1,5},{5... | collective-permute-start | bytes 86024 | tf_op jit(solution)/shard_map/ppermute | solution.py:267
  154.3 4.1 %collective-permute-start.32 = (f32[2,3584]{1,0:T(2,128)S(1)}, f32[2,3584]{1,0:T(2,128)S(1)}, u32[]{:S(2)}, u32[]{:S(2)}) collective-permute-start(f32[2,3584]{1,0:T(2,128)S(1)} %shard_map.75.mine_ref), channel_id=1, source_target_pairs={{0,8},{4,12},{8,0},{12,4},{16,24},{20,28},{24,16},{28,20},{1,9},{5... | collective-permute-start | bytes 86024 | tf_op jit(solution)/shard_map/ppermute | solution.py:267
  157.5 3.9 %collective-permute-start.29 = (f32[2,3584]{1,0:T(2,128)S(1)}, f32[2,3584]{1,0:T(2,128)S(1)}, u32[]{:S(2)}, u32[]{:S(2)}) collective-permute-start(f32[2,3584]{1,0:T(2,128)S(1)} %shard_map.71.mine_ref), channel_id=1, source_target_pairs={{0,8},{4,12},{8,0},{12,4},{16,24},{20,28},{24,16},{28,20},{1,9},{5... | collective-permute-start | bytes 86024 | tf_op jit(solution)/shard_map/ppermute | solution.py:267
  158.4 4.8 %collective-permute-start.33 = (f32[2,3584]{1,0:T(2,128)S(1)}, f32[2,3584]{1,0:T(2,128)S(1)}, u32[]{:S(2)}, u32[]{:S(2)}) collective-permute-start(f32[2,3584]{1,0:T(2,128)S(1)} %shard_map.76.mine_ref), channel_id=1, source_target_pairs={{0,16},{4,20},{8,24},{12,28},{16,0},{20,4},{24,8},{28,12},{1,17},{... | collective-permute-start | bytes 86024 | tf_op jit(solution)/shard_map/ppermute | solution.py:267
  161.5 8.0 %collective-permute-start.30 = (f32[2,3584]{1,0:T(2,128)S(1)}, f32[2,3584]{1,0:T(2,128)S(1)}, u32[]{:S(2)}, u32[]{:S(2)}) collective-permute-start(f32[2,3584]{1,0:T(2,128)S(1)} %shard_map.72.mine_ref), channel_id=1, source_target_pairs={{0,16},{4,20},{8,24},{12,28},{16,0},{20,4},{24,8},{28,12},{1,17},{... | collective-permute-start | bytes 86024 | tf_op jit(solution)/shard_map/ppermute | solution.py:267
  163.3 8.3 %copy-start.1 = (bf16[3584,3584]{1,0:T(8,128)(2,1)S(1)}, bf16[3584,3584]{1,0:T(8,128)(2,1)}, u32[]{:S(2)}) copy-start(bf16[3584,3584]{1,0:T(8,128)(2,1)} %copy-done) | copy-start | bytes 77070336
  177.8 1.2 collective-permute-start.34
  179.1 3.7 %collective-permute-start.35 = (f32[1,3584]{1,0:T(1,128)S(1)}, f32[1,3584]{1,0:T(1,128)S(1)}, u32[]{:S(2)}, u32[]{:S(2)}) collective-permute-start(f32[1,3584]{1,0:T(1,128)S(1)} %shard_map.80.mine_ref), channel_id=1, source_target_pairs={{0,2},{1,3},{2,0},{3,1},{4,6},{5,7},{6,4},{7,5},{8,10},{9,11},{10,... | collective-permute-start | bytes 43016 | tf_op jit(solution)/shard_map/ppermute | solution.py:267
  188.8 20.0 %copy-start.6 = (bf16[256,3584]{1,0:T(8,128)(2,1)S(1)}, bf16[256,3584]{1,0:T(8,128)(2,1)}, u32[]{:S(2)}) copy-start(bf16[256,3584]{1,0:T(8,128)(2,1)} %copy-done.5) | copy-start | bytes 5505028
  188.9 8.4 %collective-permute-start.36 = (f32[1,3712]{1,0:T(1,128)S(1)}, f32[1,3712]{1,0:T(1,128)S(1)}, u32[]{:S(2)}, u32[]{:S(2)}) collective-permute-start(f32[1,3712]{1,0:T(1,128)S(1)} %shard_map.82.mine_ref), channel_id=1, source_target_pairs={{0,4},{4,0},{8,12},{12,8},{16,20},{20,16},{24,28},{28,24},{1,5},{5... | collective-permute-start | bytes 44552 | tf_op jit(solution)/shard_map/ppermute | solution.py:267
  196.7 3.8 %collective-permute-start.39 = (f32[1,3712]{1,0:T(1,128)S(1)}, f32[1,3712]{1,0:T(1,128)S(1)}, u32[]{:S(2)}, u32[]{:S(2)}) collective-permute-start(f32[1,3712]{1,0:T(1,128)S(1)} %shard_map.86.mine_ref), channel_id=1, source_target_pairs={{0,4},{4,0},{8,12},{12,8},{16,20},{20,16},{24,28},{28,24},{1,5},{5... | collective-permute-start | bytes 44552 | tf_op jit(solution)/shard_map/ppermute | solution.py:267
  197.2 3.8 %collective-permute-start.37 = (f32[1,3712]{1,0:T(1,128)S(1)}, f32[1,3712]{1,0:T(1,128)S(1)}, u32[]{:S(2)}, u32[]{:S(2)}) collective-permute-start(f32[1,3712]{1,0:T(1,128)S(1)} %shard_map.83.mine_ref), channel_id=1, source_target_pairs={{0,8},{4,12},{8,0},{12,4},{16,24},{20,28},{24,16},{28,20},{1,9},{5... | collective-permute-start | bytes 44552 | tf_op jit(solution)/shard_map/ppermute | solution.py:267
  200.5 3.7 %collective-permute-start.40 = (f32[1,3712]{1,0:T(1,128)S(1)}, f32[1,3712]{1,0:T(1,128)S(1)}, u32[]{:S(2)}, u32[]{:S(2)}) collective-permute-start(f32[1,3712]{1,0:T(1,128)S(1)} %shard_map.87.mine_ref), channel_id=1, source_target_pairs={{0,8},{4,12},{8,0},{12,4},{16,24},{20,28},{24,16},{28,20},{1,9},{5... | collective-permute-start | bytes 44552 | tf_op jit(solution)/shard_map/ppermute | solution.py:267
  201.0 4.6 %collective-permute-start.38 = (f32[1,3712]{1,0:T(1,128)S(1)}, f32[1,3712]{1,0:T(1,128)S(1)}, u32[]{:S(2)}, u32[]{:S(2)}) collective-permute-start(f32[1,3712]{1,0:T(1,128)S(1)} %shard_map.84.mine_ref), channel_id=1, source_target_pairs={{0,16},{4,20},{8,24},{12,28},{16,0},{20,4},{24,8},{28,12},{1,17},{... | collective-permute-start | bytes 44552 | tf_op jit(solution)/shard_map/ppermute | solution.py:267
  204.2 4.6 %collective-permute-start.41 = (f32[1,3712]{1,0:T(1,128)S(1)}, f32[1,3712]{1,0:T(1,128)S(1)}, u32[]{:S(2)}, u32[]{:S(2)}) collective-permute-start(f32[1,3712]{1,0:T(1,128)S(1)} %shard_map.88.mine_ref), channel_id=1, source_target_pairs={{0,16},{4,20},{8,24},{12,28},{16,0},{20,4},{24,8},{28,12},{1,17},{... | collective-permute-start | bytes 44552 | tf_op jit(solution)/shard_map/ppermute | solution.py:267

commit v4 on v3

--- a/solution.py
+++ b/solution.py
@@ -37,7 +37,7 @@
     turned, wide, *blocks = rest
     row_tiles = lhs_ref.shape[1] // tm
     total = row_tiles * (rhs_ref.shape[1] // tn)
-    sub = 64
+    sub = 64 if keep or tm % 128 else 128
     lanes = tn // 128
 
     @pl.loop(0, lhs_ref.shape[1] // 128)
@@ -59,27 +59,42 @@
         rows = pl.ds(pl.multiple_of(t * tm, tm), tm)
         block[...] = jnp.dot(turned[rows, :], rhs_ref[:, cols(n)], preferred_element_type=f32)
 
-    def reduce(n, t, block, upper, total_sum):
+    def scores(t, k, block):
+        rows = pl.ds(pl.multiple_of(t * tm + k, 64), sub)
+        return block[k : k + sub, :] + jnp.concatenate([wide[rows, :]] * lanes, 1)
+
+    def raised(n, t, block, upper, total_sum):
         new = upper
-        for k in range(tm // sub):
-            rows = pl.ds(pl.multiple_of(t * tm + k * sub, sub), sub)
-            bias = jnp.concatenate([wide[rows, :]] * lanes, 1)
-            x = block[k * sub : (k + 1) * sub, :] + bias
-            block[k * sub : (k + 1) * sub, :] = x
+        for k in range(0, tm, sub):
+            x = scores(t, k, block)
+            if keep:
+                block[k : k + sub, :] = x
             new = jnp.maximum(new, x.reshape(sub // 8, 8, tn).max(0))
         row = new.max(0, keepdims=True)
         new = jnp.broadcast_to(row, (8, tn))
-        total_sum = total_sum * jnp.exp2((upper - new) * KAPPA)
-        for k in range(tm // sub):
-            rows = pl.ds(pl.multiple_of(t * tm + k * sub, sub), sub)
-            p = jnp.exp2((block[k * sub : (k + 1) * sub, :] - row) * KAPPA)
+        return row, new, total_sum * jnp.exp2((upper - new) * KAPPA)
+
+    def reduce_kept(n, t, block, upper, total_sum):
+        row, new, total_sum = raised(n, t, block, upper, total_sum)
+        for k in range(0, tm, sub):
+            rows = pl.ds(pl.multiple_of(t * tm + k, 64), sub)
+            p = jnp.exp2((block[k : k + sub, :] - row) * KAPPA)
             total_sum = total_sum + p.reshape(sub // 8, 8, tn).sum(0)
-            if keep:
-                kept_ref[rows, cols(n)] = p.astype(bf16)
-        if keep:
-            tile_max_ref[pl.ds(t, 1), cols(n)] = row
+            kept_ref[rows, cols(n)] = p.astype(bf16)
+        tile_max_ref[pl.ds(t, 1), cols(n)] = row
         return new, total_sum
 
+    def reduce_only(n, t, block, upper, total_sum):
+        row, new, total_sum = raised(n, t, block, upper, total_sum)
+        for k in range(0, tm, sub):
+            p = jnp.exp2(((scores(t, k, block) - row) * KAPPA).astype(bf16))
+            for g in range(0, sub, 64):
+                part = (p[g : g + 16] + p[g + 16 : g + 32]) + (p[g + 32 : g + 48] + p[g + 48 : g + 64])
+                part = part.astype(f32)
+                total_sum = total_sum + (part[:8] + part[8:])
+        return new, total_sum
+
+    reduce = reduce_kept if keep else reduce_only
     product(0, 0, blocks[0])
     first_sublane = lax.broadcasted_iota(jnp.int32, (8, tn), 0) == 0
 
@@ -261,17 +276,25 @@
     )(kept, tile_max, lse, row_sums)
 
 
-def group_steps(axis, size):
-    step = 1
-    while step < size:
-        yield lambda x, s=step: lax.ppermute(x, axis, [(i, i ^ s) for i in range(size)])
-        step *= 2
-
-
-def merge_kernel(last, mine_ref, other_ref, out_ref):
-    mine, other = mine_ref[...], other_ref[...]
-    top = jnp.maximum(mine[:1], other[:1])
-    total = mine[1:] * jnp.exp2((mine[:1] - top) * KAPPA) + other[1:] * jnp.exp2((other[:1] - top) * KAPPA)
+def near_first(near):
+    return [[1 << k] for k in range(near.bit_length() - 1)] + [[near, 2 * near, 3 * near]]
+
+
+def pairwise(size):
+    return [[1 << k] for k in range(size.bit_length() - 1)]
+
+
+def add_in_pairs(values):
+    while len(values) > 1:
+        values = [values[k] + values[k + 1] for k in range(0, len(values), 2)]
+    return values[0]
+
+
+def merge_kernel(last, *refs):
+    *in_refs, out_ref = refs
+    pairs = [ref[...] for ref in in_refs]
+    top = functools.reduce(jnp.maximum, [pair[:1] for pair in pairs])
+    total = add_in_pairs([pair[1:] * jnp.exp2((pair[:1] - top) * KAPPA) for pair in pairs])
     if last:
         out_ref[...] = KAPPA * top + jnp.log2(total)
     else:
@@ -279,8 +302,9 @@
         out_ref[1:2, :] = total
 
 
-def add_kernel(mine_ref, other_ref, out_ref):
-    out_ref[...] = mine_ref[...] + other_ref[...]
+def add_kernel(*refs):
+    *in_refs, out_ref = refs
+    out_ref[...] = add_in_pairs([ref[...] for ref in in_refs])
 
 
 def small_call(kernel, shape, *operands):
@@ -293,23 +317,23 @@
     )(*operands)
 
 
-def group_lse(pair, exchange_steps):
-    exchange_steps = list(exchange_steps)
-    for k, exchange in enumerate(exchange_steps):
-        last = k + 1 == len(exchange_steps)
-        shape = (1 if last else 2, pair.shape[1])
-        pair = small_call(functools.partial(merge_kernel, last), shape, pair, exchange(pair))
-    return pair
-
-
-def group_sum(x, exchange_steps):
-    for exchange in exchange_steps:
-        x = small_call(add_kernel, x.shape, x, exchange(x))
-    return x
-
-
 def swap(x, axis, size, mask):
     return lax.ppermute(x, axis, [(i, i ^ mask) for i in range(size)])
+
+
+def group_lse(pair, axis, size, steps):
+    for k, masks in enumerate(steps):
+        last = k + 1 == len(steps)
+        shape = (1 if last else 2, pair.shape[1])
+        others = [swap(pair, axis, size, mask) for mask in masks]
+        pair = small_call(functools.partial(merge_kernel, last), shape, pair, *others)
+    return pair
+
+
+def group_sum(x, axis, size, steps):
+    for masks in steps:
+        x = small_call(add_kernel, x.shape, x, *[swap(x, axis, size, mask) for mask in masks])
+    return x
 
 
 def gather_order(size, near):
@@ -326,17 +350,13 @@
 
 
 def per_device(aa_size, ba_size, acts_a, acts_b):
-    def over_a():
-        return group_steps("aa", aa_size)
-
-    def over_b():
-        return group_steps("ba", ba_size)
-
     cols_here = acts_b.shape[1]
     width = cols_here // CHUNKS
     half = cols_here // HALVES
     near = aa_size // 4
     far_masks = [f * near for f in range(1, 4)]
+    over_a = ("aa", aa_size, near_first(near))
+    over_b = ("ba", ba_size, pairwise(ba_size))
 
     tokens = acts_b.shape[0]
     per_block = aa_size // ba_size
@@ -356,7 +376,8 @@
         if c:
             own = after(own, sides[c - 1] if c >= 2 else far_a)
         group = [own] + [swap(own, "aa", aa_size, mask) for mask in far_masks]
-        group[-1] = after(group[-1], states[c - 2] if c >= 2 else far_a)
+        first = states[c - 2] if c >= 2 else far_a
+        group = [own] + [after(piece, first) for piece in group[1:]]
         mine = jnp.concatenate(group, 0)
         sides.append(mine)
         return [mine] + [swap(mine, "aa", aa_size, k) for k in range(1, near)]
@@ -364,7 +385,8 @@
     coming = start_chunk(0)
     for c in range(CHUNKS):
         group = coming
-        group[-1] = after(group[-1], states[c - 1] if c else whole_a)
+        first = states[c - 1] if c else whole_a
+        group = group[:1] + [after(piece, first) for piece in group[1:]]
         chunk = jnp.concatenate(group, 0)
         chunks.append(chunk)
         if c + 1 < CHUNKS:
@@ -373,7 +395,7 @@
         state, norm = lse_call(chunk, whole_a, None, states[c - 1] if c else None)
         states.append(state)
         norms_b.append(norm)
-    row_lse = group_lse(states[-1], over_b())
+    row_lse = group_lse(states[-1], *over_b)
     per_half = CHUNKS // HALVES
     halves = [jnp.concatenate(chunks[h * per_half : (h + 1) * per_half], 1) for h in range(HALVES)]
     log_n = math.log(NA)
@@ -388,17 +410,17 @@
     col_lse, tile_max, kept = [], [], []
     for part in halves:
         state, top, p = lse_call(whole_a, part, row_bias, keep=True)
-        col_lse.append(group_lse(state, over_a()))
+        col_lse.append(group_lse(state, *over_a))
         tile_max.append(top)
         kept.append(pltpu.with_memory_space_constraint(p, pltpu.VMEM))
     row_sums = None
     for h in range(HALVES):
         row_sums = row_sum_call(kept[h], tile_max[h], col_lse[h], row_sums)
-    row_sums = group_sum(row_sums, over_b())
+    row_sums = group_sum(row_sums, *over_b)
     col_sums = []
     for h in range(HALVES):
         sums = col_sum_call(kept[h], tile_max[h], col_lse[h], row_sums)
-        col_sums.append(group_sum(sums, over_a()))
+        col_sums.append(group_sum(sums, *over_a))
 
     def half_norms(h):
         return jnp.concatenate(norms_b[h * per_half : (h + 1) * per_half], 1)
@@ -415,11 +437,11 @@
         state = None
         for part, lse in zip(halves, col_lse):
             (state,) = lse_call(part, whole_a, lse * (-1.0 / KAPPA), state)
-        again = group_lse(state, over_b())
+        again = group_lse(state, *over_b)
         second_b = []
         for h, part in enumerate(halves):
             (state,) = lse_call(whole_a, part, again * (-1.0 / KAPPA))
-            second_b.append(potential_b_of(group_lse(state, over_a()), half_norms(h)))
+            second_b.append(potential_b_of(group_lse(state, *over_a), half_norms(h)))
         return potential_a_of(again), jnp.concatenate(second_b, 1)
 
     second_a, second_b = lax.cond(col_sums[-1][0, half] > 0.0, exact, quick, 0)

time: 211 us -> 201 us (0.953)
  waiting for transfers between devices: 40.5 us -> 23.3 us
  starting transfers between devices: 41.1 us -> 51.4 us
  Pallas kernels: 111 us -> 107 us
    ppermute x18 -> x38, starting transfers between devices: 26 us -> 51.4 us  [swap(): return lax.ppermute(x, axis, [(i, i ^ mask) for i in range(size)])]
    ppermute x16 -> x0, waiting for transfers between devices: 18.4 us -> none  [group_steps(): lax.ppermute(x, axis, [(i, i ^ s) for i in range(size)])]
    ppermute x16 -> x0, starting transfers between devices: 15.1 us -> none  [group_steps(): lax.ppermute(x, axis, [(i, i ^ s) for i in range(size)])]
    pallas_call x6, Pallas kernels: 84 us -> 80.1 us  [lse_call(): pl.pallas_call(functools.partial(lse_kernel, tm, tn, bias is not None, st...]
    unnamed x29 -> x25, local copies, waits for them, and re-layouts: 11.9 us -> 10.8 us
    ppermute x18 -> x38, waiting for transfers between devices: 22.2 us -> 23.3 us  [swap(): return lax.ppermute(x, axis, [(i, i ^ mask) for i in range(size)])]
  transfers between devices with their start and end apart: 34 -> 38, of which waited for: 21 -> 8; matrix products, arithmetic and copies ran while one was open for 1% -> 2% of each run, Pallas kernels for 32% -> 32%
where the time goes in v4:
time: 201 us; the launch traced here: 200 us
  Pallas kernels  107 us (53%)
  starting transfers between devices  51.4 us (26%)
  waiting for transfers between devices  23.3 us (12%)
  local copies, waits for them, and re-layouts  13.9 us (7%)
  other arithmetic  3.18 us (2%)
    pallas_call x6, Pallas kernels, lse_call(): pl.pallas_call(functools.partial(lse_kernel, tm, tn, bias is not None, st...  80.1 us
    ppermute x38, starting transfers between devices, swap(): return lax.ppermute(x, axis, [(i, i ^ mask) for i in range(size)])  51.4 us
    ppermute x38, waiting for transfers between devices, swap(): return lax.ppermute(x, axis, [(i, i ^ mask) for i in range(size)])  23.3 us
    pallas_call x2, Pallas kernels, row_sum_call(): pl.pallas_call(functools.partial(row_sum_kernel, first is not None), out_...  12.3 us
    pallas_call x2, Pallas kernels, col_sum_call(): pl.pallas_call(col_sum_kernel, out_shape=jax.ShapeDtypeStruct((1, n + 128...  12.3 us
    unnamed x25, local copies, waits for them, and re-layouts  10.8 us
  transfers between devices with their start and end apart: 38, of which 8 were waited for; matrix products, arithmetic and copies ran while one was open for 2% of the time, Pallas kernels for 32%

profile of v4, /device:TPU:0, one launch (start us, length us, event | category | flops | bytes accessed | tf_op | source)
XLA Modules:
  0.0 200.3 jit_solution(6224193756964528415)
XLA Ops:
  0.6 1.2 fusion.7
  1.8 5.1 %collective-permute-start.18 = (bf16[32,1792]{1,0:T(8,128)(2,1)S(1)}, bf16[32,1792]{1,0:T(8,128)(2,1)S(1)}, u32[]{:S(2)}, u32[]{:S(2)}) collective-permute-start(bf16[32,1792]{1,0:T(8,128)(2,1)S(1)} %get-tuple-element.157), channel_id=1, source_target_pairs={{0,24},{4,28},{8,16},{12,20},{16,8},{20,12},{24,0},{28,4},{1,25},{... | collective-permute-start | bytes 344072 | tf_op jit(solution)/shard_map/ppermute | solution.py:321
  7.6 1.7 collective-permute-start.10
  9.9 1.3 gather_fusion
  11.9 7.6 %collective-permute-done.10 = bf16[64,3584]{1,0:T(8,128)(2,1)S(1)} collective-permute-done((bf16[64,3584]{1,0:T(8,128)(2,1)}, bf16[64,3584]{1,0:T(8,128)(2,1)S(1)}, u32[]{:S(2)}, u32[]{:S(2)}) %collective-permute-start.10) | collective-permute-done | bytes 458784 | tf_op jit(solution)/shard_map/ppermute | solution.py:321
  19.6 3.5 %collective-permute-start.14 = (bf16[32,1792]{1,0:T(8,128)(2,1)S(1)}, bf16[32,1792]{1,0:T(8,128)(2,1)S(1)}, u32[]{:S(2)}, u32[]{:S(2)}) collective-permute-start(bf16[32,1792]{1,0:T(8,128)(2,1)S(1)} %get-tuple-element.109), channel_id=1, source_target_pairs={{0,24},{4,28},{8,16},{12,20},{16,8},{20,12},{24,0},{28,4},{1,25},{... | collective-permute-start | bytes 344072 | tf_op jit(solution)/shard_map/ppermute | solution.py:321
  23.2 0.9 collective-permute-start.12
  24.2 1.6 collective-permute-start.19
  25.8 1.7 collective-permute-done.14
  27.5 5.8 %collective-permute-done.13 = bf16[32,1792]{1,0:T(8,128)(2,1)S(1)} collective-permute-done((bf16[32,1792]{1,0:T(8,128)(2,1)S(1)}, bf16[32,1792]{1,0:T(8,128)(2,1)S(1)}, u32[]{:S(2)}, u32[]{:S(2)}) %collective-permute-start.13) | collective-permute-done | bytes 114720 | tf_op jit(solution)/shard_map/ppermute | solution.py:321
  33.4 2.4 %collective-permute-start.21 = (bf16[32,1792]{1,0:T(8,128)(2,1)S(1)}, bf16[32,1792]{1,0:T(8,128)(2,1)S(1)}, u32[]{:S(2)}, u32[]{:S(2)}) collective-permute-start(bf16[32,1792]{1,0:T(8,128)(2,1)S(1)} %get-tuple-element.113), channel_id=1, source_target_pairs={{0,24},{4,28},{8,16},{12,20},{16,8},{20,12},{24,0},{28,4},{1,25},{... | collective-permute-start | bytes 344072 | tf_op jit(solution)/shard_map/ppermute | solution.py:321
  35.9 2.0 collective-permute-start.15
  37.9 1.6 collective-permute-start.23
  39.6 1.8 shard_map.63
  41.5 9.4 %shard_map.64 = (f32[2,3584]{1,0:T(2,128)S(1)}, f32[1,1792]{1,0:T(1,128)S(1)}) custom-call(bf16[256,1792]{1,0:T(8,128)(2,1)S(1)} %constant_dynamic-update-slice_fusion.6.lhs_ref, bf16[256,3584]{1,0:T(8,128)(2,1)S(1)} %get-tuple-element.108.rhs_ref.lhs_ref), custom_call_target="tpu_custom_call" | custom-call | flops 3288334336 | bytes 2752512 | tf_op jit(solution)/shard_map/pallas_call | solution.py:141
  51.0 2.4 %collective-permute-start.25 = (bf16[32,1792]{1,0:T(8,128)(2,1)S(1)}, bf16[32,1792]{1,0:T(8,128)(2,1)S(1)}, u32[]{:S(2)}, u32[]{:S(2)}) collective-permute-start(bf16[32,1792]{1,0:T(8,128)(2,1)S(1)} %get-tuple-element.123), channel_id=1, source_target_pairs={{0,24},{4,28},{8,16},{12,20},{16,8},{20,12},{24,0},{28,4},{1,25},{... | collective-permute-start | bytes 344072 | tf_op jit(solution)/shard_map/ppermute | solution.py:321
  53.5 2.0 %collective-permute-start.22 = (bf16[32,1792]{1,0:T(8,128)(2,1)S(1)}, bf16[32,1792]{1,0:T(8,128)(2,1)S(1)}, u32[]{:S(2)}, u32[]{:S(2)}) collective-permute-start(bf16[32,1792]{1,0:T(8,128)(2,1)S(1)} %get-tuple-element.123), channel_id=1, source_target_pairs={{0,8},{4,12},{8,0},{12,4},{16,24},{20,28},{24,16},{28,20},{1,9},{5... | collective-permute-start | bytes 344072 | tf_op jit(solution)/shard_map/ppermute | solution.py:321
  56.1 9.5 %shard_map.65 = (f32[2,3584]{1,0:T(2,128)S(1)}, f32[1,1792]{1,0:T(1,128)S(1)}) custom-call(bf16[256,1792]{1,0:T(8,128)(2,1)S(1)} %constant_dynamic-update-slice_fusion.15.lhs_ref, bf16[256,3584]{1,0:T(8,128)(2,1)S(1)} %get-tuple-element.108.rhs_ref.lhs_ref, f32[2,3584]{1,0:T(2,128)S(1)} %get-tuple-element.119.rest_0_), custom_call_target="tpu_custom_call" | custom-call | flops 3288334336 | bytes 2752512 | tf_op jit(solution)/shard_map/pallas_call | solution.py:141
  65.7 1.6 collective-permute-start.26
  67.3 9.5 %shard_map.66 = (f32[2,3584]{1,0:T(2,128)S(1)}, f32[1,1792]{1,0:T(1,128)S(1)}) custom-call(bf16[256,1792]{1,0:T(8,128)(2,1)S(1)} %constant_dynamic-update-slice_fusion.24.lhs_ref, bf16[256,3584]{1,0:T(8,128)(2,1)S(1)} %get-tuple-element.108.rhs_ref.lhs_ref, f32[2,3584]{1,0:T(2,128)S(1)} %get-tuple-element.126.rest_0_), custom_call_target="tpu_custom_call" | custom-call | flops 3288334336 | bytes 2752512 | tf_op jit(solution)/shard_map/pallas_call | solution.py:141
  76.8 9.5 %shard_map.67 = (f32[2,3584]{1,0:T(2,128)S(1)}, f32[1,1792]{1,0:T(1,128)S(1)}) custom-call(bf16[256,1792]{1,0:T(8,128)(2,1)S(1)} %constant_dynamic-update-slice_fusion.29.lhs_ref, bf16[256,3584]{1,0:T(8,128)(2,1)S(1)} %get-tuple-element.108.rhs_ref.lhs_ref, f32[2,3584]{1,0:T(2,128)S(1)} %get-tuple-element.132.rest_0_), custom_call_target="tpu_custom_call" | custom-call | flops 3288334336 | bytes 2752512 | tf_op jit(solution)/shard_map/pallas_call | solution.py:141
  86.5 1.1 collective-permute-done.28.refs_1_
  87.6 1.6 collective-permute-start.29
  89.3 2.2 %collective-permute-done.29.refs_1_ = f32[2,3584]{1,0:T(2,128)S(1)} collective-permute-done((f32[2,3584]{1,0:T(2,128)S(1)}, f32[2,3584]{1,0:T(2,128)S(1)}, u32[]{:S(2)}, u32[]{:S(2)}) %collective-permute-start.29) | collective-permute-done | bytes 28704 | tf_op jit(solution)/shard_map/ppermute | solution.py:321
  91.6 20.4 %shard_map.73 = (f32[2,3584]{1,0:T(2,128)S(1)}, f32[4,3584]{1,0:T(4,128)S(1)}, bf16[3584,3584]{1,0:T(8,128)(2,1)S(1)}) custom-call(bf16[256,3584]{1,0:T(8,128)(2,1)S(1)} %get-tuple-element.108.rhs_ref.lhs_ref, bf16[256,3584]{1,0:T(8,128)(2,1)S(1)} %pad_maximum_fusion.3.rhs_ref, f32[1,3584]{1,0:T(1,128)S(1)} %broadcast_multiply_fusion.3.rest_0_), custom_call_target="tpu_custom_call" | custom-call | flops 6576668672 | bytes 3670016 | tf_op jit(solution)/shard_map/pallas_call | solution.py:141
  112.5 21.9 %shard_map.70 = (f32[2,3584]{1,0:T(2,128)S(1)}, f32[4,3584]{1,0:T(4,128)S(1)}, bf16[3584,3584]{1,0:T(8,128)(2,1)S(1)}) custom-call(bf16[256,3584]{1,0:T(8,128)(2,1)} %copy-done.3, bf16[256,3584]{1,0:T(8,128)(2,1)S(1)} %pad_maximum_fusion.4.rhs_ref, f32[1,3584]{1,0:T(1,128)S(1)} %broadcast_multiply_fusion.3.rest_0_), custom_call_target="tpu_custom_call" | custom-call | flops 6576668672 | bytes 3670016 | tf_op jit(solution)/shard_map/pallas_call | solution.py:141
  134.4 8.5 %copy-done = bf16[3584,3584]{1,0:T(8,128)(2,1)} copy-done((bf16[3584,3584]{1,0:T(8,128)(2,1)}, bf16[3584,3584]{1,0:T(8,128)(2,1)S(1)}, u32[]{:S(2)}) %copy-start) | copy-done | bytes 25690136
  142.9 1.5 collective-permute-start.30
  144.4 2.4 %collective-permute-start.37 = (f32[2,3584]{1,0:T(2,128)S(1)}, f32[2,3584]{1,0:T(2,128)S(1)}, u32[]{:S(2)}, u32[]{:S(2)}) collective-permute-start(f32[2,3584]{1,0:T(2,128)S(1)} %shard_map.74.refs_0_), channel_id=1, source_target_pairs={{0,24},{4,28},{8,16},{12,20},{16,8},{20,12},{24,0},{28,4},{1,25},{... | collective-permute-start | bytes 86024 | tf_op jit(solution)/shard_map/ppermute | solution.py:321
  146.9 2.0 %collective-permute-start.35 = (f32[2,3584]{1,0:T(2,128)S(1)}, f32[2,3584]{1,0:T(2,128)S(1)}, u32[]{:S(2)}, u32[]{:S(2)}) collective-permute-start(f32[2,3584]{1,0:T(2,128)S(1)} %shard_map.74.refs_0_), channel_id=1, source_target_pairs={{0,8},{4,12},{8,0},{12,4},{16,24},{20,28},{24,16},{28,20},{1,9},{5... | collective-permute-start | bytes 86024 | tf_op jit(solution)/shard_map/ppermute | solution.py:321
  148.9 2.4 %collective-permute-start.33 = (f32[2,3584]{1,0:T(2,128)S(1)}, f32[2,3584]{1,0:T(2,128)S(1)}, u32[]{:S(2)}, u32[]{:S(2)}) collective-permute-start(f32[2,3584]{1,0:T(2,128)S(1)} %shard_map.71.refs_0_), channel_id=1, source_target_pairs={{0,24},{4,28},{8,16},{12,20},{16,8},{20,12},{24,0},{28,4},{1,25},{... | collective-permute-start | bytes 86024 | tf_op jit(solution)/shard_map/ppermute | solution.py:321
  151.4 2.0 %collective-permute-start.31 = (f32[2,3584]{1,0:T(2,128)S(1)}, f32[2,3584]{1,0:T(2,128)S(1)}, u32[]{:S(2)}, u32[]{:S(2)}) collective-permute-start(f32[2,3584]{1,0:T(2,128)S(1)} %shard_map.71.refs_0_), channel_id=1, source_target_pairs={{0,8},{4,12},{8,0},{12,4},{16,24},{20,28},{24,16},{28,20},{1,9},{5... | collective-permute-start | bytes 86024 | tf_op jit(solution)/shard_map/ppermute | solution.py:321
  153.4 6.2 %shard_map.76.rest_0_ = f32[1,3584]{1,0:T(1,128)S(1)} custom-call(bf16[3584,3584]{1,0:T(8,128)(2,1)S(1)} %get-tuple-element.141.kept_ref, f32[4,3584]{1,0:T(4,128)S(1)} %get-tuple-element.142.tile_max_ref, f32[1,3584]{1,0:T(1,128)S(1)} %shard_map.75.lse_ref), custom_call_target="tpu_custom_call" | custom-call | flops 25690112 | bytes 25690112 | tf_op jit(solution)/shard_map/pallas_call | solution.py:219
  159.7 2.0 %copy-done.1 = bf16[3584,3584]{1,0:T(8,128)(2,1)S(1)} copy-done((bf16[3584,3584]{1,0:T(8,128)(2,1)S(1)}, bf16[3584,3584]{1,0:T(8,128)(2,1)}, u32[]{:S(2)}) %copy-start.1) | copy-done | bytes 25690136
  161.7 6.2 %shard_map.77.refs_0_ = f32[1,3584]{1,0:T(1,128)S(1)} custom-call(bf16[3584,3584]{1,0:T(8,128)(2,1)S(1)} %copy-done.1, f32[4,3584]{1,0:T(4,128)S(1)} %get-tuple-element.138.tile_max_ref, f32[1,3584]{1,0:T(1,128)S(1)} %shard_map.72.lse_ref, f32[1,3584]{1,0:T(1,128)S(1)} %shard_map.76.rest_0_), custom_call_target="tpu_custom_call" | custom-call | flops 25690112 | bytes 25690112 | tf_op jit(solution)/shard_map/pallas_call | solution.py:219
  168.0 1.2 collective-permute-done.38.refs_1_
  169.2 1.5 collective-permute-start.39
  170.7 2.2 %collective-permute-done.39.refs_1_ = f32[1,3584]{1,0:T(1,128)S(1)} collective-permute-done((f32[1,3584]{1,0:T(1,128)S(1)}, f32[1,3584]{1,0:T(1,128)S(1)}, u32[]{:S(2)}, u32[]{:S(2)}) %collective-permute-start.39) | collective-permute-done | bytes 14368 | tf_op jit(solution)/shard_map/ppermute | solution.py:321
  172.9 6.1 %shard_map.80.refs_0_ = f32[1,3712]{1,0:T(1,128)S(1)} custom-call(bf16[3584,3584]{1,0:T(8,128)(2,1)S(1)} %copy-done.1, f32[4,3584]{1,0:T(4,128)S(1)} %get-tuple-element.138.tile_max_ref, f32[1,3584]{1,0:T(1,128)S(1)} %shard_map.72.lse_ref, f32[1,3584]{1,0:T(1,128)S(1)} %shard_map.79.row_sum_ref), custom_call_target="tpu_custom_call" | custom-call | flops 25690112 | bytes 25690112 | tf_op jit(solution)/shard_map/pallas_call | solution.py:268
  179.6 6.2 %shard_map.83.refs_0_ = f32[1,3712]{1,0:T(1,128)S(1)} custom-call(bf16[3584,3584]{1,0:T(8,128)(2,1)S(1)} %get-tuple-element.141.kept_ref, f32[4,3584]{1,0:T(4,128)S(1)} %get-tuple-element.142.tile_max_ref, f32[1,3584]{1,0:T(1,128)S(1)} %shard_map.75.lse_ref, f32[1,3584]{1,0:T(1,128)S(1)} %shard_map.79.row_sum_ref), custom_call_target="tpu_custom_call" | custom-call | flops 25690112 | bytes 25690112 | tf_op jit(solution)/shard_map/pallas_call | solution.py:268
  185.8 1.6 collective-permute-start.44
  187.4 2.4 %collective-permute-start.43 = (f32[1,3712]{1,0:T(1,128)S(1)}, f32[1,3712]{1,0:T(1,128)S(1)}, u32[]{:S(2)}, u32[]{:S(2)}) collective-permute-start(f32[1,3712]{1,0:T(1,128)S(1)} %shard_map.81.refs_0_), channel_id=1, source_target_pairs={{0,24},{4,28},{8,16},{12,20},{16,8},{20,12},{24,0},{28,4},{1,25},{... | collective-permute-start | bytes 44552 | tf_op jit(solution)/shard_map/ppermute | solution.py:321
  189.8 2.0 %collective-permute-start.41 = (f32[1,3712]{1,0:T(1,128)S(1)}, f32[1,3712]{1,0:T(1,128)S(1)}, u32[]{:S(2)}, u32[]{:S(2)}) collective-permute-start(f32[1,3712]{1,0:T(1,128)S(1)} %shard_map.81.refs_0_), channel_id=1, source_target_pairs={{0,8},{4,12},{8,0},{12,4},{16,24},{20,28},{24,16},{28,20},{1,9},{5... | collective-permute-start | bytes 44552 | tf_op jit(solution)/shard_map/ppermute | solution.py:321
  191.8 2.4 %collective-permute-start.47 = (f32[1,3712]{1,0:T(1,128)S(1)}, f32[1,3712]{1,0:T(1,128)S(1)}, u32[]{:S(2)}, u32[]{:S(2)}) collective-permute-start(f32[1,3712]{1,0:T(1,128)S(1)} %shard_map.84.refs_0_), channel_id=1, source_target_pairs={{0,24},{4,28},{8,16},{12,20},{16,8},{20,12},{24,0},{28,4},{1,25},{... | collective-permute-start | bytes 44552 | tf_op jit(solution)/shard_map/ppermute | solution.py:321
  194.3 2.0 %collective-permute-start.45 = (f32[1,3712]{1,0:T(1,128)S(1)}, f32[1,3712]{1,0:T(1,128)S(1)}, u32[]{:S(2)}, u32[]{:S(2)}) collective-permute-start(f32[1,3712]{1,0:T(1,128)S(1)} %shard_map.84.refs_0_), channel_id=1, source_target_pairs={{0,8},{4,12},{8,0},{12,4},{16,24},{20,28},{24,16},{28,20},{1,9},{5... | collective-permute-start | bytes 44552 | tf_op jit(solution)/shard_map/ppermute | solution.py:321
  197.5 1.4 collective-permute-done.46.refs_2_
  198.9 1.4 conditional.1
  198.9 0.7 subtract_reduce_fusion
  (97 shorter events, 6.4 us)
Async XLA Ops:
  0.6 11.3 %copy-start.2 = (bf16[64,3584]{1,0:T(8,128)(2,1)S(1)}, bf16[64,3584]{1,0:T(8,128)(2,1)}, u32[]{:S(2)}) copy-start(bf16[64,3584]{1,0:T(8,128)(2,1)} %param.6) | copy-start | bytes 1376260
  1.8 21.3 %collective-permute-start.18 = (bf16[32,1792]{1,0:T(8,128)(2,1)S(1)}, bf16[32,1792]{1,0:T(8,128)(2,1)S(1)}, u32[]{:S(2)}, u32[]{:S(2)}) collective-permute-start(bf16[32,1792]{1,0:T(8,128)(2,1)S(1)} %get-tuple-element.157), channel_id=1, source_target_pairs={{0,24},{4,28},{8,16},{12,20},{16,8},{20,12},{24,0},{28,4},{1,25},{... | collective-permute-start | bytes 344072 | tf_op jit(solution)/shard_map/ppermute | solution.py:321
  6.9 16.3 %collective-permute-start.17 = (bf16[32,1792]{1,0:T(8,128)(2,1)S(1)}, bf16[32,1792]{1,0:T(8,128)(2,1)S(1)}, u32[]{:S(2)}, u32[]{:S(2)}) collective-permute-start(bf16[32,1792]{1,0:T(8,128)(2,1)S(1)} %get-tuple-element.157), channel_id=1, source_target_pairs={{0,16},{4,20},{8,24},{12,28},{16,0},{20,4},{24,8},{28,12},{1,17},{... | collective-permute-start | bytes 344072 | tf_op jit(solution)/shard_map/ppermute | solution.py:321
  6.9 17.2 %collective-permute-start.16 = (bf16[32,1792]{1,0:T(8,128)(2,1)S(1)}, bf16[32,1792]{1,0:T(8,128)(2,1)S(1)}, u32[]{:S(2)}, u32[]{:S(2)}) collective-permute-start(bf16[32,1792]{1,0:T(8,128)(2,1)S(1)} %get-tuple-element.157), channel_id=1, source_target_pairs={{0,8},{4,12},{8,0},{12,4},{16,24},{20,28},{24,16},{28,20},{1,9},{5... | collective-permute-start | bytes 344072 | tf_op jit(solution)/shard_map/ppermute | solution.py:321
  7.6 11.9 %collective-permute-start.10 = (bf16[64,3584]{1,0:T(8,128)(2,1)}, bf16[64,3584]{1,0:T(8,128)(2,1)S(1)}, u32[]{:S(2)}, u32[]{:S(2)}) collective-permute-start(bf16[64,3584]{1,0:T(8,128)(2,1)} %param.6), channel_id=1, source_target_pairs={{0,2},{1,3},{2,0},{3,1},{4,6},{5,7},{6,4},{7,5},{8,10},{9,11},{10,... | collective-permute-start | bytes 1376264 | tf_op jit(solution)/shard_map/ppermute | solution.py:321
  19.5 18.4 %collective-permute-start.11 = (bf16[128,3584]{1,0:T(8,128)(2,1)S(1)}, bf16[128,3584]{1,0:T(8,128)(2,1)S(1)}, u32[]{:S(2)}, u32[]{:S(2)}) collective-permute-start(bf16[128,3584]{1,0:T(8,128)(2,1)S(1)} %constant_dynamic-update-slice_fusion), channel_id=1, source_target_pairs={{0,1},{1,0},{2,3},{3,2},{4,5},{5,4},{6,7},{7,6},{8,9},{9,8},{10,11... | collective-permute-start | bytes 2752520 | tf_op jit(solution)/shard_map/ppermute | solution.py:321
  19.6 7.9 %collective-permute-start.14 = (bf16[32,1792]{1,0:T(8,128)(2,1)S(1)}, bf16[32,1792]{1,0:T(8,128)(2,1)S(1)}, u32[]{:S(2)}, u32[]{:S(2)}) collective-permute-start(bf16[32,1792]{1,0:T(8,128)(2,1)S(1)} %get-tuple-element.109), channel_id=1, source_target_pairs={{0,24},{4,28},{8,16},{12,20},{16,8},{20,12},{24,0},{28,4},{1,25},{... | collective-permute-start | bytes 344072 | tf_op jit(solution)/shard_map/ppermute | solution.py:321
  23.1 10.2 %collective-permute-start.13 = (bf16[32,1792]{1,0:T(8,128)(2,1)S(1)}, bf16[32,1792]{1,0:T(8,128)(2,1)S(1)}, u32[]{:S(2)}, u32[]{:S(2)}) collective-permute-start(bf16[32,1792]{1,0:T(8,128)(2,1)S(1)} %get-tuple-element.109), channel_id=1, source_target_pairs={{0,16},{4,20},{8,24},{12,28},{16,0},{20,4},{24,8},{28,12},{1,17},{... | collective-permute-start | bytes 344072 | tf_op jit(solution)/shard_map/ppermute | solution.py:321
  23.2 10.1 %collective-permute-start.12 = (bf16[32,1792]{1,0:T(8,128)(2,1)S(1)}, bf16[32,1792]{1,0:T(8,128)(2,1)S(1)}, u32[]{:S(2)}, u32[]{:S(2)}) collective-permute-start(bf16[32,1792]{1,0:T(8,128)(2,1)S(1)} %get-tuple-element.109), channel_id=1, source_target_pairs={{0,8},{4,12},{8,0},{12,4},{16,24},{20,28},{24,16},{28,20},{1,9},{5... | collective-permute-start | bytes 344072 | tf_op jit(solution)/shard_map/ppermute | solution.py:321
  24.2 17.2 %collective-permute-start.19 = (bf16[128,1792]{1,0:T(8,128)(2,1)S(1)}, bf16[128,1792]{1,0:T(8,128)(2,1)S(1)}, u32[]{:S(2)}, u32[]{:S(2)}) collective-permute-start(bf16[128,1792]{1,0:T(8,128)(2,1)S(1)} %pad_maximum_fusion.5), channel_id=1, source_target_pairs={{0,4},{4,0},{8,12},{12,8},{16,20},{20,16},{24,28},{28,24},{1,5},{5... | collective-permute-start | bytes 1376264 | tf_op jit(solution)/shard_map/ppermute | solution.py:321
  33.4 17.5 %collective-permute-start.21 = (bf16[32,1792]{1,0:T(8,128)(2,1)S(1)}, bf16[32,1792]{1,0:T(8,128)(2,1)S(1)}, u32[]{:S(2)}, u32[]{:S(2)}) collective-permute-start(bf16[32,1792]{1,0:T(8,128)(2,1)S(1)} %get-tuple-element.113), channel_id=1, source_target_pairs={{0,24},{4,28},{8,16},{12,20},{16,8},{20,12},{24,0},{28,4},{1,25},{... | collective-permute-start | bytes 344072 | tf_op jit(solution)/shard_map/ppermute | solution.py:321
  35.9 15.1 %collective-permute-start.20 = (bf16[32,1792]{1,0:T(8,128)(2,1)S(1)}, bf16[32,1792]{1,0:T(8,128)(2,1)S(1)}, u32[]{:S(2)}, u32[]{:S(2)}) collective-permute-start(bf16[32,1792]{1,0:T(8,128)(2,1)S(1)} %get-tuple-element.113), channel_id=1, source_target_pairs={{0,16},{4,20},{8,24},{12,28},{16,0},{20,4},{24,8},{28,12},{1,17},{... | collective-permute-start | bytes 344072 | tf_op jit(solution)/shard_map/ppermute | solution.py:321
  35.9 15.1 %collective-permute-start.15 = (bf16[32,1792]{1,0:T(8,128)(2,1)S(1)}, bf16[32,1792]{1,0:T(8,128)(2,1)S(1)}, u32[]{:S(2)}, u32[]{:S(2)}) collective-permute-start(bf16[32,1792]{1,0:T(8,128)(2,1)S(1)} %get-tuple-element.113), channel_id=1, source_target_pairs={{0,8},{4,12},{8,0},{12,4},{16,24},{20,28},{24,16},{28,20},{1,9},{5... | collective-permute-start | bytes 344072 | tf_op jit(solution)/shard_map/ppermute | solution.py:321
  37.9 18.1 %collective-permute-start.23 = (bf16[128,1792]{1,0:T(8,128)(2,1)S(1)}, bf16[128,1792]{1,0:T(8,128)(2,1)S(1)}, u32[]{:S(2)}, u32[]{:S(2)}) collective-permute-start(bf16[128,1792]{1,0:T(8,128)(2,1)S(1)} %get-tuple-element.179), channel_id=1, source_target_pairs={{0,4},{4,0},{8,12},{12,8},{16,20},{20,16},{24,28},{28,24},{1,5},{5... | collective-permute-start | bytes 1376264 | tf_op jit(solution)/shard_map/ppermute | solution.py:321
  41.4 50.1 %copy-start.3 = (bf16[256,3584]{1,0:T(8,128)(2,1)}, bf16[256,3584]{1,0:T(8,128)(2,1)S(1)}, u32[]{:S(2)}) copy-start(bf16[256,3584]{1,0:T(8,128)(2,1)S(1)} %get-tuple-element.108.rhs_ref.lhs_ref) | copy-start | bytes 5505028
  51.0 14.5 %collective-permute-start.25 = (bf16[32,1792]{1,0:T(8,128)(2,1)S(1)}, bf16[32,1792]{1,0:T(8,128)(2,1)S(1)}, u32[]{:S(2)}, u32[]{:S(2)}) collective-permute-start(bf16[32,1792]{1,0:T(8,128)(2,1)S(1)} %get-tuple-element.123), channel_id=1, source_target_pairs={{0,24},{4,28},{8,16},{12,20},{16,8},{20,12},{24,0},{28,4},{1,25},{... | collective-permute-start | bytes 344072 | tf_op jit(solution)/shard_map/ppermute | solution.py:321
  53.5 12.1 %collective-permute-start.24 = (bf16[32,1792]{1,0:T(8,128)(2,1)S(1)}, bf16[32,1792]{1,0:T(8,128)(2,1)S(1)}, u32[]{:S(2)}, u32[]{:S(2)}) collective-permute-start(bf16[32,1792]{1,0:T(8,128)(2,1)S(1)} %get-tuple-element.123), channel_id=1, source_target_pairs={{0,16},{4,20},{8,24},{12,28},{16,0},{20,4},{24,8},{28,12},{1,17},{... | collective-permute-start | bytes 344072 | tf_op jit(solution)/shard_map/ppermute | solution.py:321
  53.5 12.1 %collective-permute-start.22 = (bf16[32,1792]{1,0:T(8,128)(2,1)S(1)}, bf16[32,1792]{1,0:T(8,128)(2,1)S(1)}, u32[]{:S(2)}, u32[]{:S(2)}) collective-permute-start(bf16[32,1792]{1,0:T(8,128)(2,1)S(1)} %get-tuple-element.123), channel_id=1, source_target_pairs={{0,8},{4,12},{8,0},{12,4},{16,24},{20,28},{24,16},{28,20},{1,9},{5... | collective-permute-start | bytes 344072 | tf_op jit(solution)/shard_map/ppermute | solution.py:321
  55.5 11.7 %collective-permute-start.27 = (bf16[128,1792]{1,0:T(8,128)(2,1)S(1)}, bf16[128,1792]{1,0:T(8,128)(2,1)S(1)}, u32[]{:S(2)}, u32[]{:S(2)}) collective-permute-start(bf16[128,1792]{1,0:T(8,128)(2,1)S(1)} %get-tuple-element.163), channel_id=1, source_target_pairs={{0,4},{4,0},{8,12},{12,8},{16,20},{20,16},{24,28},{28,24},{1,5},{5... | collective-permute-start | bytes 1376264 | tf_op jit(solution)/shard_map/ppermute | solution.py:321
  65.7 11.1 %collective-permute-start.26 = (bf16[128,1792]{1,0:T(8,128)(2,1)S(1)}, bf16[128,1792]{1,0:T(8,128)(2,1)S(1)}, u32[]{:S(2)}, u32[]{:S(2)}) collective-permute-start(bf16[128,1792]{1,0:T(8,128)(2,1)S(1)} %get-tuple-element.170), channel_id=1, source_target_pairs={{0,4},{4,0},{8,12},{12,8},{16,20},{20,16},{24,28},{28,24},{1,5},{5... | collective-permute-start | bytes 1376264 | tf_op jit(solution)/shard_map/ppermute | solution.py:321
  86.3 1.3 collective-permute-start.28
  87.6 3.9 %collective-permute-start.29 = (f32[2,3584]{1,0:T(2,128)S(1)}, f32[2,3584]{1,0:T(2,128)S(1)}, u32[]{:S(2)}, u32[]{:S(2)}) collective-permute-start(f32[2,3584]{1,0:T(2,128)S(1)} %shard_map.68.refs_0_), channel_id=1, source_target_pairs={{0,2},{1,3},{2,0},{3,1},{4,6},{5,7},{6,4},{7,5},{8,10},{9,11},{10,... | collective-permute-start | bytes 86024 | tf_op jit(solution)/shard_map/ppermute | solution.py:321
  111.9 32.5 %collective-permute-start.34 = (f32[2,3584]{1,0:T(2,128)S(1)}, f32[2,3584]{1,0:T(2,128)S(1)}, u32[]{:S(2)}, u32[]{:S(2)}) collective-permute-start(f32[2,3584]{1,0:T(2,128)S(1)} %get-tuple-element.143.refs_0_), channel_id=1, source_target_pairs={{0,4},{4,0},{8,12},{12,8},{16,20},{20,16},{24,28},{28,24},{1,5},{5... | collective-permute-start | bytes 86024 | tf_op jit(solution)/shard_map/ppermute | solution.py:321
  134.4 8.5 %copy-start = (bf16[3584,3584]{1,0:T(8,128)(2,1)}, bf16[3584,3584]{1,0:T(8,128)(2,1)S(1)}, u32[]{:S(2)}) copy-start(bf16[3584,3584]{1,0:T(8,128)(2,1)S(1)} %get-tuple-element.137.kept_ref) | copy-start | bytes 77070336
  142.9 6.0 %collective-permute-start.30 = (f32[2,3584]{1,0:T(2,128)S(1)}, f32[2,3584]{1,0:T(2,128)S(1)}, u32[]{:S(2)}, u32[]{:S(2)}) collective-permute-start(f32[2,3584]{1,0:T(2,128)S(1)} %get-tuple-element.139.refs_0_), channel_id=1, source_target_pairs={{0,4},{4,0},{8,12},{12,8},{16,20},{20,16},{24,28},{28,24},{1,5},{5... | collective-permute-start | bytes 86024 | tf_op jit(solution)/shard_map/ppermute | solution.py:321
  144.4 6.9 %collective-permute-start.37 = (f32[2,3584]{1,0:T(2,128)S(1)}, f32[2,3584]{1,0:T(2,128)S(1)}, u32[]{:S(2)}, u32[]{:S(2)}) collective-permute-start(f32[2,3584]{1,0:T(2,128)S(1)} %shard_map.74.refs_0_), channel_id=1, source_target_pairs={{0,24},{4,28},{8,16},{12,20},{16,8},{20,12},{24,0},{28,4},{1,25},{... | collective-permute-start | bytes 86024 | tf_op jit(solution)/shard_map/ppermute | solution.py:321
  146.9 6.5 %collective-permute-start.36 = (f32[2,3584]{1,0:T(2,128)S(1)}, f32[2,3584]{1,0:T(2,128)S(1)}, u32[]{:S(2)}, u32[]{:S(2)}) collective-permute-start(f32[2,3584]{1,0:T(2,128)S(1)} %shard_map.74.refs_0_), channel_id=1, source_target_pairs={{0,16},{4,20},{8,24},{12,28},{16,0},{20,4},{24,8},{28,12},{1,17},{... | collective-permute-start | bytes 86024 | tf_op jit(solution)/shard_map/ppermute | solution.py:321
  146.9 6.5 %collective-permute-start.35 = (f32[2,3584]{1,0:T(2,128)S(1)}, f32[2,3584]{1,0:T(2,128)S(1)}, u32[]{:S(2)}, u32[]{:S(2)}) collective-permute-start(f32[2,3584]{1,0:T(2,128)S(1)} %shard_map.74.refs_0_), channel_id=1, source_target_pairs={{0,8},{4,12},{8,0},{12,4},{16,24},{20,28},{24,16},{28,20},{1,9},{5... | collective-permute-start | bytes 86024 | tf_op jit(solution)/shard_map/ppermute | solution.py:321
  148.9 10.7 %collective-permute-start.33 = (f32[2,3584]{1,0:T(2,128)S(1)}, f32[2,3584]{1,0:T(2,128)S(1)}, u32[]{:S(2)}, u32[]{:S(2)}) collective-permute-start(f32[2,3584]{1,0:T(2,128)S(1)} %shard_map.71.refs_0_), channel_id=1, source_target_pairs={{0,24},{4,28},{8,16},{12,20},{16,8},{20,12},{24,0},{28,4},{1,25},{... | collective-permute-start | bytes 86024 | tf_op jit(solution)/shard_map/ppermute | solution.py:321
  151.4 8.3 %collective-permute-start.32 = (f32[2,3584]{1,0:T(2,128)S(1)}, f32[2,3584]{1,0:T(2,128)S(1)}, u32[]{:S(2)}, u32[]{:S(2)}) collective-permute-start(f32[2,3584]{1,0:T(2,128)S(1)} %shard_map.71.refs_0_), channel_id=1, source_target_pairs={{0,16},{4,20},{8,24},{12,28},{16,0},{20,4},{24,8},{28,12},{1,17},{... | collective-permute-start | bytes 86024 | tf_op jit(solution)/shard_map/ppermute | solution.py:321
  151.4 8.3 %collective-permute-start.31 = (f32[2,3584]{1,0:T(2,128)S(1)}, f32[2,3584]{1,0:T(2,128)S(1)}, u32[]{:S(2)}, u32[]{:S(2)}) collective-permute-start(f32[2,3584]{1,0:T(2,128)S(1)} %shard_map.71.refs_0_), channel_id=1, source_target_pairs={{0,8},{4,12},{8,0},{12,4},{16,24},{20,28},{24,16},{28,20},{1,9},{5... | collective-permute-start | bytes 86024 | tf_op jit(solution)/shard_map/ppermute | solution.py:321
  153.4 8.3 %copy-start.1 = (bf16[3584,3584]{1,0:T(8,128)(2,1)S(1)}, bf16[3584,3584]{1,0:T(8,128)(2,1)}, u32[]{:S(2)}) copy-start(bf16[3584,3584]{1,0:T(8,128)(2,1)} %copy-done) | copy-start | bytes 77070336
  167.9 1.2 collective-permute-start.38
  169.2 3.7 %collective-permute-start.39 = (f32[1,3584]{1,0:T(1,128)S(1)}, f32[1,3584]{1,0:T(1,128)S(1)}, u32[]{:S(2)}, u32[]{:S(2)}) collective-permute-start(f32[1,3584]{1,0:T(1,128)S(1)} %shard_map.78.refs_0_), channel_id=1, source_target_pairs={{0,2},{1,3},{2,0},{3,1},{4,6},{5,7},{6,4},{7,5},{8,10},{9,11},{10,... | collective-permute-start | bytes 43016 | tf_op jit(solution)/shard_map/ppermute | solution.py:321
  179.0 19.9 %copy-start.4 = (bf16[256,3584]{1,0:T(8,128)(2,1)S(1)}, bf16[256,3584]{1,0:T(8,128)(2,1)}, u32[]{:S(2)}) copy-start(bf16[256,3584]{1,0:T(8,128)(2,1)} %copy-done.3) | copy-start | bytes 5505028
  179.0 8.4 %collective-permute-start.40 = (f32[1,3712]{1,0:T(1,128)S(1)}, f32[1,3712]{1,0:T(1,128)S(1)}, u32[]{:S(2)}, u32[]{:S(2)}) collective-permute-start(f32[1,3712]{1,0:T(1,128)S(1)} %shard_map.80.refs_0_), channel_id=1, source_target_pairs={{0,4},{4,0},{8,12},{12,8},{16,20},{20,16},{24,28},{28,24},{1,5},{5... | collective-permute-start | bytes 44552 | tf_op jit(solution)/shard_map/ppermute | solution.py:321
  185.8 6.0 %collective-permute-start.44 = (f32[1,3712]{1,0:T(1,128)S(1)}, f32[1,3712]{1,0:T(1,128)S(1)}, u32[]{:S(2)}, u32[]{:S(2)}) collective-permute-start(f32[1,3712]{1,0:T(1,128)S(1)} %shard_map.83.refs_0_), channel_id=1, source_target_pairs={{0,4},{4,0},{8,12},{12,8},{16,20},{20,16},{24,28},{28,24},{1,5},{5... | collective-permute-start | bytes 44552 | tf_op jit(solution)/shard_map/ppermute | solution.py:321
  187.4 6.9 %collective-permute-start.43 = (f32[1,3712]{1,0:T(1,128)S(1)}, f32[1,3712]{1,0:T(1,128)S(1)}, u32[]{:S(2)}, u32[]{:S(2)}) collective-permute-start(f32[1,3712]{1,0:T(1,128)S(1)} %shard_map.81.refs_0_), channel_id=1, source_target_pairs={{0,24},{4,28},{8,16},{12,20},{16,8},{20,12},{24,0},{28,4},{1,25},{... | collective-permute-start | bytes 44552 | tf_op jit(solution)/shard_map/ppermute | solution.py:321
  189.8 6.5 %collective-permute-start.42 = (f32[1,3712]{1,0:T(1,128)S(1)}, f32[1,3712]{1,0:T(1,128)S(1)}, u32[]{:S(2)}, u32[]{:S(2)}) collective-permute-start(f32[1,3712]{1,0:T(1,128)S(1)} %shard_map.81.refs_0_), channel_id=1, source_target_pairs={{0,16},{4,20},{8,24},{12,28},{16,0},{20,4},{24,8},{28,12},{1,17},{... | collective-permute-start | bytes 44552 | tf_op jit(solution)/shard_map/ppermute | solution.py:321
  189.8 6.5 %collective-permute-start.41 = (f32[1,3712]{1,0:T(1,128)S(1)}, f32[1,3712]{1,0:T(1,128)S(1)}, u32[]{:S(2)}, u32[]{:S(2)}) collective-permute-start(f32[1,3712]{1,0:T(1,128)S(1)} %shard_map.81.refs_0_), channel_id=1, source_target_pairs={{0,8},{4,12},{8,0},{12,4},{16,24},{20,28},{24,16},{28,20},{1,9},{5... | collective-permute-start | bytes 44552 | tf_op jit(solution)/shard_map/ppermute | solution.py:321
  191.8 5.6 %collective-permute-start.47 = (f32[1,3712]{1,0:T(1,128)S(1)}, f32[1,3712]{1,0:T(1,128)S(1)}, u32[]{:S(2)}, u32[]{:S(2)}) collective-permute-start(f32[1,3712]{1,0:T(1,128)S(1)} %shard_map.84.refs_0_), channel_id=1, source_target_pairs={{0,24},{4,28},{8,16},{12,20},{16,8},{20,12},{24,0},{28,4},{1,25},{... | collective-permute-start | bytes 44552 | tf_op jit(solution)/shard_map/ppermute | solution.py:321
  194.3 4.6 %collective-permute-start.46 = (f32[1,3712]{1,0:T(1,128)S(1)}, f32[1,3712]{1,0:T(1,128)S(1)}, u32[]{:S(2)}, u32[]{:S(2)}) collective-permute-start(f32[1,3712]{1,0:T(1,128)S(1)} %shard_map.84.refs_0_), channel_id=1, source_target_pairs={{0,16},{4,20},{8,24},{12,28},{16,0},{20,4},{24,8},{28,12},{1,17},{... | collective-permute-start | bytes 44552 | tf_op jit(solution)/shard_map/ppermute | solution.py:321
  194.3 4.6 %collective-permute-start.45 = (f32[1,3712]{1,0:T(1,128)S(1)}, f32[1,3712]{1,0:T(1,128)S(1)}, u32[]{:S(2)}, u32[]{:S(2)}) collective-permute-start(f32[1,3712]{1,0:T(1,128)S(1)} %shard_map.84.refs_0_), channel_id=1, source_target_pairs={{0,8},{4,12},{8,0},{12,4},{16,24},{20,28},{24,16},{28,20},{1,9},{5... | collective-permute-start | bytes 44552 | tf_op jit(solution)/shard_map/ppermute | solution.py:321

commit v5 on v4

--- a/solution.py
+++ b/solution.py
@@ -26,7 +26,7 @@
     return pltpu.CompilerParams(vmem_limit_bytes=mib << 20)
 
 
-def lse_kernel(tm, tn, biased, chained, keep, lhs_ref, rhs_ref, *rest):
+def lse_kernel(tm, tn, biased, chained, keep, staged, lhs_ref, rhs_ref, *rest):
     rest = list(rest)
     bias_ref = rest.pop(0) if biased else None
     state_in = rest.pop(0) if chained else None
@@ -35,6 +35,9 @@
     if keep:
         tile_max_ref, kept_ref = rest.pop(0), rest.pop(0)
     turned, wide, *blocks = rest
+    if staged:
+        sent = blocks.pop()
+        stage = blocks.pop()
     row_tiles = lhs_ref.shape[1] // tm
     total = row_tiles * (rhs_ref.shape[1] // tn)
     sub = 64 if keep or tm % 128 else 128
@@ -74,17 +77,27 @@
         new = jnp.broadcast_to(row, (8, tn))
         return row, new, total_sum * jnp.exp2((upper - new) * KAPPA)
 
-    def reduce_kept(n, t, block, upper, total_sum):
+    def send(step, parity, half):
+        n = step // row_tiles
+        rows = pl.ds(pl.multiple_of((step - n * row_tiles) * tm, tm), tm)
+        return pltpu.make_async_copy(
+            stage.at[parity, half], kept_ref.at[rows, cols(n)], sent.at[parity, half]
+        )
+
+    def reduce_kept(n, t, block, upper, total_sum, slot):
         row, new, total_sum = raised(n, t, block, upper, total_sum)
         for k in range(0, tm, sub):
             rows = pl.ds(pl.multiple_of(t * tm + k, 64), sub)
             p = jnp.exp2((block[k : k + sub, :] - row) * KAPPA)
             total_sum = total_sum + p.reshape(sub // 8, 8, tn).sum(0)
-            kept_ref[rows, cols(n)] = p.astype(bf16)
+            if staged:
+                stage[slot[0], slot[1], k : k + sub, :] = p.astype(bf16)
+            else:
+                kept_ref[rows, cols(n)] = p.astype(bf16)
         tile_max_ref[pl.ds(t, 1), cols(n)] = row
         return new, total_sum
 
-    def reduce_only(n, t, block, upper, total_sum):
+    def reduce_only(n, t, block, upper, total_sum, slot):
         row, new, total_sum = raised(n, t, block, upper, total_sum)
         for k in range(0, tm, sub):
             p = jnp.exp2(((scores(t, k, block) - row) * KAPPA).astype(bf16))
@@ -100,6 +113,12 @@
 
     def pair(k, carry):
         upper, total_sum = carry
+        if staged:
+            @pl.when(k >= 2)
+            def _():
+                for half in range(2):
+                    send(2 * k + half, k % 2, half).wait()
+
         for half in range(2):
             step = 2 * k + half
             n = step // row_tiles
@@ -115,16 +134,22 @@
             upper = jnp.where(t == 0, start_max, upper)
             total_sum = jnp.where(t == 0, start_sum, total_sum)
             product(n_after, after - n_after * row_tiles, blocks[1 - half])
-            upper, total_sum = reduce(n, t, blocks[half], upper, total_sum)
+            upper, total_sum = reduce(n, t, blocks[half], upper, total_sum, (k % 2, half))
             state_ref[0:1, cols(n)] = upper[:1]
             state_ref[1:2, cols(n)] = jnp.sum(total_sum, 0, keepdims=True)
+        if staged:
+            for half in range(2):
+                send(2 * k + half, k % 2, half).start()
         return upper, total_sum
 
     zeros = jnp.zeros((8, tn), f32)
     lax.fori_loop(0, total // 2, pair, (zeros, zeros))
-
-
-def lse_call(lhs, rhs, bias=None, state=None, keep=False):
+    if staged:
+        for step in range(4):
+            send(step, step // 2, step % 2).wait()
+
+
+def lse_call(lhs, rhs, bias=None, state=None, keep=False, staged=False):
     depth, m = lhs.shape
     n = rhs.shape[1]
     tm, tn = (896, 512) if n % 512 == 0 else (448, 896)
@@ -137,15 +162,17 @@
     if state is not None:
         operands += [state]
     if keep:
-        outs += [jax.ShapeDtypeStruct((m // tm, n), f32), pltpu.VMEM((m, n), bf16)]
+        place = pltpu.HBM if staged else pltpu.VMEM
+        outs += [jax.ShapeDtypeStruct((m // tm, n), f32), place((m, n), bf16)]
     return pl.pallas_call(
-        functools.partial(lse_kernel, tm, tn, bias is not None, state is not None, keep),
+        functools.partial(lse_kernel, tm, tn, bias is not None, state is not None, keep, staged),
         out_shape=outs,
         in_specs=[VMEM] * len(operands),
-        out_specs=[VMEM] * len(outs),
+        out_specs=[VMEM] * (len(outs) - 1) + [pl.BlockSpec(memory_space=pltpu.HBM) if staged else VMEM],
         scratch_shapes=[pltpu.VMEM((m, depth), bf16), pltpu.VMEM((m, 128), f32)]
-        + [pltpu.VMEM((tm, tn), f32)] * 2,
-        compiler_params=params(9 if keep else 12),
+        + [pltpu.VMEM((tm, tn), f32)] * 2
+        + ([pltpu.VMEM((2, 2, tm, tn), bf16), pltpu.SemaphoreType.DMA((2, 2))] if staged else []),
+        compiler_params=params(14 if staged else 9 if keep else 12),
         cost_estimate=pl.CostEstimate(flops=512 * m * n, bytes_accessed=512 * (m + n), transcendentals=m * n),
     )(*operands)
 
@@ -408,8 +435,8 @@
 
     row_bias, halves = lax.optimization_barrier((row_lse * (-1.0 / KAPPA), halves))
     col_lse, tile_max, kept = [], [], []
-    for part in halves:
-        state, top, p = lse_call(whole_a, part, row_bias, keep=True)
+    for h, part in enumerate(halves):
+        state, top, p = lse_call(whole_a, part, row_bias, keep=True, staged=h + 1 == HALVES)
         col_lse.append(group_lse(state, *over_a))
         tile_max.append(top)
         kept.append(pltpu.with_memory_space_constraint(p, pltpu.VMEM))

time: 201 us -> 194 us (0.965)
  local copies, waits for them, and re-layouts: 13.9 us -> 5.46 us
    unnamed x25 -> x19, local copies, waits for them, and re-layouts: 10.8 us -> 2.31 us
    pallas_call x6, Pallas kernels: 80.1 us -> 82.4 us  [lse_call(): pl.pallas_call(functools.partial(lse_kernel, tm, tn, bias is not None, st...]
  transfers between devices with their start and end apart: 38 -> 38, of which waited for: 8 -> 8; matrix products, arithmetic and copies ran while one was open for 2% -> 2% of each run, Pallas kernels for 32% -> 34%
where the time goes in v5:
time: 194 us
  Pallas kernels  109 us (56%)
  starting transfers between devices  51.5 us (27%)
  waiting for transfers between devices  23.2 us (12%)
  local copies, waits for them, and re-layouts  5.46 us (3%)
  other arithmetic  3.18 us (2%)
    pallas_call x6, Pallas kernels, lse_call(): pl.pallas_call(functools.partial(lse_kernel, tm, tn, bias is not None, st...  82.4 us
    ppermute x38, starting transfers between devices, swap(): return lax.ppermute(x, axis, [(i, i ^ mask) for i in range(size)])  51.5 us
    ppermute x38, waiting for transfers between devices, swap(): return lax.ppermute(x, axis, [(i, i ^ mask) for i in range(size)])  23.2 us
    pallas_call x2, Pallas kernels, row_sum_call(): pl.pallas_call(functools.partial(row_sum_kernel, first is not None), out_...  12.3 us
    pallas_call x2, Pallas kernels, col_sum_call(): pl.pallas_call(col_sum_kernel, out_shape=jax.ShapeDtypeStruct((1, n + 128...  12.3 us
  transfers between devices with their start and end apart: 38, of which 8 were waited for; matrix products, arithmetic and copies ran while one was open for 2% of the time, Pallas kernels for 34%

profile of v5, /device:TPU:0, one launch (start us, length us, event | category | flops | bytes accessed | tf_op | source)
XLA Modules:
  0.0 194.2 jit_solution(3416957676439846058)
XLA Ops:
  0.6 1.2 fusion.7
  1.8 5.1 %collective-permute-start.18 = (bf16[32,1792]{1,0:T(8,128)(2,1)S(1)}, bf16[32,1792]{1,0:T(8,128)(2,1)S(1)}, u32[]{:S(2)}, u32[]{:S(2)}) collective-permute-start(bf16[32,1792]{1,0:T(8,128)(2,1)S(1)} %get-tuple-element.157), channel_id=1, source_target_pairs={{0,24},{4,28},{8,16},{12,20},{16,8},{20,12},{24,0},{28,4},{1,25},{... | collective-permute-start | bytes 344072 | tf_op jit(solution)/shard_map/ppermute | solution.py:348
  7.6 1.7 collective-permute-start.10
  9.9 1.3 gather_fusion
  11.2 0.7 fusion.6.table_ref
  11.9 7.6 %collective-permute-done.10 = bf16[64,3584]{1,0:T(8,128)(2,1)S(1)} collective-permute-done((bf16[64,3584]{1,0:T(8,128)(2,1)}, bf16[64,3584]{1,0:T(8,128)(2,1)S(1)}, u32[]{:S(2)}, u32[]{:S(2)}) %collective-permute-start.10) | collective-permute-done | bytes 458784 | tf_op jit(solution)/shard_map/ppermute | solution.py:348
  19.6 3.5 %collective-permute-start.14 = (bf16[32,1792]{1,0:T(8,128)(2,1)S(1)}, bf16[32,1792]{1,0:T(8,128)(2,1)S(1)}, u32[]{:S(2)}, u32[]{:S(2)}) collective-permute-start(bf16[32,1792]{1,0:T(8,128)(2,1)S(1)} %get-tuple-element.109), channel_id=1, source_target_pairs={{0,24},{4,28},{8,16},{12,20},{16,8},{20,12},{24,0},{28,4},{1,25},{... | collective-permute-start | bytes 344072 | tf_op jit(solution)/shard_map/ppermute | solution.py:348
  23.2 0.9 collective-permute-start.12
  24.2 1.6 collective-permute-start.19
  25.8 1.7 collective-permute-done.14
  27.5 5.8 %collective-permute-done.13 = bf16[32,1792]{1,0:T(8,128)(2,1)S(1)} collective-permute-done((bf16[32,1792]{1,0:T(8,128)(2,1)S(1)}, bf16[32,1792]{1,0:T(8,128)(2,1)S(1)}, u32[]{:S(2)}, u32[]{:S(2)}) %collective-permute-start.13) | collective-permute-done | bytes 114720 | tf_op jit(solution)/shard_map/ppermute | solution.py:348
  33.4 2.4 %collective-permute-start.21 = (bf16[32,1792]{1,0:T(8,128)(2,1)S(1)}, bf16[32,1792]{1,0:T(8,128)(2,1)S(1)}, u32[]{:S(2)}, u32[]{:S(2)}) collective-permute-start(bf16[32,1792]{1,0:T(8,128)(2,1)S(1)} %get-tuple-element.113), channel_id=1, source_target_pairs={{0,24},{4,28},{8,16},{12,20},{16,8},{20,12},{24,0},{28,4},{1,25},{... | collective-permute-start | bytes 344072 | tf_op jit(solution)/shard_map/ppermute | solution.py:348
  35.9 2.0 %collective-permute-start.15 = (bf16[32,1792]{1,0:T(8,128)(2,1)S(1)}, bf16[32,1792]{1,0:T(8,128)(2,1)S(1)}, u32[]{:S(2)}, u32[]{:S(2)}) collective-permute-start(bf16[32,1792]{1,0:T(8,128)(2,1)S(1)} %get-tuple-element.113), channel_id=1, source_target_pairs={{0,8},{4,12},{8,0},{12,4},{16,24},{20,28},{24,16},{28,20},{1,9},{5... | collective-permute-start | bytes 344072 | tf_op jit(solution)/shard_map/ppermute | solution.py:348
  37.9 1.6 collective-permute-start.23
  39.6 1.8 shard_map.63
  41.5 9.4 %shard_map.64 = (f32[2,3584]{1,0:T(2,128)S(1)}, f32[1,1792]{1,0:T(1,128)S(1)}) custom-call(bf16[256,1792]{1,0:T(8,128)(2,1)S(1)} %constant_dynamic-update-slice_fusion.6.lhs_ref, bf16[256,3584]{1,0:T(8,128)(2,1)S(1)} %get-tuple-element.108.rhs_ref.lhs_ref), custom_call_target="tpu_custom_call" | custom-call | flops 3288334336 | bytes 2752512 | tf_op jit(solution)/shard_map/pallas_call | solution.py:167
  51.0 2.4 %collective-permute-start.25 = (bf16[32,1792]{1,0:T(8,128)(2,1)S(1)}, bf16[32,1792]{1,0:T(8,128)(2,1)S(1)}, u32[]{:S(2)}, u32[]{:S(2)}) collective-permute-start(bf16[32,1792]{1,0:T(8,128)(2,1)S(1)} %get-tuple-element.123), channel_id=1, source_target_pairs={{0,24},{4,28},{8,16},{12,20},{16,8},{20,12},{24,0},{28,4},{1,25},{... | collective-permute-start | bytes 344072 | tf_op jit(solution)/shard_map/ppermute | solution.py:348
  53.5 2.0 %collective-permute-start.22 = (bf16[32,1792]{1,0:T(8,128)(2,1)S(1)}, bf16[32,1792]{1,0:T(8,128)(2,1)S(1)}, u32[]{:S(2)}, u32[]{:S(2)}) collective-permute-start(bf16[32,1792]{1,0:T(8,128)(2,1)S(1)} %get-tuple-element.123), channel_id=1, source_target_pairs={{0,8},{4,12},{8,0},{12,4},{16,24},{20,28},{24,16},{28,20},{1,9},{5... | collective-permute-start | bytes 344072 | tf_op jit(solution)/shard_map/ppermute | solution.py:348
  56.1 9.5 %shard_map.65 = (f32[2,3584]{1,0:T(2,128)S(1)}, f32[1,1792]{1,0:T(1,128)S(1)}) custom-call(bf16[256,1792]{1,0:T(8,128)(2,1)S(1)} %constant_dynamic-update-slice_fusion.15.lhs_ref, bf16[256,3584]{1,0:T(8,128)(2,1)S(1)} %get-tuple-element.108.rhs_ref.lhs_ref, f32[2,3584]{1,0:T(2,128)S(1)} %get-tuple-element.119.rest_0_), custom_call_target="tpu_custom_call" | custom-call | flops 3288334336 | bytes 2752512 | tf_op jit(solution)/shard_map/pallas_call | solution.py:167
  65.7 1.6 collective-permute-start.26
  67.3 9.5 %shard_map.66 = (f32[2,3584]{1,0:T(2,128)S(1)}, f32[1,1792]{1,0:T(1,128)S(1)}) custom-call(bf16[256,1792]{1,0:T(8,128)(2,1)S(1)} %constant_dynamic-update-slice_fusion.24.lhs_ref, bf16[256,3584]{1,0:T(8,128)(2,1)S(1)} %get-tuple-element.108.rhs_ref.lhs_ref, f32[2,3584]{1,0:T(2,128)S(1)} %get-tuple-element.126.rest_0_), custom_call_target="tpu_custom_call" | custom-call | flops 3288334336 | bytes 2752512 | tf_op jit(solution)/shard_map/pallas_call | solution.py:167
  76.8 9.5 %shard_map.67 = (f32[2,3584]{1,0:T(2,128)S(1)}, f32[1,1792]{1,0:T(1,128)S(1)}) custom-call(bf16[256,1792]{1,0:T(8,128)(2,1)S(1)} %constant_dynamic-update-slice_fusion.29.lhs_ref, bf16[256,3584]{1,0:T(8,128)(2,1)S(1)} %get-tuple-element.108.rhs_ref.lhs_ref, f32[2,3584]{1,0:T(2,128)S(1)} %get-tuple-element.132.rest_0_), custom_call_target="tpu_custom_call" | custom-call | flops 3288334336 | bytes 2752512 | tf_op jit(solution)/shard_map/pallas_call | solution.py:167
  86.5 1.1 collective-permute-done.28.refs_1_
  87.6 1.6 collective-permute-start.29
  89.3 2.2 %collective-permute-done.29.refs_1_ = f32[2,3584]{1,0:T(2,128)S(1)} collective-permute-done((f32[2,3584]{1,0:T(2,128)S(1)}, f32[2,3584]{1,0:T(2,128)S(1)}, u32[]{:S(2)}, u32[]{:S(2)}) %collective-permute-start.29) | collective-permute-done | bytes 28704 | tf_op jit(solution)/shard_map/ppermute | solution.py:348
  91.5 20.4 %shard_map.73 = (f32[2,3584]{1,0:T(2,128)S(1)}, f32[4,3584]{1,0:T(4,128)S(1)}, bf16[3584,3584]{1,0:T(8,128)(2,1)S(1)}) custom-call(bf16[256,3584]{1,0:T(8,128)(2,1)S(1)} %get-tuple-element.108.rhs_ref.lhs_ref, bf16[256,3584]{1,0:T(8,128)(2,1)S(1)} %pad_maximum_fusion.3.rhs_ref, f32[1,3584]{1,0:T(1,128)S(1)} %broadcast_multiply_fusion.3.rest_0_), custom_call_target="tpu_custom_call" | custom-call | flops 6576668672 | bytes 3670016 | tf_op jit(solution)/shard_map/pallas_call | solution.py:167
  112.5 24.2 %shard_map.70 = (f32[2,3584]{1,0:T(2,128)S(1)}, f32[4,3584]{1,0:T(4,128)S(1)}, bf16[3584,3584]{1,0:T(8,128)(2,1)}) custom-call(bf16[256,3584]{1,0:T(8,128)(2,1)S(1)} %get-tuple-element.108.rhs_ref.lhs_ref, bf16[256,3584]{1,0:T(8,128)(2,1)S(1)} %pad_maximum_fusion.4.rhs_ref, f32[1,3584]{1,0:T(1,128)S(1)} %broadcast_multiply_fusion.3.rest_0_), custom_call_target="tpu_custom_call" | custom-call | flops 6576668672 | bytes 3670016 | tf_op jit(solution)/shard_map/pallas_call | solution.py:167
  136.7 1.6 collective-permute-start.30
  138.3 2.4 %collective-permute-start.37 = (f32[2,3584]{1,0:T(2,128)S(1)}, f32[2,3584]{1,0:T(2,128)S(1)}, u32[]{:S(2)}, u32[]{:S(2)}) collective-permute-start(f32[2,3584]{1,0:T(2,128)S(1)} %shard_map.74.refs_0_), channel_id=1, source_target_pairs={{0,24},{4,28},{8,16},{12,20},{16,8},{20,12},{24,0},{28,4},{1,25},{... | collective-permute-start | bytes 86024 | tf_op jit(solution)/shard_map/ppermute | solution.py:348
  140.8 2.0 %collective-permute-start.35 = (f32[2,3584]{1,0:T(2,128)S(1)}, f32[2,3584]{1,0:T(2,128)S(1)}, u32[]{:S(2)}, u32[]{:S(2)}) collective-permute-start(f32[2,3584]{1,0:T(2,128)S(1)} %shard_map.74.refs_0_), channel_id=1, source_target_pairs={{0,8},{4,12},{8,0},{12,4},{16,24},{20,28},{24,16},{28,20},{1,9},{5... | collective-permute-start | bytes 86024 | tf_op jit(solution)/shard_map/ppermute | solution.py:348
  142.8 2.4 %collective-permute-start.33 = (f32[2,3584]{1,0:T(2,128)S(1)}, f32[2,3584]{1,0:T(2,128)S(1)}, u32[]{:S(2)}, u32[]{:S(2)}) collective-permute-start(f32[2,3584]{1,0:T(2,128)S(1)} %shard_map.71.refs_0_), channel_id=1, source_target_pairs={{0,24},{4,28},{8,16},{12,20},{16,8},{20,12},{24,0},{28,4},{1,25},{... | collective-permute-start | bytes 86024 | tf_op jit(solution)/shard_map/ppermute | solution.py:348
  145.2 2.0 %collective-permute-start.31 = (f32[2,3584]{1,0:T(2,128)S(1)}, f32[2,3584]{1,0:T(2,128)S(1)}, u32[]{:S(2)}, u32[]{:S(2)}) collective-permute-start(f32[2,3584]{1,0:T(2,128)S(1)} %shard_map.71.refs_0_), channel_id=1, source_target_pairs={{0,8},{4,12},{8,0},{12,4},{16,24},{20,28},{24,16},{28,20},{1,9},{5... | collective-permute-start | bytes 86024 | tf_op jit(solution)/shard_map/ppermute | solution.py:348
  147.3 6.1 %shard_map.76.rest_0_ = f32[1,3584]{1,0:T(1,128)S(1)} custom-call(bf16[3584,3584]{1,0:T(8,128)(2,1)S(1)} %get-tuple-element.141.kept_ref, f32[4,3584]{1,0:T(4,128)S(1)} %get-tuple-element.142.tile_max_ref, f32[1,3584]{1,0:T(1,128)S(1)} %shard_map.75.lse_ref), custom_call_target="tpu_custom_call" | custom-call | flops 25690112 | bytes 25690112 | tf_op jit(solution)/shard_map/pallas_call | solution.py:246
  153.6 2.1 %copy-done = bf16[3584,3584]{1,0:T(8,128)(2,1)S(1)} copy-done((bf16[3584,3584]{1,0:T(8,128)(2,1)S(1)}, bf16[3584,3584]{1,0:T(8,128)(2,1)}, u32[]{:S(2)}) %copy-start) | copy-done | bytes 25690136
  155.6 6.2 %shard_map.77.refs_0_ = f32[1,3584]{1,0:T(1,128)S(1)} custom-call(bf16[3584,3584]{1,0:T(8,128)(2,1)S(1)} %copy-done, f32[4,3584]{1,0:T(4,128)S(1)} %get-tuple-element.138.tile_max_ref, f32[1,3584]{1,0:T(1,128)S(1)} %shard_map.72.lse_ref, f32[1,3584]{1,0:T(1,128)S(1)} %shard_map.76.rest_0_), custom_call_target="tpu_custom_call" | custom-call | flops 25690112 | bytes 25690112 | tf_op jit(solution)/shard_map/pallas_call | solution.py:246
  161.9 1.2 collective-permute-done.38.refs_1_
  163.0 1.5 collective-permute-start.39
  164.6 2.2 %collective-permute-done.39.refs_1_ = f32[1,3584]{1,0:T(1,128)S(1)} collective-permute-done((f32[1,3584]{1,0:T(1,128)S(1)}, f32[1,3584]{1,0:T(1,128)S(1)}, u32[]{:S(2)}, u32[]{:S(2)}) %collective-permute-start.39) | collective-permute-done | bytes 14368 | tf_op jit(solution)/shard_map/ppermute | solution.py:348
  166.8 6.1 %shard_map.80.refs_0_ = f32[1,3712]{1,0:T(1,128)S(1)} custom-call(bf16[3584,3584]{1,0:T(8,128)(2,1)S(1)} %copy-done, f32[4,3584]{1,0:T(4,128)S(1)} %get-tuple-element.138.tile_max_ref, f32[1,3584]{1,0:T(1,128)S(1)} %shard_map.72.lse_ref, f32[1,3584]{1,0:T(1,128)S(1)} %shard_map.79.row_sum_ref), custom_call_target="tpu_custom_call" | custom-call | flops 25690112 | bytes 25690112 | tf_op jit(solution)/shard_map/pallas_call | solution.py:295
  173.4 6.2 %shard_map.83.refs_0_ = f32[1,3712]{1,0:T(1,128)S(1)} custom-call(bf16[3584,3584]{1,0:T(8,128)(2,1)S(1)} %get-tuple-element.141.kept_ref, f32[4,3584]{1,0:T(4,128)S(1)} %get-tuple-element.142.tile_max_ref, f32[1,3584]{1,0:T(1,128)S(1)} %shard_map.75.lse_ref, f32[1,3584]{1,0:T(1,128)S(1)} %shard_map.79.row_sum_ref), custom_call_target="tpu_custom_call" | custom-call | flops 25690112 | bytes 25690112 | tf_op jit(solution)/shard_map/pallas_call | solution.py:295
  179.7 1.6 collective-permute-start.44
  181.3 2.4 %collective-permute-start.43 = (f32[1,3712]{1,0:T(1,128)S(1)}, f32[1,3712]{1,0:T(1,128)S(1)}, u32[]{:S(2)}, u32[]{:S(2)}) collective-permute-start(f32[1,3712]{1,0:T(1,128)S(1)} %shard_map.81.refs_0_), channel_id=1, source_target_pairs={{0,24},{4,28},{8,16},{12,20},{16,8},{20,12},{24,0},{28,4},{1,25},{... | collective-permute-start | bytes 44552 | tf_op jit(solution)/shard_map/ppermute | solution.py:348
  183.7 2.0 %collective-permute-start.41 = (f32[1,3712]{1,0:T(1,128)S(1)}, f32[1,3712]{1,0:T(1,128)S(1)}, u32[]{:S(2)}, u32[]{:S(2)}) collective-permute-start(f32[1,3712]{1,0:T(1,128)S(1)} %shard_map.81.refs_0_), channel_id=1, source_target_pairs={{0,8},{4,12},{8,0},{12,4},{16,24},{20,28},{24,16},{28,20},{1,9},{5... | collective-permute-start | bytes 44552 | tf_op jit(solution)/shard_map/ppermute | solution.py:348
  185.7 2.4 %collective-permute-start.47 = (f32[1,3712]{1,0:T(1,128)S(1)}, f32[1,3712]{1,0:T(1,128)S(1)}, u32[]{:S(2)}, u32[]{:S(2)}) collective-permute-start(f32[1,3712]{1,0:T(1,128)S(1)} %shard_map.84.refs_0_), channel_id=1, source_target_pairs={{0,24},{4,28},{8,16},{12,20},{16,8},{20,12},{24,0},{28,4},{1,25},{... | collective-permute-start | bytes 44552 | tf_op jit(solution)/shard_map/ppermute | solution.py:348
  188.2 2.0 %collective-permute-start.45 = (f32[1,3712]{1,0:T(1,128)S(1)}, f32[1,3712]{1,0:T(1,128)S(1)}, u32[]{:S(2)}, u32[]{:S(2)}) collective-permute-start(f32[1,3712]{1,0:T(1,128)S(1)} %shard_map.84.refs_0_), channel_id=1, source_target_pairs={{0,8},{4,12},{8,0},{12,4},{16,24},{20,28},{24,16},{28,20},{1,9},{5... | collective-permute-start | bytes 44552 | tf_op jit(solution)/shard_map/ppermute | solution.py:348
  191.4 1.4 collective-permute-done.46.refs_2_
  192.8 1.4 conditional.1
  192.8 0.7 subtract_reduce_fusion
  (91 shorter events, 5.7 us)
Async XLA Ops:
  0.6 11.3 %copy-start.1 = (bf16[64,3584]{1,0:T(8,128)(2,1)S(1)}, bf16[64,3584]{1,0:T(8,128)(2,1)}, u32[]{:S(2)}) copy-start(bf16[64,3584]{1,0:T(8,128)(2,1)} %param.6) | copy-start | bytes 1376260
  1.8 21.3 %collective-permute-start.18 = (bf16[32,1792]{1,0:T(8,128)(2,1)S(1)}, bf16[32,1792]{1,0:T(8,128)(2,1)S(1)}, u32[]{:S(2)}, u32[]{:S(2)}) collective-permute-start(bf16[32,1792]{1,0:T(8,128)(2,1)S(1)} %get-tuple-element.157), channel_id=1, source_target_pairs={{0,24},{4,28},{8,16},{12,20},{16,8},{20,12},{24,0},{28,4},{1,25},{... | collective-permute-start | bytes 344072 | tf_op jit(solution)/shard_map/ppermute | solution.py:348
  6.9 16.3 %collective-permute-start.17 = (bf16[32,1792]{1,0:T(8,128)(2,1)S(1)}, bf16[32,1792]{1,0:T(8,128)(2,1)S(1)}, u32[]{:S(2)}, u32[]{:S(2)}) collective-permute-start(bf16[32,1792]{1,0:T(8,128)(2,1)S(1)} %get-tuple-element.157), channel_id=1, source_target_pairs={{0,16},{4,20},{8,24},{12,28},{16,0},{20,4},{24,8},{28,12},{1,17},{... | collective-permute-start | bytes 344072 | tf_op jit(solution)/shard_map/ppermute | solution.py:348
  6.9 17.2 %collective-permute-start.16 = (bf16[32,1792]{1,0:T(8,128)(2,1)S(1)}, bf16[32,1792]{1,0:T(8,128)(2,1)S(1)}, u32[]{:S(2)}, u32[]{:S(2)}) collective-permute-start(bf16[32,1792]{1,0:T(8,128)(2,1)S(1)} %get-tuple-element.157), channel_id=1, source_target_pairs={{0,8},{4,12},{8,0},{12,4},{16,24},{20,28},{24,16},{28,20},{1,9},{5... | collective-permute-start | bytes 344072 | tf_op jit(solution)/shard_map/ppermute | solution.py:348
  7.6 11.9 %collective-permute-start.10 = (bf16[64,3584]{1,0:T(8,128)(2,1)}, bf16[64,3584]{1,0:T(8,128)(2,1)S(1)}, u32[]{:S(2)}, u32[]{:S(2)}) collective-permute-start(bf16[64,3584]{1,0:T(8,128)(2,1)} %param.6), channel_id=1, source_target_pairs={{0,2},{1,3},{2,0},{3,1},{4,6},{5,7},{6,4},{7,5},{8,10},{9,11},{10,... | collective-permute-start | bytes 1376264 | tf_op jit(solution)/shard_map/ppermute | solution.py:348
  19.5 18.4 %collective-permute-start.11 = (bf16[128,3584]{1,0:T(8,128)(2,1)S(1)}, bf16[128,3584]{1,0:T(8,128)(2,1)S(1)}, u32[]{:S(2)}, u32[]{:S(2)}) collective-permute-start(bf16[128,3584]{1,0:T(8,128)(2,1)S(1)} %constant_dynamic-update-slice_fusion), channel_id=1, source_target_pairs={{0,1},{1,0},{2,3},{3,2},{4,5},{5,4},{6,7},{7,6},{8,9},{9,8},{10,11... | collective-permute-start | bytes 2752520 | tf_op jit(solution)/shard_map/ppermute | solution.py:348
  19.6 7.9 %collective-permute-start.14 = (bf16[32,1792]{1,0:T(8,128)(2,1)S(1)}, bf16[32,1792]{1,0:T(8,128)(2,1)S(1)}, u32[]{:S(2)}, u32[]{:S(2)}) collective-permute-start(bf16[32,1792]{1,0:T(8,128)(2,1)S(1)} %get-tuple-element.109), channel_id=1, source_target_pairs={{0,24},{4,28},{8,16},{12,20},{16,8},{20,12},{24,0},{28,4},{1,25},{... | collective-permute-start | bytes 344072 | tf_op jit(solution)/shard_map/ppermute | solution.py:348
  23.1 10.2 %collective-permute-start.13 = (bf16[32,1792]{1,0:T(8,128)(2,1)S(1)}, bf16[32,1792]{1,0:T(8,128)(2,1)S(1)}, u32[]{:S(2)}, u32[]{:S(2)}) collective-permute-start(bf16[32,1792]{1,0:T(8,128)(2,1)S(1)} %get-tuple-element.109), channel_id=1, source_target_pairs={{0,16},{4,20},{8,24},{12,28},{16,0},{20,4},{24,8},{28,12},{1,17},{... | collective-permute-start | bytes 344072 | tf_op jit(solution)/shard_map/ppermute | solution.py:348
  23.2 10.1 %collective-permute-start.12 = (bf16[32,1792]{1,0:T(8,128)(2,1)S(1)}, bf16[32,1792]{1,0:T(8,128)(2,1)S(1)}, u32[]{:S(2)}, u32[]{:S(2)}) collective-permute-start(bf16[32,1792]{1,0:T(8,128)(2,1)S(1)} %get-tuple-element.109), channel_id=1, source_target_pairs={{0,8},{4,12},{8,0},{12,4},{16,24},{20,28},{24,16},{28,20},{1,9},{5... | collective-permute-start | bytes 344072 | tf_op jit(solution)/shard_map/ppermute | solution.py:348
  24.2 17.2 %collective-permute-start.19 = (bf16[128,1792]{1,0:T(8,128)(2,1)S(1)}, bf16[128,1792]{1,0:T(8,128)(2,1)S(1)}, u32[]{:S(2)}, u32[]{:S(2)}) collective-permute-start(bf16[128,1792]{1,0:T(8,128)(2,1)S(1)} %pad_maximum_fusion.5), channel_id=1, source_target_pairs={{0,4},{4,0},{8,12},{12,8},{16,20},{20,16},{24,28},{28,24},{1,5},{5... | collective-permute-start | bytes 1376264 | tf_op jit(solution)/shard_map/ppermute | solution.py:348
  33.4 17.5 %collective-permute-start.21 = (bf16[32,1792]{1,0:T(8,128)(2,1)S(1)}, bf16[32,1792]{1,0:T(8,128)(2,1)S(1)}, u32[]{:S(2)}, u32[]{:S(2)}) collective-permute-start(bf16[32,1792]{1,0:T(8,128)(2,1)S(1)} %get-tuple-element.113), channel_id=1, source_target_pairs={{0,24},{4,28},{8,16},{12,20},{16,8},{20,12},{24,0},{28,4},{1,25},{... | collective-permute-start | bytes 344072 | tf_op jit(solution)/shard_map/ppermute | solution.py:348
  35.9 15.1 %collective-permute-start.20 = (bf16[32,1792]{1,0:T(8,128)(2,1)S(1)}, bf16[32,1792]{1,0:T(8,128)(2,1)S(1)}, u32[]{:S(2)}, u32[]{:S(2)}) collective-permute-start(bf16[32,1792]{1,0:T(8,128)(2,1)S(1)} %get-tuple-element.113), channel_id=1, source_target_pairs={{0,16},{4,20},{8,24},{12,28},{16,0},{20,4},{24,8},{28,12},{1,17},{... | collective-permute-start | bytes 344072 | tf_op jit(solution)/shard_map/ppermute | solution.py:348
  35.9 15.1 %collective-permute-start.15 = (bf16[32,1792]{1,0:T(8,128)(2,1)S(1)}, bf16[32,1792]{1,0:T(8,128)(2,1)S(1)}, u32[]{:S(2)}, u32[]{:S(2)}) collective-permute-start(bf16[32,1792]{1,0:T(8,128)(2,1)S(1)} %get-tuple-element.113), channel_id=1, source_target_pairs={{0,8},{4,12},{8,0},{12,4},{16,24},{20,28},{24,16},{28,20},{1,9},{5... | collective-permute-start | bytes 344072 | tf_op jit(solution)/shard_map/ppermute | solution.py:348
  37.9 18.1 %collective-permute-start.23 = (bf16[128,1792]{1,0:T(8,128)(2,1)S(1)}, bf16[128,1792]{1,0:T(8,128)(2,1)S(1)}, u32[]{:S(2)}, u32[]{:S(2)}) collective-permute-start(bf16[128,1792]{1,0:T(8,128)(2,1)S(1)} %get-tuple-element.179), channel_id=1, source_target_pairs={{0,4},{4,0},{8,12},{12,8},{16,20},{20,16},{24,28},{28,24},{1,5},{5... | collective-permute-start | bytes 1376264 | tf_op jit(solution)/shard_map/ppermute | solution.py:348
  51.0 14.5 %collective-permute-start.25 = (bf16[32,1792]{1,0:T(8,128)(2,1)S(1)}, bf16[32,1792]{1,0:T(8,128)(2,1)S(1)}, u32[]{:S(2)}, u32[]{:S(2)}) collective-permute-start(bf16[32,1792]{1,0:T(8,128)(2,1)S(1)} %get-tuple-element.123), channel_id=1, source_target_pairs={{0,24},{4,28},{8,16},{12,20},{16,8},{20,12},{24,0},{28,4},{1,25},{... | collective-permute-start | bytes 344072 | tf_op jit(solution)/shard_map/ppermute | solution.py:348
  53.5 12.1 %collective-permute-start.24 = (bf16[32,1792]{1,0:T(8,128)(2,1)S(1)}, bf16[32,1792]{1,0:T(8,128)(2,1)S(1)}, u32[]{:S(2)}, u32[]{:S(2)}) collective-permute-start(bf16[32,1792]{1,0:T(8,128)(2,1)S(1)} %get-tuple-element.123), channel_id=1, source_target_pairs={{0,16},{4,20},{8,24},{12,28},{16,0},{20,4},{24,8},{28,12},{1,17},{... | collective-permute-start | bytes 344072 | tf_op jit(solution)/shard_map/ppermute | solution.py:348
  53.5 12.1 %collective-permute-start.22 = (bf16[32,1792]{1,0:T(8,128)(2,1)S(1)}, bf16[32,1792]{1,0:T(8,128)(2,1)S(1)}, u32[]{:S(2)}, u32[]{:S(2)}) collective-permute-start(bf16[32,1792]{1,0:T(8,128)(2,1)S(1)} %get-tuple-element.123), channel_id=1, source_target_pairs={{0,8},{4,12},{8,0},{12,4},{16,24},{20,28},{24,16},{28,20},{1,9},{5... | collective-permute-start | bytes 344072 | tf_op jit(solution)/shard_map/ppermute | solution.py:348
  55.5 11.7 %collective-permute-start.27 = (bf16[128,1792]{1,0:T(8,128)(2,1)S(1)}, bf16[128,1792]{1,0:T(8,128)(2,1)S(1)}, u32[]{:S(2)}, u32[]{:S(2)}) collective-permute-start(bf16[128,1792]{1,0:T(8,128)(2,1)S(1)} %get-tuple-element.163), channel_id=1, source_target_pairs={{0,4},{4,0},{8,12},{12,8},{16,20},{20,16},{24,28},{28,24},{1,5},{5... | collective-permute-start | bytes 1376264 | tf_op jit(solution)/shard_map/ppermute | solution.py:348
  65.7 11.1 %collective-permute-start.26 = (bf16[128,1792]{1,0:T(8,128)(2,1)S(1)}, bf16[128,1792]{1,0:T(8,128)(2,1)S(1)}, u32[]{:S(2)}, u32[]{:S(2)}) collective-permute-start(bf16[128,1792]{1,0:T(8,128)(2,1)S(1)} %get-tuple-element.170), channel_id=1, source_target_pairs={{0,4},{4,0},{8,12},{12,8},{16,20},{20,16},{24,28},{28,24},{1,5},{5... | collective-permute-start | bytes 1376264 | tf_op jit(solution)/shard_map/ppermute | solution.py:348
  86.3 1.3 collective-permute-start.28
  87.6 3.9 %collective-permute-start.29 = (f32[2,3584]{1,0:T(2,128)S(1)}, f32[2,3584]{1,0:T(2,128)S(1)}, u32[]{:S(2)}, u32[]{:S(2)}) collective-permute-start(f32[2,3584]{1,0:T(2,128)S(1)} %shard_map.68.refs_0_), channel_id=1, source_target_pairs={{0,2},{1,3},{2,0},{3,1},{4,6},{5,7},{6,4},{7,5},{8,10},{9,11},{10,... | collective-permute-start | bytes 86024 | tf_op jit(solution)/shard_map/ppermute | solution.py:348
  111.9 26.4 %collective-permute-start.34 = (f32[2,3584]{1,0:T(2,128)S(1)}, f32[2,3584]{1,0:T(2,128)S(1)}, u32[]{:S(2)}, u32[]{:S(2)}) collective-permute-start(f32[2,3584]{1,0:T(2,128)S(1)} %get-tuple-element.143.refs_0_), channel_id=1, source_target_pairs={{0,4},{4,0},{8,12},{12,8},{16,20},{20,16},{24,28},{28,24},{1,5},{5... | collective-permute-start | bytes 86024 | tf_op jit(solution)/shard_map/ppermute | solution.py:348
  136.7 6.1 %collective-permute-start.30 = (f32[2,3584]{1,0:T(2,128)S(1)}, f32[2,3584]{1,0:T(2,128)S(1)}, u32[]{:S(2)}, u32[]{:S(2)}) collective-permute-start(f32[2,3584]{1,0:T(2,128)S(1)} %get-tuple-element.139.refs_0_), channel_id=1, source_target_pairs={{0,4},{4,0},{8,12},{12,8},{16,20},{20,16},{24,28},{28,24},{1,5},{5... | collective-permute-start | bytes 86024 | tf_op jit(solution)/shard_map/ppermute | solution.py:348
  138.3 6.9 %collective-permute-start.37 = (f32[2,3584]{1,0:T(2,128)S(1)}, f32[2,3584]{1,0:T(2,128)S(1)}, u32[]{:S(2)}, u32[]{:S(2)}) collective-permute-start(f32[2,3584]{1,0:T(2,128)S(1)} %shard_map.74.refs_0_), channel_id=1, source_target_pairs={{0,24},{4,28},{8,16},{12,20},{16,8},{20,12},{24,0},{28,4},{1,25},{... | collective-permute-start | bytes 86024 | tf_op jit(solution)/shard_map/ppermute | solution.py:348
  140.8 6.5 %collective-permute-start.36 = (f32[2,3584]{1,0:T(2,128)S(1)}, f32[2,3584]{1,0:T(2,128)S(1)}, u32[]{:S(2)}, u32[]{:S(2)}) collective-permute-start(f32[2,3584]{1,0:T(2,128)S(1)} %shard_map.74.refs_0_), channel_id=1, source_target_pairs={{0,16},{4,20},{8,24},{12,28},{16,0},{20,4},{24,8},{28,12},{1,17},{... | collective-permute-start | bytes 86024 | tf_op jit(solution)/shard_map/ppermute | solution.py:348
  140.8 6.5 %collective-permute-start.35 = (f32[2,3584]{1,0:T(2,128)S(1)}, f32[2,3584]{1,0:T(2,128)S(1)}, u32[]{:S(2)}, u32[]{:S(2)}) collective-permute-start(f32[2,3584]{1,0:T(2,128)S(1)} %shard_map.74.refs_0_), channel_id=1, source_target_pairs={{0,8},{4,12},{8,0},{12,4},{16,24},{20,28},{24,16},{28,20},{1,9},{5... | collective-permute-start | bytes 86024 | tf_op jit(solution)/shard_map/ppermute | solution.py:348
  142.8 10.7 %collective-permute-start.33 = (f32[2,3584]{1,0:T(2,128)S(1)}, f32[2,3584]{1,0:T(2,128)S(1)}, u32[]{:S(2)}, u32[]{:S(2)}) collective-permute-start(f32[2,3584]{1,0:T(2,128)S(1)} %shard_map.71.refs_0_), channel_id=1, source_target_pairs={{0,24},{4,28},{8,16},{12,20},{16,8},{20,12},{24,0},{28,4},{1,25},{... | collective-permute-start | bytes 86024 | tf_op jit(solution)/shard_map/ppermute | solution.py:348
  145.2 8.2 %collective-permute-start.32 = (f32[2,3584]{1,0:T(2,128)S(1)}, f32[2,3584]{1,0:T(2,128)S(1)}, u32[]{:S(2)}, u32[]{:S(2)}) collective-permute-start(f32[2,3584]{1,0:T(2,128)S(1)} %shard_map.71.refs_0_), channel_id=1, source_target_pairs={{0,16},{4,20},{8,24},{12,28},{16,0},{20,4},{24,8},{28,12},{1,17},{... | collective-permute-start | bytes 86024 | tf_op jit(solution)/shard_map/ppermute | solution.py:348
  145.2 8.2 %collective-permute-start.31 = (f32[2,3584]{1,0:T(2,128)S(1)}, f32[2,3584]{1,0:T(2,128)S(1)}, u32[]{:S(2)}, u32[]{:S(2)}) collective-permute-start(f32[2,3584]{1,0:T(2,128)S(1)} %shard_map.71.refs_0_), channel_id=1, source_target_pairs={{0,8},{4,12},{8,0},{12,4},{16,24},{20,28},{24,16},{28,20},{1,9},{5... | collective-permute-start | bytes 86024 | tf_op jit(solution)/shard_map/ppermute | solution.py:348
  147.3 8.3 %copy-start = (bf16[3584,3584]{1,0:T(8,128)(2,1)S(1)}, bf16[3584,3584]{1,0:T(8,128)(2,1)}, u32[]{:S(2)}) copy-start(bf16[3584,3584]{1,0:T(8,128)(2,1)} %get-tuple-element.137.kept_ref) | copy-start | bytes 77070336
  161.8 1.2 collective-permute-start.38
  163.0 3.7 %collective-permute-start.39 = (f32[1,3584]{1,0:T(1,128)S(1)}, f32[1,3584]{1,0:T(1,128)S(1)}, u32[]{:S(2)}, u32[]{:S(2)}) collective-permute-start(f32[1,3584]{1,0:T(1,128)S(1)} %shard_map.78.refs_0_), channel_id=1, source_target_pairs={{0,2},{1,3},{2,0},{3,1},{4,6},{5,7},{6,4},{7,5},{8,10},{9,11},{10,... | collective-permute-start | bytes 43016 | tf_op jit(solution)/shard_map/ppermute | solution.py:348
  172.8 8.4 %collective-permute-start.40 = (f32[1,3712]{1,0:T(1,128)S(1)}, f32[1,3712]{1,0:T(1,128)S(1)}, u32[]{:S(2)}, u32[]{:S(2)}) collective-permute-start(f32[1,3712]{1,0:T(1,128)S(1)} %shard_map.80.refs_0_), channel_id=1, source_target_pairs={{0,4},{4,0},{8,12},{12,8},{16,20},{20,16},{24,28},{28,24},{1,5},{5... | collective-permute-start | bytes 44552 | tf_op jit(solution)/shard_map/ppermute | solution.py:348
  179.7 6.0 %collective-permute-start.44 = (f32[1,3712]{1,0:T(1,128)S(1)}, f32[1,3712]{1,0:T(1,128)S(1)}, u32[]{:S(2)}, u32[]{:S(2)}) collective-permute-start(f32[1,3712]{1,0:T(1,128)S(1)} %shard_map.83.refs_0_), channel_id=1, source_target_pairs={{0,4},{4,0},{8,12},{12,8},{16,20},{20,16},{24,28},{28,24},{1,5},{5... | collective-permute-start | bytes 44552 | tf_op jit(solution)/shard_map/ppermute | solution.py:348
  181.3 6.9 %collective-permute-start.43 = (f32[1,3712]{1,0:T(1,128)S(1)}, f32[1,3712]{1,0:T(1,128)S(1)}, u32[]{:S(2)}, u32[]{:S(2)}) collective-permute-start(f32[1,3712]{1,0:T(1,128)S(1)} %shard_map.81.refs_0_), channel_id=1, source_target_pairs={{0,24},{4,28},{8,16},{12,20},{16,8},{20,12},{24,0},{28,4},{1,25},{... | collective-permute-start | bytes 44552 | tf_op jit(solution)/shard_map/ppermute | solution.py:348
  183.7 6.5 %collective-permute-start.42 = (f32[1,3712]{1,0:T(1,128)S(1)}, f32[1,3712]{1,0:T(1,128)S(1)}, u32[]{:S(2)}, u32[]{:S(2)}) collective-permute-start(f32[1,3712]{1,0:T(1,128)S(1)} %shard_map.81.refs_0_), channel_id=1, source_target_pairs={{0,16},{4,20},{8,24},{12,28},{16,0},{20,4},{24,8},{28,12},{1,17},{... | collective-permute-start | bytes 44552 | tf_op jit(solution)/shard_map/ppermute | solution.py:348
  183.7 6.5 %collective-permute-start.41 = (f32[1,3712]{1,0:T(1,128)S(1)}, f32[1,3712]{1,0:T(1,128)S(1)}, u32[]{:S(2)}, u32[]{:S(2)}) collective-permute-start(f32[1,3712]{1,0:T(1,128)S(1)} %shard_map.81.refs_0_), channel_id=1, source_target_pairs={{0,8},{4,12},{8,0},{12,4},{16,24},{20,28},{24,16},{28,20},{1,9},{5... | collective-permute-start | bytes 44552 | tf_op jit(solution)/shard_map/ppermute | solution.py:348
  185.7 5.6 %collective-permute-start.47 = (f32[1,3712]{1,0:T(1,128)S(1)}, f32[1,3712]{1,0:T(1,128)S(1)}, u32[]{:S(2)}, u32[]{:S(2)}) collective-permute-start(f32[1,3712]{1,0:T(1,128)S(1)} %shard_map.84.refs_0_), channel_id=1, source_target_pairs={{0,24},{4,28},{8,16},{12,20},{16,8},{20,12},{24,0},{28,4},{1,25},{... | collective-permute-start | bytes 44552 | tf_op jit(solution)/shard_map/ppermute | solution.py:348
  188.2 4.6 %collective-permute-start.46 = (f32[1,3712]{1,0:T(1,128)S(1)}, f32[1,3712]{1,0:T(1,128)S(1)}, u32[]{:S(2)}, u32[]{:S(2)}) collective-permute-start(f32[1,3712]{1,0:T(1,128)S(1)} %shard_map.84.refs_0_), channel_id=1, source_target_pairs={{0,16},{4,20},{8,24},{12,28},{16,0},{20,4},{24,8},{28,12},{1,17},{... | collective-permute-start | bytes 44552 | tf_op jit(solution)/shard_map/ppermute | solution.py:348
  188.2 4.6 %collective-permute-start.45 = (f32[1,3712]{1,0:T(1,128)S(1)}, f32[1,3712]{1,0:T(1,128)S(1)}, u32[]{:S(2)}, u32[]{:S(2)}) collective-permute-start(f32[1,3712]{1,0:T(1,128)S(1)} %shard_map.84.refs_0_), channel_id=1, source_target_pairs={{0,8},{4,12},{8,0},{12,4},{16,24},{20,28},{24,16},{28,20},{1,9},{5... | collective-permute-start | bytes 44552 | tf_op jit(solution)/shard_map/ppermute | solution.py:348

commit v6 on v5

--- a/solution.py
+++ b/solution.py
@@ -43,7 +43,7 @@
     sub = 64 if keep or tm % 128 else 128
     lanes = tn // 128
 
-    @pl.loop(0, lhs_ref.shape[1] // 128)
+    @pl.loop(0, lhs_ref.shape[1] // 128, unroll=7)
     def _(g):
         rows = pl.ds(pl.multiple_of(g * 128, 128), 128)
         turned[rows, :] = lhs_ref[:, rows].T
@@ -182,7 +182,7 @@
         start = pl.multiple_of(table_ref[p] * tokens, tokens)
         out_ref[p * tokens : (p + 1) * tokens, :] = arrived_ref[pl.ds(start, tokens), :]
 
-    @pl.loop(0, arrived_ref.shape[1] // 128)
+    @pl.loop(0, arrived_ref.shape[1] // 128, unroll=7)
     def _(g):
         cols = pl.ds(pl.multiple_of(g * 128, 128), 128)
         norm_ref[:, cols] = jnp.sum(jnp.square(arrived_ref[:, cols].astype(f32)), 0, keepdims=True)
@@ -218,7 +218,7 @@
     def _(t):
         wide[...] = jnp.broadcast_to(weights(tile_max_ref, lse_ref, t), (16, cols_here)).astype(bf16)
 
-        @pl.loop(0, tm // height)
+        @pl.loop(0, tm // height, unroll=2 if tm % (2 * height) == 0 else 1)
         def _(g):
             rows = pl.ds(pl.multiple_of(t * tm + g * height, height), height)
             acc = jnp.zeros((height, 128), f32)
@@ -233,7 +233,7 @@
                     acc = acc + part[:, k : k + 128]
             partial[rows, :] = acc
 
-    @pl.loop(0, rows_here // 128)
+    @pl.loop(0, rows_here // 128, unroll=7)
     def _(g):
         rows = pl.ds(pl.multiple_of(g * 128, 128), 128)
         total = jnp.sum(partial[rows, :].T, axis=0, keepdims=True)
@@ -260,7 +260,7 @@
     tm = rows_here // tiles
     width = 896
 
-    @pl.loop(0, rows_here // 128)
+    @pl.loop(0, rows_here // 128, unroll=7)
     def _(g):
         rows = pl.ds(pl.multiple_of(g * 128, 128), 128)
         scale = 1.0 / jnp.maximum(row_sum_ref[:, rows], SMALLEST)

time: 194 us -> 179 us (0.923)
  Pallas kernels: 109 us -> 90.2 us
  local copies, waits for them, and re-layouts: 5.46 us -> 7.92 us
    pallas_call x6, Pallas kernels: 82.4 us -> 74.2 us  [lse_call(): pl.pallas_call(functools.partial(lse_kernel, tm, tn, bias is not None, st...]
    pallas_call x2, Pallas kernels: 12.3 us -> 7.26 us  [col_sum_call(): pl.pallas_call(col_sum_kernel, out_shape=jax.ShapeDtypeStruct((1, n + 128...]
    pallas_call x2, Pallas kernels: 12.3 us -> 7.38 us  [row_sum_call(): pl.pallas_call(functools.partial(row_sum_kernel, first is not None), out_...]
    unnamed x19, local copies, waits for them, and re-layouts: 2.31 us -> 4.78 us
  transfers between devices with their start and end apart: 38 -> 38, of which waited for: 8 -> 10; matrix products, arithmetic and copies ran while one was open for 2% -> 2% of each run, Pallas kernels for 34% -> 31%
where the time goes in v6:
time: 179 us
  Pallas kernels  90.2 us (50%)
  starting transfers between devices  51.5 us (29%)
  waiting for transfers between devices  24.5 us (14%)
  local copies, waits for them, and re-layouts  7.92 us (4%)
  other arithmetic  3.18 us (2%)
    pallas_call x6, Pallas kernels, lse_call(): pl.pallas_call(functools.partial(lse_kernel, tm, tn, bias is not None, st...  74.2 us
    ppermute x38, starting transfers between devices, swap(): return lax.ppermute(x, axis, [(i, i ^ mask) for i in range(size)])  51.5 us
    ppermute x38, waiting for transfers between devices, swap(): return lax.ppermute(x, axis, [(i, i ^ mask) for i in range(size)])  24.5 us
    pallas_call x2, Pallas kernels, row_sum_call(): pl.pallas_call(functools.partial(row_sum_kernel, first is not None), out_...  7.38 us
    pallas_call x2, Pallas kernels, col_sum_call(): pl.pallas_call(col_sum_kernel, out_shape=jax.ShapeDtypeStruct((1, n + 128...  7.26 us
    unnamed x19, local copies, waits for them, and re-layouts  4.78 us
  transfers between devices with their start and end apart: 38, of which 10 were waited for; matrix products, arithmetic and copies ran while one was open for 2% of the time, Pallas kernels for 31%

profile of v6, /device:TPU:0, one launch (start us, length us, event | category | flops | bytes accessed | tf_op | source)
XLA Modules:
  0.0 179.0 jit_solution(13438551603573525188)
XLA Ops:
  0.6 1.2 fusion.7
  1.8 5.1 %collective-permute-start.18 = (bf16[32,1792]{1,0:T(8,128)(2,1)S(1)}, bf16[32,1792]{1,0:T(8,128)(2,1)S(1)}, u32[]{:S(2)}, u32[]{:S(2)}) collective-permute-start(bf16[32,1792]{1,0:T(8,128)(2,1)S(1)} %get-tuple-element.157), channel_id=1, source_target_pairs={{0,24},{4,28},{8,16},{12,20},{16,8},{20,12},{24,0},{28,4},{1,25},{... | collective-permute-start | bytes 344072 | tf_op jit(solution)/shard_map/ppermute | solution.py:348
  7.6 1.7 collective-permute-start.10
  9.9 1.3 gather_fusion
  11.9 7.6 %collective-permute-done.10 = bf16[64,3584]{1,0:T(8,128)(2,1)S(1)} collective-permute-done((bf16[64,3584]{1,0:T(8,128)(2,1)}, bf16[64,3584]{1,0:T(8,128)(2,1)S(1)}, u32[]{:S(2)}, u32[]{:S(2)}) %collective-permute-start.10) | collective-permute-done | bytes 458784 | tf_op jit(solution)/shard_map/ppermute | solution.py:348
  19.6 3.5 %collective-permute-start.14 = (bf16[32,1792]{1,0:T(8,128)(2,1)S(1)}, bf16[32,1792]{1,0:T(8,128)(2,1)S(1)}, u32[]{:S(2)}, u32[]{:S(2)}) collective-permute-start(bf16[32,1792]{1,0:T(8,128)(2,1)S(1)} %get-tuple-element.109), channel_id=1, source_target_pairs={{0,24},{4,28},{8,16},{12,20},{16,8},{20,12},{24,0},{28,4},{1,25},{... | collective-permute-start | bytes 344072 | tf_op jit(solution)/shard_map/ppermute | solution.py:348
  23.2 0.9 collective-permute-start.12
  24.2 1.6 collective-permute-start.19
  25.8 1.7 collective-permute-done.14
  27.5 5.8 %collective-permute-done.13 = bf16[32,1792]{1,0:T(8,128)(2,1)S(1)} collective-permute-done((bf16[32,1792]{1,0:T(8,128)(2,1)S(1)}, bf16[32,1792]{1,0:T(8,128)(2,1)S(1)}, u32[]{:S(2)}, u32[]{:S(2)}) %collective-permute-start.13) | collective-permute-done | bytes 114720 | tf_op jit(solution)/shard_map/ppermute | solution.py:348
  33.4 2.4 %collective-permute-start.21 = (bf16[32,1792]{1,0:T(8,128)(2,1)S(1)}, bf16[32,1792]{1,0:T(8,128)(2,1)S(1)}, u32[]{:S(2)}, u32[]{:S(2)}) collective-permute-start(bf16[32,1792]{1,0:T(8,128)(2,1)S(1)} %get-tuple-element.113), channel_id=1, source_target_pairs={{0,24},{4,28},{8,16},{12,20},{16,8},{20,12},{24,0},{28,4},{1,25},{... | collective-permute-start | bytes 344072 | tf_op jit(solution)/shard_map/ppermute | solution.py:348
  35.9 2.0 %collective-permute-start.15 = (bf16[32,1792]{1,0:T(8,128)(2,1)S(1)}, bf16[32,1792]{1,0:T(8,128)(2,1)S(1)}, u32[]{:S(2)}, u32[]{:S(2)}) collective-permute-start(bf16[32,1792]{1,0:T(8,128)(2,1)S(1)} %get-tuple-element.113), channel_id=1, source_target_pairs={{0,8},{4,12},{8,0},{12,4},{16,24},{20,28},{24,16},{28,20},{1,9},{5... | collective-permute-start | bytes 344072 | tf_op jit(solution)/shard_map/ppermute | solution.py:348
  37.9 1.6 collective-permute-start.23
  39.6 1.1 shard_map.63
  40.8 8.2 %shard_map.64 = (f32[2,3584]{1,0:T(2,128)S(1)}, f32[1,1792]{1,0:T(1,128)S(1)}) custom-call(bf16[256,1792]{1,0:T(8,128)(2,1)S(1)} %constant_dynamic-update-slice_fusion.6.lhs_ref, bf16[256,3584]{1,0:T(8,128)(2,1)S(1)} %get-tuple-element.108.rhs_ref.lhs_ref), custom_call_target="tpu_custom_call" | custom-call | flops 3288334336 | bytes 2752512 | tf_op jit(solution)/shard_map/pallas_call | solution.py:167
  49.0 2.4 %collective-permute-start.25 = (bf16[32,1792]{1,0:T(8,128)(2,1)S(1)}, bf16[32,1792]{1,0:T(8,128)(2,1)S(1)}, u32[]{:S(2)}, u32[]{:S(2)}) collective-permute-start(bf16[32,1792]{1,0:T(8,128)(2,1)S(1)} %get-tuple-element.123), channel_id=1, source_target_pairs={{0,24},{4,28},{8,16},{12,20},{16,8},{20,12},{24,0},{28,4},{1,25},{... | collective-permute-start | bytes 344072 | tf_op jit(solution)/shard_map/ppermute | solution.py:348
  51.5 2.0 %collective-permute-start.22 = (bf16[32,1792]{1,0:T(8,128)(2,1)S(1)}, bf16[32,1792]{1,0:T(8,128)(2,1)S(1)}, u32[]{:S(2)}, u32[]{:S(2)}) collective-permute-start(bf16[32,1792]{1,0:T(8,128)(2,1)S(1)} %get-tuple-element.123), channel_id=1, source_target_pairs={{0,8},{4,12},{8,0},{12,4},{16,24},{20,28},{24,16},{28,20},{1,9},{5... | collective-permute-start | bytes 344072 | tf_op jit(solution)/shard_map/ppermute | solution.py:348
  54.1 8.2 %shard_map.65 = (f32[2,3584]{1,0:T(2,128)S(1)}, f32[1,1792]{1,0:T(1,128)S(1)}) custom-call(bf16[256,1792]{1,0:T(8,128)(2,1)S(1)} %constant_dynamic-update-slice_fusion.15.lhs_ref, bf16[256,3584]{1,0:T(8,128)(2,1)S(1)} %get-tuple-element.108.rhs_ref.lhs_ref, f32[2,3584]{1,0:T(2,128)S(1)} %get-tuple-element.119.rest_0_), custom_call_target="tpu_custom_call" | custom-call | flops 3288334336 | bytes 2752512 | tf_op jit(solution)/shard_map/pallas_call | solution.py:167
  62.4 1.6 collective-permute-start.26
  64.0 0.7 collective-permute-done.27
  64.7 8.2 %shard_map.66 = (f32[2,3584]{1,0:T(2,128)S(1)}, f32[1,1792]{1,0:T(1,128)S(1)}) custom-call(bf16[256,1792]{1,0:T(8,128)(2,1)S(1)} %constant_dynamic-update-slice_fusion.24.lhs_ref, bf16[256,3584]{1,0:T(8,128)(2,1)S(1)} %get-tuple-element.108.rhs_ref.lhs_ref, f32[2,3584]{1,0:T(2,128)S(1)} %get-tuple-element.126.rest_0_), custom_call_target="tpu_custom_call" | custom-call | flops 3288334336 | bytes 2752512 | tf_op jit(solution)/shard_map/pallas_call | solution.py:167
  73.5 8.2 %shard_map.67 = (f32[2,3584]{1,0:T(2,128)S(1)}, f32[1,1792]{1,0:T(1,128)S(1)}) custom-call(bf16[256,1792]{1,0:T(8,128)(2,1)S(1)} %constant_dynamic-update-slice_fusion.29.lhs_ref, bf16[256,3584]{1,0:T(8,128)(2,1)S(1)} %get-tuple-element.108.rhs_ref.lhs_ref, f32[2,3584]{1,0:T(2,128)S(1)} %get-tuple-element.132.rest_0_), custom_call_target="tpu_custom_call" | custom-call | flops 3288334336 | bytes 2752512 | tf_op jit(solution)/shard_map/pallas_call | solution.py:167
  81.9 1.1 collective-permute-done.28.refs_1_
  83.0 1.6 collective-permute-start.29
  84.7 2.2 %collective-permute-done.29.refs_1_ = f32[2,3584]{1,0:T(2,128)S(1)} collective-permute-done((f32[2,3584]{1,0:T(2,128)S(1)}, f32[2,3584]{1,0:T(2,128)S(1)}, u32[]{:S(2)}, u32[]{:S(2)}) %collective-permute-start.29) | collective-permute-done | bytes 28704 | tf_op jit(solution)/shard_map/ppermute | solution.py:348
  87.0 18.8 %shard_map.73 = (f32[2,3584]{1,0:T(2,128)S(1)}, f32[4,3584]{1,0:T(4,128)S(1)}, bf16[3584,3584]{1,0:T(8,128)(2,1)S(1)}) custom-call(bf16[256,3584]{1,0:T(8,128)(2,1)S(1)} %get-tuple-element.108.rhs_ref.lhs_ref, bf16[256,3584]{1,0:T(8,128)(2,1)S(1)} %pad_maximum_fusion.3.rhs_ref, f32[1,3584]{1,0:T(1,128)S(1)} %broadcast_multiply_fusion.3.rest_0_), custom_call_target="tpu_custom_call" | custom-call | flops 6576668672 | bytes 3670016 | tf_op jit(solution)/shard_map/pallas_call | solution.py:167
  106.4 22.6 %shard_map.70 = (f32[2,3584]{1,0:T(2,128)S(1)}, f32[4,3584]{1,0:T(4,128)S(1)}, bf16[3584,3584]{1,0:T(8,128)(2,1)}) custom-call(bf16[256,3584]{1,0:T(8,128)(2,1)S(1)} %get-tuple-element.108.rhs_ref.lhs_ref, bf16[256,3584]{1,0:T(8,128)(2,1)S(1)} %pad_maximum_fusion.4.rhs_ref, f32[1,3584]{1,0:T(1,128)S(1)} %broadcast_multiply_fusion.3.rest_0_), custom_call_target="tpu_custom_call" | custom-call | flops 6576668672 | bytes 3670016 | tf_op jit(solution)/shard_map/pallas_call | solution.py:167
  129.0 1.6 collective-permute-start.30
  130.6 2.4 %collective-permute-start.37 = (f32[2,3584]{1,0:T(2,128)S(1)}, f32[2,3584]{1,0:T(2,128)S(1)}, u32[]{:S(2)}, u32[]{:S(2)}) collective-permute-start(f32[2,3584]{1,0:T(2,128)S(1)} %shard_map.74.refs_0_), channel_id=1, source_target_pairs={{0,24},{4,28},{8,16},{12,20},{16,8},{20,12},{24,0},{28,4},{1,25},{... | collective-permute-start | bytes 86024 | tf_op jit(solution)/shard_map/ppermute | solution.py:348
  133.0 2.0 %collective-permute-start.35 = (f32[2,3584]{1,0:T(2,128)S(1)}, f32[2,3584]{1,0:T(2,128)S(1)}, u32[]{:S(2)}, u32[]{:S(2)}) collective-permute-start(f32[2,3584]{1,0:T(2,128)S(1)} %shard_map.74.refs_0_), channel_id=1, source_target_pairs={{0,8},{4,12},{8,0},{12,4},{16,24},{20,28},{24,16},{28,20},{1,9},{5... | collective-permute-start | bytes 86024 | tf_op jit(solution)/shard_map/ppermute | solution.py:348
  135.1 2.4 %collective-permute-start.33 = (f32[2,3584]{1,0:T(2,128)S(1)}, f32[2,3584]{1,0:T(2,128)S(1)}, u32[]{:S(2)}, u32[]{:S(2)}) collective-permute-start(f32[2,3584]{1,0:T(2,128)S(1)} %shard_map.71.refs_0_), channel_id=1, source_target_pairs={{0,24},{4,28},{8,16},{12,20},{16,8},{20,12},{24,0},{28,4},{1,25},{... | collective-permute-start | bytes 86024 | tf_op jit(solution)/shard_map/ppermute | solution.py:348
  137.5 2.0 %collective-permute-start.31 = (f32[2,3584]{1,0:T(2,128)S(1)}, f32[2,3584]{1,0:T(2,128)S(1)}, u32[]{:S(2)}, u32[]{:S(2)}) collective-permute-start(f32[2,3584]{1,0:T(2,128)S(1)} %shard_map.71.refs_0_), channel_id=1, source_target_pairs={{0,8},{4,12},{8,0},{12,4},{16,24},{20,28},{24,16},{28,20},{1,9},{5... | collective-permute-start | bytes 86024 | tf_op jit(solution)/shard_map/ppermute | solution.py:348
  139.6 3.7 %shard_map.76.rest_0_ = f32[1,3584]{1,0:T(1,128)S(1)} custom-call(bf16[3584,3584]{1,0:T(8,128)(2,1)S(1)} %get-tuple-element.141.kept_ref, f32[4,3584]{1,0:T(4,128)S(1)} %get-tuple-element.142.tile_max_ref, f32[1,3584]{1,0:T(1,128)S(1)} %shard_map.75.lse_ref), custom_call_target="tpu_custom_call" | custom-call | flops 25690112 | bytes 25690112 | tf_op jit(solution)/shard_map/pallas_call | solution.py:246
  143.4 4.5 %copy-done = bf16[3584,3584]{1,0:T(8,128)(2,1)S(1)} copy-done((bf16[3584,3584]{1,0:T(8,128)(2,1)S(1)}, bf16[3584,3584]{1,0:T(8,128)(2,1)}, u32[]{:S(2)}) %copy-start) | copy-done | bytes 25690136
  147.9 3.7 %shard_map.77.refs_0_ = f32[1,3584]{1,0:T(1,128)S(1)} custom-call(bf16[3584,3584]{1,0:T(8,128)(2,1)S(1)} %copy-done, f32[4,3584]{1,0:T(4,128)S(1)} %get-tuple-element.138.tile_max_ref, f32[1,3584]{1,0:T(1,128)S(1)} %shard_map.72.lse_ref, f32[1,3584]{1,0:T(1,128)S(1)} %shard_map.76.rest_0_), custom_call_target="tpu_custom_call" | custom-call | flops 25690112 | bytes 25690112 | tf_op jit(solution)/shard_map/pallas_call | solution.py:246
  151.7 1.2 collective-permute-done.38.refs_1_
  152.9 1.5 collective-permute-start.39
  154.4 2.2 %collective-permute-done.39.refs_1_ = f32[1,3584]{1,0:T(1,128)S(1)} collective-permute-done((f32[1,3584]{1,0:T(1,128)S(1)}, f32[1,3584]{1,0:T(1,128)S(1)}, u32[]{:S(2)}, u32[]{:S(2)}) %collective-permute-start.39) | collective-permute-done | bytes 14368 | tf_op jit(solution)/shard_map/ppermute | solution.py:348
  156.6 3.6 %shard_map.80.refs_0_ = f32[1,3712]{1,0:T(1,128)S(1)} custom-call(bf16[3584,3584]{1,0:T(8,128)(2,1)S(1)} %copy-done, f32[4,3584]{1,0:T(4,128)S(1)} %get-tuple-element.138.tile_max_ref, f32[1,3584]{1,0:T(1,128)S(1)} %shard_map.72.lse_ref, f32[1,3584]{1,0:T(1,128)S(1)} %shard_map.79.row_sum_ref), custom_call_target="tpu_custom_call" | custom-call | flops 25690112 | bytes 25690112 | tf_op jit(solution)/shard_map/pallas_call | solution.py:295
  160.8 3.6 %shard_map.83.refs_0_ = f32[1,3712]{1,0:T(1,128)S(1)} custom-call(bf16[3584,3584]{1,0:T(8,128)(2,1)S(1)} %get-tuple-element.141.kept_ref, f32[4,3584]{1,0:T(4,128)S(1)} %get-tuple-element.142.tile_max_ref, f32[1,3584]{1,0:T(1,128)S(1)} %shard_map.75.lse_ref, f32[1,3584]{1,0:T(1,128)S(1)} %shard_map.79.row_sum_ref), custom_call_target="tpu_custom_call" | custom-call | flops 25690112 | bytes 25690112 | tf_op jit(solution)/shard_map/pallas_call | solution.py:295
  164.4 1.6 collective-permute-start.44
  166.0 2.4 %collective-permute-start.43 = (f32[1,3712]{1,0:T(1,128)S(1)}, f32[1,3712]{1,0:T(1,128)S(1)}, u32[]{:S(2)}, u32[]{:S(2)}) collective-permute-start(f32[1,3712]{1,0:T(1,128)S(1)} %shard_map.81.refs_0_), channel_id=1, source_target_pairs={{0,24},{4,28},{8,16},{12,20},{16,8},{20,12},{24,0},{28,4},{1,25},{... | collective-permute-start | bytes 44552 | tf_op jit(solution)/shard_map/ppermute | solution.py:348
  168.4 2.0 %collective-permute-start.41 = (f32[1,3712]{1,0:T(1,128)S(1)}, f32[1,3712]{1,0:T(1,128)S(1)}, u32[]{:S(2)}, u32[]{:S(2)}) collective-permute-start(f32[1,3712]{1,0:T(1,128)S(1)} %shard_map.81.refs_0_), channel_id=1, source_target_pairs={{0,8},{4,12},{8,0},{12,4},{16,24},{20,28},{24,16},{28,20},{1,9},{5... | collective-permute-start | bytes 44552 | tf_op jit(solution)/shard_map/ppermute | solution.py:348
  170.5 2.4 %collective-permute-start.47 = (f32[1,3712]{1,0:T(1,128)S(1)}, f32[1,3712]{1,0:T(1,128)S(1)}, u32[]{:S(2)}, u32[]{:S(2)}) collective-permute-start(f32[1,3712]{1,0:T(1,128)S(1)} %shard_map.84.refs_0_), channel_id=1, source_target_pairs={{0,24},{4,28},{8,16},{12,20},{16,8},{20,12},{24,0},{28,4},{1,25},{... | collective-permute-start | bytes 44552 | tf_op jit(solution)/shard_map/ppermute | solution.py:348
  172.9 2.0 %collective-permute-start.45 = (f32[1,3712]{1,0:T(1,128)S(1)}, f32[1,3712]{1,0:T(1,128)S(1)}, u32[]{:S(2)}, u32[]{:S(2)}) collective-permute-start(f32[1,3712]{1,0:T(1,128)S(1)} %shard_map.84.refs_0_), channel_id=1, source_target_pairs={{0,8},{4,12},{8,0},{12,4},{16,24},{20,28},{24,16},{28,20},{1,9},{5... | collective-permute-start | bytes 44552 | tf_op jit(solution)/shard_map/ppermute | solution.py:348
  176.1 1.4 collective-permute-done.46.refs_2_
  177.5 1.4 conditional.1
  177.6 0.7 subtract_reduce_fusion
  (91 shorter events, 6.9 us)
Async XLA Ops:
  0.6 11.3 %copy-start.1 = (bf16[64,3584]{1,0:T(8,128)(2,1)S(1)}, bf16[64,3584]{1,0:T(8,128)(2,1)}, u32[]{:S(2)}) copy-start(bf16[64,3584]{1,0:T(8,128)(2,1)} %param.6) | copy-start | bytes 1376260
  1.8 21.3 %collective-permute-start.18 = (bf16[32,1792]{1,0:T(8,128)(2,1)S(1)}, bf16[32,1792]{1,0:T(8,128)(2,1)S(1)}, u32[]{:S(2)}, u32[]{:S(2)}) collective-permute-start(bf16[32,1792]{1,0:T(8,128)(2,1)S(1)} %get-tuple-element.157), channel_id=1, source_target_pairs={{0,24},{4,28},{8,16},{12,20},{16,8},{20,12},{24,0},{28,4},{1,25},{... | collective-permute-start | bytes 344072 | tf_op jit(solution)/shard_map/ppermute | solution.py:348
  6.9 16.3 %collective-permute-start.17 = (bf16[32,1792]{1,0:T(8,128)(2,1)S(1)}, bf16[32,1792]{1,0:T(8,128)(2,1)S(1)}, u32[]{:S(2)}, u32[]{:S(2)}) collective-permute-start(bf16[32,1792]{1,0:T(8,128)(2,1)S(1)} %get-tuple-element.157), channel_id=1, source_target_pairs={{0,16},{4,20},{8,24},{12,28},{16,0},{20,4},{24,8},{28,12},{1,17},{... | collective-permute-start | bytes 344072 | tf_op jit(solution)/shard_map/ppermute | solution.py:348
  6.9 17.2 %collective-permute-start.16 = (bf16[32,1792]{1,0:T(8,128)(2,1)S(1)}, bf16[32,1792]{1,0:T(8,128)(2,1)S(1)}, u32[]{:S(2)}, u32[]{:S(2)}) collective-permute-start(bf16[32,1792]{1,0:T(8,128)(2,1)S(1)} %get-tuple-element.157), channel_id=1, source_target_pairs={{0,8},{4,12},{8,0},{12,4},{16,24},{20,28},{24,16},{28,20},{1,9},{5... | collective-permute-start | bytes 344072 | tf_op jit(solution)/shard_map/ppermute | solution.py:348
  7.6 11.9 %collective-permute-start.10 = (bf16[64,3584]{1,0:T(8,128)(2,1)}, bf16[64,3584]{1,0:T(8,128)(2,1)S(1)}, u32[]{:S(2)}, u32[]{:S(2)}) collective-permute-start(bf16[64,3584]{1,0:T(8,128)(2,1)} %param.6), channel_id=1, source_target_pairs={{0,2},{1,3},{2,0},{3,1},{4,6},{5,7},{6,4},{7,5},{8,10},{9,11},{10,... | collective-permute-start | bytes 1376264 | tf_op jit(solution)/shard_map/ppermute | solution.py:348
  19.5 18.4 %collective-permute-start.11 = (bf16[128,3584]{1,0:T(8,128)(2,1)S(1)}, bf16[128,3584]{1,0:T(8,128)(2,1)S(1)}, u32[]{:S(2)}, u32[]{:S(2)}) collective-permute-start(bf16[128,3584]{1,0:T(8,128)(2,1)S(1)} %constant_dynamic-update-slice_fusion), channel_id=1, source_target_pairs={{0,1},{1,0},{2,3},{3,2},{4,5},{5,4},{6,7},{7,6},{8,9},{9,8},{10,11... | collective-permute-start | bytes 2752520 | tf_op jit(solution)/shard_map/ppermute | solution.py:348
  19.6 7.9 %collective-permute-start.14 = (bf16[32,1792]{1,0:T(8,128)(2,1)S(1)}, bf16[32,1792]{1,0:T(8,128)(2,1)S(1)}, u32[]{:S(2)}, u32[]{:S(2)}) collective-permute-start(bf16[32,1792]{1,0:T(8,128)(2,1)S(1)} %get-tuple-element.109), channel_id=1, source_target_pairs={{0,24},{4,28},{8,16},{12,20},{16,8},{20,12},{24,0},{28,4},{1,25},{... | collective-permute-start | bytes 344072 | tf_op jit(solution)/shard_map/ppermute | solution.py:348
  23.1 10.2 %collective-permute-start.13 = (bf16[32,1792]{1,0:T(8,128)(2,1)S(1)}, bf16[32,1792]{1,0:T(8,128)(2,1)S(1)}, u32[]{:S(2)}, u32[]{:S(2)}) collective-permute-start(bf16[32,1792]{1,0:T(8,128)(2,1)S(1)} %get-tuple-element.109), channel_id=1, source_target_pairs={{0,16},{4,20},{8,24},{12,28},{16,0},{20,4},{24,8},{28,12},{1,17},{... | collective-permute-start | bytes 344072 | tf_op jit(solution)/shard_map/ppermute | solution.py:348
  23.2 10.1 %collective-permute-start.12 = (bf16[32,1792]{1,0:T(8,128)(2,1)S(1)}, bf16[32,1792]{1,0:T(8,128)(2,1)S(1)}, u32[]{:S(2)}, u32[]{:S(2)}) collective-permute-start(bf16[32,1792]{1,0:T(8,128)(2,1)S(1)} %get-tuple-element.109), channel_id=1, source_target_pairs={{0,8},{4,12},{8,0},{12,4},{16,24},{20,28},{24,16},{28,20},{1,9},{5... | collective-permute-start | bytes 344072 | tf_op jit(solution)/shard_map/ppermute | solution.py:348
  24.2 16.5 %collective-permute-start.19 = (bf16[128,1792]{1,0:T(8,128)(2,1)S(1)}, bf16[128,1792]{1,0:T(8,128)(2,1)S(1)}, u32[]{:S(2)}, u32[]{:S(2)}) collective-permute-start(bf16[128,1792]{1,0:T(8,128)(2,1)S(1)} %pad_maximum_fusion.5), channel_id=1, source_target_pairs={{0,4},{4,0},{8,12},{12,8},{16,20},{20,16},{24,28},{28,24},{1,5},{5... | collective-permute-start | bytes 1376264 | tf_op jit(solution)/shard_map/ppermute | solution.py:348
  33.4 15.5 %collective-permute-start.21 = (bf16[32,1792]{1,0:T(8,128)(2,1)S(1)}, bf16[32,1792]{1,0:T(8,128)(2,1)S(1)}, u32[]{:S(2)}, u32[]{:S(2)}) collective-permute-start(bf16[32,1792]{1,0:T(8,128)(2,1)S(1)} %get-tuple-element.113), channel_id=1, source_target_pairs={{0,24},{4,28},{8,16},{12,20},{16,8},{20,12},{24,0},{28,4},{1,25},{... | collective-permute-start | bytes 344072 | tf_op jit(solution)/shard_map/ppermute | solution.py:348
  35.9 13.1 %collective-permute-start.20 = (bf16[32,1792]{1,0:T(8,128)(2,1)S(1)}, bf16[32,1792]{1,0:T(8,128)(2,1)S(1)}, u32[]{:S(2)}, u32[]{:S(2)}) collective-permute-start(bf16[32,1792]{1,0:T(8,128)(2,1)S(1)} %get-tuple-element.113), channel_id=1, source_target_pairs={{0,16},{4,20},{8,24},{12,28},{16,0},{20,4},{24,8},{28,12},{1,17},{... | collective-permute-start | bytes 344072 | tf_op jit(solution)/shard_map/ppermute | solution.py:348
  35.9 13.1 %collective-permute-start.15 = (bf16[32,1792]{1,0:T(8,128)(2,1)S(1)}, bf16[32,1792]{1,0:T(8,128)(2,1)S(1)}, u32[]{:S(2)}, u32[]{:S(2)}) collective-permute-start(bf16[32,1792]{1,0:T(8,128)(2,1)S(1)} %get-tuple-element.113), channel_id=1, source_target_pairs={{0,8},{4,12},{8,0},{12,4},{16,24},{20,28},{24,16},{28,20},{1,9},{5... | collective-permute-start | bytes 344072 | tf_op jit(solution)/shard_map/ppermute | solution.py:348
  37.9 16.1 %collective-permute-start.23 = (bf16[128,1792]{1,0:T(8,128)(2,1)S(1)}, bf16[128,1792]{1,0:T(8,128)(2,1)S(1)}, u32[]{:S(2)}, u32[]{:S(2)}) collective-permute-start(bf16[128,1792]{1,0:T(8,128)(2,1)S(1)} %get-tuple-element.179), channel_id=1, source_target_pairs={{0,4},{4,0},{8,12},{12,8},{16,20},{20,16},{24,28},{28,24},{1,5},{5... | collective-permute-start | bytes 1376264 | tf_op jit(solution)/shard_map/ppermute | solution.py:348
  49.0 13.2 %collective-permute-start.25 = (bf16[32,1792]{1,0:T(8,128)(2,1)S(1)}, bf16[32,1792]{1,0:T(8,128)(2,1)S(1)}, u32[]{:S(2)}, u32[]{:S(2)}) collective-permute-start(bf16[32,1792]{1,0:T(8,128)(2,1)S(1)} %get-tuple-element.123), channel_id=1, source_target_pairs={{0,24},{4,28},{8,16},{12,20},{16,8},{20,12},{24,0},{28,4},{1,25},{... | collective-permute-start | bytes 344072 | tf_op jit(solution)/shard_map/ppermute | solution.py:348
  51.5 10.8 %collective-permute-start.24 = (bf16[32,1792]{1,0:T(8,128)(2,1)S(1)}, bf16[32,1792]{1,0:T(8,128)(2,1)S(1)}, u32[]{:S(2)}, u32[]{:S(2)}) collective-permute-start(bf16[32,1792]{1,0:T(8,128)(2,1)S(1)} %get-tuple-element.123), channel_id=1, source_target_pairs={{0,16},{4,20},{8,24},{12,28},{16,0},{20,4},{24,8},{28,12},{1,17},{... | collective-permute-start | bytes 344072 | tf_op jit(solution)/shard_map/ppermute | solution.py:348
  51.5 10.8 %collective-permute-start.22 = (bf16[32,1792]{1,0:T(8,128)(2,1)S(1)}, bf16[32,1792]{1,0:T(8,128)(2,1)S(1)}, u32[]{:S(2)}, u32[]{:S(2)}) collective-permute-start(bf16[32,1792]{1,0:T(8,128)(2,1)S(1)} %get-tuple-element.123), channel_id=1, source_target_pairs={{0,8},{4,12},{8,0},{12,4},{16,24},{20,28},{24,16},{28,20},{1,9},{5... | collective-permute-start | bytes 344072 | tf_op jit(solution)/shard_map/ppermute | solution.py:348
  53.5 11.2 %collective-permute-start.27 = (bf16[128,1792]{1,0:T(8,128)(2,1)S(1)}, bf16[128,1792]{1,0:T(8,128)(2,1)S(1)}, u32[]{:S(2)}, u32[]{:S(2)}) collective-permute-start(bf16[128,1792]{1,0:T(8,128)(2,1)S(1)} %get-tuple-element.163), channel_id=1, source_target_pairs={{0,4},{4,0},{8,12},{12,8},{16,20},{20,16},{24,28},{28,24},{1,5},{5... | collective-permute-start | bytes 1376264 | tf_op jit(solution)/shard_map/ppermute | solution.py:348
  62.4 11.1 %collective-permute-start.26 = (bf16[128,1792]{1,0:T(8,128)(2,1)S(1)}, bf16[128,1792]{1,0:T(8,128)(2,1)S(1)}, u32[]{:S(2)}, u32[]{:S(2)}) collective-permute-start(bf16[128,1792]{1,0:T(8,128)(2,1)S(1)} %get-tuple-element.170), channel_id=1, source_target_pairs={{0,4},{4,0},{8,12},{12,8},{16,20},{20,16},{24,28},{28,24},{1,5},{5... | collective-permute-start | bytes 1376264 | tf_op jit(solution)/shard_map/ppermute | solution.py:348
  81.7 1.3 collective-permute-start.28
  83.0 3.9 %collective-permute-start.29 = (f32[2,3584]{1,0:T(2,128)S(1)}, f32[2,3584]{1,0:T(2,128)S(1)}, u32[]{:S(2)}, u32[]{:S(2)}) collective-permute-start(f32[2,3584]{1,0:T(2,128)S(1)} %shard_map.68.refs_0_), channel_id=1, source_target_pairs={{0,2},{1,3},{2,0},{3,1},{4,6},{5,7},{6,4},{7,5},{8,10},{9,11},{10,... | collective-permute-start | bytes 86024 | tf_op jit(solution)/shard_map/ppermute | solution.py:348
  105.8 24.8 %collective-permute-start.34 = (f32[2,3584]{1,0:T(2,128)S(1)}, f32[2,3584]{1,0:T(2,128)S(1)}, u32[]{:S(2)}, u32[]{:S(2)}) collective-permute-start(f32[2,3584]{1,0:T(2,128)S(1)} %get-tuple-element.143.refs_0_), channel_id=1, source_target_pairs={{0,4},{4,0},{8,12},{12,8},{16,20},{20,16},{24,28},{28,24},{1,5},{5... | collective-permute-start | bytes 86024 | tf_op jit(solution)/shard_map/ppermute | solution.py:348
  129.0 6.1 %collective-permute-start.30 = (f32[2,3584]{1,0:T(2,128)S(1)}, f32[2,3584]{1,0:T(2,128)S(1)}, u32[]{:S(2)}, u32[]{:S(2)}) collective-permute-start(f32[2,3584]{1,0:T(2,128)S(1)} %get-tuple-element.139.refs_0_), channel_id=1, source_target_pairs={{0,4},{4,0},{8,12},{12,8},{16,20},{20,16},{24,28},{28,24},{1,5},{5... | collective-permute-start | bytes 86024 | tf_op jit(solution)/shard_map/ppermute | solution.py:348
  130.6 6.9 %collective-permute-start.37 = (f32[2,3584]{1,0:T(2,128)S(1)}, f32[2,3584]{1,0:T(2,128)S(1)}, u32[]{:S(2)}, u32[]{:S(2)}) collective-permute-start(f32[2,3584]{1,0:T(2,128)S(1)} %shard_map.74.refs_0_), channel_id=1, source_target_pairs={{0,24},{4,28},{8,16},{12,20},{16,8},{20,12},{24,0},{28,4},{1,25},{... | collective-permute-start | bytes 86024 | tf_op jit(solution)/shard_map/ppermute | solution.py:348
  133.0 6.5 %collective-permute-start.36 = (f32[2,3584]{1,0:T(2,128)S(1)}, f32[2,3584]{1,0:T(2,128)S(1)}, u32[]{:S(2)}, u32[]{:S(2)}) collective-permute-start(f32[2,3584]{1,0:T(2,128)S(1)} %shard_map.74.refs_0_), channel_id=1, source_target_pairs={{0,16},{4,20},{8,24},{12,28},{16,0},{20,4},{24,8},{28,12},{1,17},{... | collective-permute-start | bytes 86024 | tf_op jit(solution)/shard_map/ppermute | solution.py:348
  133.0 6.5 %collective-permute-start.35 = (f32[2,3584]{1,0:T(2,128)S(1)}, f32[2,3584]{1,0:T(2,128)S(1)}, u32[]{:S(2)}, u32[]{:S(2)}) collective-permute-start(f32[2,3584]{1,0:T(2,128)S(1)} %shard_map.74.refs_0_), channel_id=1, source_target_pairs={{0,8},{4,12},{8,0},{12,4},{16,24},{20,28},{24,16},{28,20},{1,9},{5... | collective-permute-start | bytes 86024 | tf_op jit(solution)/shard_map/ppermute | solution.py:348
  135.1 8.2 %collective-permute-start.33 = (f32[2,3584]{1,0:T(2,128)S(1)}, f32[2,3584]{1,0:T(2,128)S(1)}, u32[]{:S(2)}, u32[]{:S(2)}) collective-permute-start(f32[2,3584]{1,0:T(2,128)S(1)} %shard_map.71.refs_0_), channel_id=1, source_target_pairs={{0,24},{4,28},{8,16},{12,20},{16,8},{20,12},{24,0},{28,4},{1,25},{... | collective-permute-start | bytes 86024 | tf_op jit(solution)/shard_map/ppermute | solution.py:348
  137.5 5.8 %collective-permute-start.32 = (f32[2,3584]{1,0:T(2,128)S(1)}, f32[2,3584]{1,0:T(2,128)S(1)}, u32[]{:S(2)}, u32[]{:S(2)}) collective-permute-start(f32[2,3584]{1,0:T(2,128)S(1)} %shard_map.71.refs_0_), channel_id=1, source_target_pairs={{0,16},{4,20},{8,24},{12,28},{16,0},{20,4},{24,8},{28,12},{1,17},{... | collective-permute-start | bytes 86024 | tf_op jit(solution)/shard_map/ppermute | solution.py:348
  137.5 5.8 %collective-permute-start.31 = (f32[2,3584]{1,0:T(2,128)S(1)}, f32[2,3584]{1,0:T(2,128)S(1)}, u32[]{:S(2)}, u32[]{:S(2)}) collective-permute-start(f32[2,3584]{1,0:T(2,128)S(1)} %shard_map.71.refs_0_), channel_id=1, source_target_pairs={{0,8},{4,12},{8,0},{12,4},{16,24},{20,28},{24,16},{28,20},{1,9},{5... | collective-permute-start | bytes 86024 | tf_op jit(solution)/shard_map/ppermute | solution.py:348
  139.6 8.3 %copy-start = (bf16[3584,3584]{1,0:T(8,128)(2,1)S(1)}, bf16[3584,3584]{1,0:T(8,128)(2,1)}, u32[]{:S(2)}) copy-start(bf16[3584,3584]{1,0:T(8,128)(2,1)} %get-tuple-element.137.kept_ref) | copy-start | bytes 77070336
  151.6 1.2 collective-permute-start.38
  152.9 3.7 %collective-permute-start.39 = (f32[1,3584]{1,0:T(1,128)S(1)}, f32[1,3584]{1,0:T(1,128)S(1)}, u32[]{:S(2)}, u32[]{:S(2)}) collective-permute-start(f32[1,3584]{1,0:T(1,128)S(1)} %shard_map.78.refs_0_), channel_id=1, source_target_pairs={{0,2},{1,3},{2,0},{3,1},{4,6},{5,7},{6,4},{7,5},{8,10},{9,11},{10,... | collective-permute-start | bytes 43016 | tf_op jit(solution)/shard_map/ppermute | solution.py:348
  160.2 5.8 %collective-permute-start.40 = (f32[1,3712]{1,0:T(1,128)S(1)}, f32[1,3712]{1,0:T(1,128)S(1)}, u32[]{:S(2)}, u32[]{:S(2)}) collective-permute-start(f32[1,3712]{1,0:T(1,128)S(1)} %shard_map.80.refs_0_), channel_id=1, source_target_pairs={{0,4},{4,0},{8,12},{12,8},{16,20},{20,16},{24,28},{28,24},{1,5},{5... | collective-permute-start | bytes 44552 | tf_op jit(solution)/shard_map/ppermute | solution.py:348
  164.4 6.0 %collective-permute-start.44 = (f32[1,3712]{1,0:T(1,128)S(1)}, f32[1,3712]{1,0:T(1,128)S(1)}, u32[]{:S(2)}, u32[]{:S(2)}) collective-permute-start(f32[1,3712]{1,0:T(1,128)S(1)} %shard_map.83.refs_0_), channel_id=1, source_target_pairs={{0,4},{4,0},{8,12},{12,8},{16,20},{20,16},{24,28},{28,24},{1,5},{5... | collective-permute-start | bytes 44552 | tf_op jit(solution)/shard_map/ppermute | solution.py:348
  166.0 6.9 %collective-permute-start.43 = (f32[1,3712]{1,0:T(1,128)S(1)}, f32[1,3712]{1,0:T(1,128)S(1)}, u32[]{:S(2)}, u32[]{:S(2)}) collective-permute-start(f32[1,3712]{1,0:T(1,128)S(1)} %shard_map.81.refs_0_), channel_id=1, source_target_pairs={{0,24},{4,28},{8,16},{12,20},{16,8},{20,12},{24,0},{28,4},{1,25},{... | collective-permute-start | bytes 44552 | tf_op jit(solution)/shard_map/ppermute | solution.py:348
  168.4 6.5 %collective-permute-start.42 = (f32[1,3712]{1,0:T(1,128)S(1)}, f32[1,3712]{1,0:T(1,128)S(1)}, u32[]{:S(2)}, u32[]{:S(2)}) collective-permute-start(f32[1,3712]{1,0:T(1,128)S(1)} %shard_map.81.refs_0_), channel_id=1, source_target_pairs={{0,16},{4,20},{8,24},{12,28},{16,0},{20,4},{24,8},{28,12},{1,17},{... | collective-permute-start | bytes 44552 | tf_op jit(solution)/shard_map/ppermute | solution.py:348
  168.4 6.5 %collective-permute-start.41 = (f32[1,3712]{1,0:T(1,128)S(1)}, f32[1,3712]{1,0:T(1,128)S(1)}, u32[]{:S(2)}, u32[]{:S(2)}) collective-permute-start(f32[1,3712]{1,0:T(1,128)S(1)} %shard_map.81.refs_0_), channel_id=1, source_target_pairs={{0,8},{4,12},{8,0},{12,4},{16,24},{20,28},{24,16},{28,20},{1,9},{5... | collective-permute-start | bytes 44552 | tf_op jit(solution)/shard_map/ppermute | solution.py:348
  170.5 5.6 %collective-permute-start.47 = (f32[1,3712]{1,0:T(1,128)S(1)}, f32[1,3712]{1,0:T(1,128)S(1)}, u32[]{:S(2)}, u32[]{:S(2)}) collective-permute-start(f32[1,3712]{1,0:T(1,128)S(1)} %shard_map.84.refs_0_), channel_id=1, source_target_pairs={{0,24},{4,28},{8,16},{12,20},{16,8},{20,12},{24,0},{28,4},{1,25},{... | collective-permute-start | bytes 44552 | tf_op jit(solution)/shard_map/ppermute | solution.py:348
  172.9 4.6 %collective-permute-start.46 = (f32[1,3712]{1,0:T(1,128)S(1)}, f32[1,3712]{1,0:T(1,128)S(1)}, u32[]{:S(2)}, u32[]{:S(2)}) collective-permute-start(f32[1,3712]{1,0:T(1,128)S(1)} %shard_map.84.refs_0_), channel_id=1, source_target_pairs={{0,16},{4,20},{8,24},{12,28},{16,0},{20,4},{24,8},{28,12},{1,17},{... | collective-permute-start | bytes 44552 | tf_op jit(solution)/shard_map/ppermute | solution.py:348
  172.9 4.6 %collective-permute-start.45 = (f32[1,3712]{1,0:T(1,128)S(1)}, f32[1,3712]{1,0:T(1,128)S(1)}, u32[]{:S(2)}, u32[]{:S(2)}) collective-permute-start(f32[1,3712]{1,0:T(1,128)S(1)} %shard_map.84.refs_0_), channel_id=1, source_target_pairs={{0,8},{4,12},{8,0},{12,4},{16,24},{20,28},{24,16},{28,20},{1,9},{5... | collective-permute-start | bytes 44552 | tf_op jit(solution)/shard_map/ppermute | solution.py:348
